TPU v7x, 256 devices: a whole 4x4x8 slice. The times are simulated.
256 devices in a mesh: row: 8 (over x_lo, y), col: 16 (over z, x_hi), srv: 2 (over core).
Axes of the slice: x: 4 (x_hi: 2, x_lo: 2; x = x_hi * 2 + x_lo), y: 4, z: 8, core: 2. Of those that a mesh axis runs over, the one named last changes fastest.
Arguments:
- inputs: bfloat16 [8192, 8192], P(('row', 'srv'), 'col'), may hold values from -0.75 to 0.75
- grad_out: bfloat16 [8192, 8192], P(('row', 'srv'), 'col'), may hold values from -6 to 6
- weight: bfloat16 [8192, 8192], P('col', 'row'), may hold values from -0.0625 to 0.0625
- blocks: int32 [16, 128, 2], P('col'), may hold values from -1 to 63, as said below
- owner: int32 [16, 128], P('col'), may hold values from -1 to 15, as said below
Outputs:
- grad_in: bfloat16 [8192, 8192], P(('row', 'srv'), 'col')
- pushed: float32 [16, 128, 128, 128], P(('row', 'srv'), 'col')
Inputs may be any that keep to these rules, and one draw needn't show every extreme that they name: List g holds distinct blocks whose row block lies in g * 8192 / 2048 to (g + 1) * 8192 / 2048 - 1; live entries come first, the rest are (-1, -1); some list is full, and each list has 8 or more live entries. An entry that is not live has owner -1; no owner gets more than 8 live entries of one list, and in a full list every owner gets exactly 8.
All inputs are finite; a program needn't handle non-finite values.
Results may differ from a plain program's by a relative error of at most 0.001.
Values may be sent and summed in bfloat16 or wider, within the bound.
No kernel may reach another device: no remote copies, remote signals or barrier semaphores. Data moves between devices by JAX's collectives and lax.ppermute only.
A program may use at most 128 MiB of HBM per device.

v0:
```python
import jax
import jax.numpy as jnp
from jax import lax
from jax.sharding import PartitionSpec as P

DOUT = 8192
BLK = 128
CAP = 8


def body(inputs, grad_out, weight, blocks, owner):
    rows = inputs.shape[0]
    width = inputs.shape[1]
    full_grad = lax.all_gather(grad_out, "col", axis=1, tiled=True)
    summed = lax.dot_general(
        full_grad,
        lax.all_gather(weight, "row", axis=1, tiled=True),
        (((1,), (1,)), ((), ())),
        preferred_element_type=jnp.float32,
    )
    grad_in = summed.astype(jnp.bfloat16)
    listed = blocks[0]
    owners = owner[0]
    entries = listed.shape[0]
    owner_count = lax.axis_size("row") * lax.axis_size("srv")
    live = listed[:, 0] >= 0
    same = owners[:, None] == owners[None, :]
    order = jnp.arange(entries, dtype=jnp.int32)
    earlier = order[None, :] < order[:, None]
    rank = jnp.sum((same & earlier & live[None, :]).astype(jnp.int32), axis=1)
    position = jnp.where(live, owners * CAP + rank, 0)
    input_tiles = inputs.reshape(rows, width // BLK, BLK)
    grad_tiles = full_grad.reshape(rows, DOUT // BLK, BLK)
    row_local = jnp.where(live, listed[:, 0] % (width // BLK), 0)
    col_local = jnp.where(live, listed[:, 1], 0)
    live_weight = live.astype(jnp.float32)

    def tile_group(row_sel, col_sel, live_sel):
        left = jnp.take(input_tiles, row_sel, axis=1)
        right = jnp.take(grad_tiles, col_sel, axis=1)
        return (
            jnp.einsum("bmi,bmj->mij", left, right, preferred_element_type=jnp.float32)
            * live_sel[:, None, None]
        )

    live_count = jnp.sum(live.astype(jnp.int32))
    group_count = (live_count + CAP - 1) // CAP

    def one_group(group, tiles):
        first = group * CAP
        made = tile_group(
            lax.dynamic_slice_in_dim(row_local, first, CAP),
            lax.dynamic_slice_in_dim(col_local, first, CAP),
            lax.dynamic_slice_in_dim(live_weight, first, CAP),
        )
        return lax.dynamic_update_slice_in_dim(tiles, made, first, 0)

    tiles = lax.fori_loop(0, group_count, one_group, jnp.zeros((entries, BLK, BLK), jnp.float32))
    holder = jnp.zeros((owner_count * CAP, BLK, BLK), jnp.float32).at[position].add(tiles)
    pushed = lax.psum_scatter(holder, ("row", "srv"), scatter_dimension=0, tiled=True)
    return (grad_in, pushed.reshape(1, CAP, BLK, BLK))


def solution(mesh):
    in_specs = (
        P(("row", "srv"), "col"),
        P(("row", "srv"), "col"),
        P("col", "row"),
        P("col", None, None),
        P("col", None),
    )
    out_specs = (P(("row", "srv"), "col"), P(("row", "srv"), "col", None, None))
    return jax.shard_map(body, mesh=mesh, in_specs=in_specs, out_specs=out_specs, check_vma=False)
```

profile of v0, /device:TPU:1, one launch (start us, length us, event | category | flops | bytes accessed | tf_op | source)
XLA Modules:
  0.0 379.5 jit_solution(14983797913105139455)
XLA Ops:
  7.2 2.0 copy.16
  16.0 134.4 %all-gather.3.cloned.1.call-done = bf16[512,8192]{0,1:T(8,128)(2,1)} async-done(((bf16[512,512]{0,1:T(8,128)(2,1)}), bf16[512,8192]{0,1:T(8,128)(2,1)}) %all-gather.3.cloned.1.call-update) | async-done | bytes 8388624 | tf_op jit(solution)/shard_map/all_gather | solution.py:14
  150.4 11.9 %copy.19 = bf16[512,64,128]{2,0,1:T(8,128)(2,1)} copy(bf16[512,64,128]{0,2,1:T(8,128)(2,1)} %bitcast.42) | data formatting | bytes 16777216 | tf_op jit(solution)/shard_map/while | solution.py:58
  162.3 4.3 %broadcast.53.clone = f32[128,128,128]{2,1,0:T(8,128)} broadcast(f32[]{:T(128)} %constant.68.clone.1), dimensions={} | broadcast | bytes 8388612 | tf_op jit(solution)/shard_map/broadcast.20
  166.6 65.8 %while.10 = (s32[]{:T(128)}, f32[128,128,128]{2,1,0:T(8,128)}, s32[]{:T(128)}, s32[128]{0:T(128)S(1)}, bf16[512,4,128]{2,0,1:T(8,128)(2,1)S(1)}, /*index=5*/s32[...) while((s32[]{:T(128)}, f32[128,128,128]{2,1,0:T(8,128)}, ...), condition=%wide.region_3.4_spmd, body=%wide.region_2.3_spmd.sunk | while | flops 135399520 | bytes 6824495 | solution.py:58
  167.5 4.2 %gather_fusion = bf16[8,512,128]{2,1,0:T(8,128)(2,1)S(1)} fusion(bf16[512,64,128]{2,0,1:T(8,128)(2,1)} %get-tuple-element.177, s32[1024]{0:T(1024)S(1)} %pad_clamp_fusion.4), kind=kCustom, calls=%fused_computation.1.clone.1 | custom fusion | bytes 2097184 | tf_op jit(solution)/shard_map/while/body/jit(_take)/gather | solution.py:40
  171.8 1.5 fusion.22
  174.2 4.2 %gather_fusion = bf16[8,512,128]{2,1,0:T(8,128)(2,1)S(1)} fusion(bf16[512,64,128]{2,0,1:T(8,128)(2,1)} %get-tuple-element.177, s32[1024]{0:T(1024)S(1)} %pad_clamp_fusion.4), kind=kCustom, calls=%fused_computation.1.clone.1 | custom fusion | bytes 2097184 | tf_op jit(solution)/shard_map/while/body/jit(_take)/gather | solution.py:40
  178.4 1.5 fusion.22
  180.8 4.2 %gather_fusion = bf16[8,512,128]{2,1,0:T(8,128)(2,1)S(1)} fusion(bf16[512,64,128]{2,0,1:T(8,128)(2,1)} %get-tuple-element.177, s32[1024]{0:T(1024)S(1)} %pad_clamp_fusion.4), kind=kCustom, calls=%fused_computation.1.clone.1 | custom fusion | bytes 2097184 | tf_op jit(solution)/shard_map/while/body/jit(_take)/gather | solution.py:40
  187.3 4.2 %gather_fusion = bf16[8,512,128]{2,1,0:T(8,128)(2,1)S(1)} fusion(bf16[512,64,128]{2,0,1:T(8,128)(2,1)} %get-tuple-element.177, s32[1024]{0:T(1024)S(1)} %pad_clamp_fusion.4), kind=kCustom, calls=%fused_computation.1.clone.1 | custom fusion | bytes 2097184 | tf_op jit(solution)/shard_map/while/body/jit(_take)/gather | solution.py:40
  193.9 4.2 %gather_fusion = bf16[8,512,128]{2,1,0:T(8,128)(2,1)S(1)} fusion(bf16[512,64,128]{2,0,1:T(8,128)(2,1)} %get-tuple-element.177, s32[1024]{0:T(1024)S(1)} %pad_clamp_fusion.4), kind=kCustom, calls=%fused_computation.1.clone.1 | custom fusion | bytes 2097184 | tf_op jit(solution)/shard_map/while/body/jit(_take)/gather | solution.py:40
  198.1 1.4 fusion.22
  200.4 4.2 %gather_fusion = bf16[8,512,128]{2,1,0:T(8,128)(2,1)S(1)} fusion(bf16[512,64,128]{2,0,1:T(8,128)(2,1)} %get-tuple-element.177, s32[1024]{0:T(1024)S(1)} %pad_clamp_fusion.4), kind=kCustom, calls=%fused_computation.1.clone.1 | custom fusion | bytes 2097184 | tf_op jit(solution)/shard_map/while/body/jit(_take)/gather | solution.py:40
  207.0 4.2 %gather_fusion = bf16[8,512,128]{2,1,0:T(8,128)(2,1)S(1)} fusion(bf16[512,64,128]{2,0,1:T(8,128)(2,1)} %get-tuple-element.177, s32[1024]{0:T(1024)S(1)} %pad_clamp_fusion.4), kind=kCustom, calls=%fused_computation.1.clone.1 | custom fusion | bytes 2097184 | tf_op jit(solution)/shard_map/while/body/jit(_take)/gather | solution.py:40
  213.6 4.2 %gather_fusion = bf16[8,512,128]{2,1,0:T(8,128)(2,1)S(1)} fusion(bf16[512,64,128]{2,0,1:T(8,128)(2,1)} %get-tuple-element.177, s32[1024]{0:T(1024)S(1)} %pad_clamp_fusion.4), kind=kCustom, calls=%fused_computation.1.clone.1 | custom fusion | bytes 2097184 | tf_op jit(solution)/shard_map/while/body/jit(_take)/gather | solution.py:40
  220.1 4.2 %gather_fusion = bf16[8,512,128]{2,1,0:T(8,128)(2,1)S(1)} fusion(bf16[512,64,128]{2,0,1:T(8,128)(2,1)} %get-tuple-element.177, s32[1024]{0:T(1024)S(1)} %pad_clamp_fusion.4), kind=kCustom, calls=%fused_computation.1.clone.1 | custom fusion | bytes 2097184 | tf_op jit(solution)/shard_map/while/body/jit(_take)/gather | solution.py:40
  224.3 1.4 fusion.22
  226.7 4.2 %gather_fusion = bf16[8,512,128]{2,1,0:T(8,128)(2,1)S(1)} fusion(bf16[512,64,128]{2,0,1:T(8,128)(2,1)} %get-tuple-element.177, s32[1024]{0:T(1024)S(1)} %pad_clamp_fusion.4), kind=kCustom, calls=%fused_computation.1.clone.1 | custom fusion | bytes 2097184 | tf_op jit(solution)/shard_map/while/body/jit(_take)/gather | solution.py:40
  231.0 1.4 fusion.22
  232.4 4.3 %broadcast.53 = f32[128,128,128]{2,1,0:T(8,128)} broadcast(f32[]{:T(128)} %constant.68.clone.1), dimensions={} | broadcast | bytes 8388612 | tf_op jit(solution)/shard_map/broadcast.20
  236.7 27.2 %scatter_fusion = f32[128,128,128]{2,1,0:T(8,128)} fusion(f32[128,128,128]{2,1,0:T(8,128)} %broadcast.53, s32[128]{0:T(128)S(1)} %fusion.13, f32[128,128,128]{2,1,0:T(8,128)} %get-tuple-element.45), kind=kCustom, calls=%fused_computation.2 | custom fusion | flops 2097152 | bytes 25166336 | tf_op jit(solution)/shard_map/scatter-add | solution.py:59
  264.0 11.1 %convolution_convert_fusion = bf16[512,512]{1,0:T(8,128)(2,1)} fusion(bf16[512,8192]{0,1:T(8,128)(2,1)} %all-gather.3.cloned.1.call-done, bf16[512,8192]{1,0:T(8,128)(2,1)} %all-gather.5.cloned.1.call-done), kind=kOutput, calls=%fused_computation.19 | convolution fusion | flops 4295229440 | bytes 17301504 | tf_op jit(solution)/shard_map/dot_general | solution.py:15
  275.1 97.9 %reduce-scatter.2.cloned.1.call-done = f32[8,128,128]{2,1,0:T(8,128)} async-done(((f32[128,128,128]{2,1,0:T(8,128)}), f32[8,128,128]{2,1,0:T(8,128)}) %reduce-scatter.2.cloned.1.call-update) | async-done | bytes 524304 | tf_op jit(solution)/shard_map/reduce_scatter | solution.py:60
  (68 shorter events, 22.3 us)
Async XLA Ops:
  7.2 143.2 %all-gather.3.cloned.1.call-start = ((), (), s32[]{:S(2)}) async-start(), calls=%async_computation.1 | async-start | bytes 8912896 | tf_op jit(solution)/shard_map/all_gather | solution.py:14
  9.3 254.7 %all-gather.5.cloned.1.call-start = ((), (), s32[]{:S(2)}) async-start(), calls=%async_computation.2 | async-start | bytes 9437184 | tf_op jit(solution)/shard_map/all_gather | solution.py:17
  10.0 362.9 %reduce-scatter.2.cloned.1.call-start = ((), (), s32[]{:S(2)}) async-start(), calls=%async_computation.3 | async-start | bytes 8912896 | tf_op jit(solution)/shard_map/reduce_scatter | solution.py:60
Sparse Core Ops, SparseCore 0:
  11.2 139.1 all-gather.2
  152.2 91.6 all-gather.4
  264.0 108.8 reduce-scatter.1
where the time goes:
time: 383 us; the launch traced here: 380 us
  waiting for transfers between devices  233 us (61%)
  local copies, waits for them, and re-layouts  74.4 us (19%)
  other arithmetic  31.9 us (8%)
  matrix products  25.4 us (7%)
  between operations  14.4 us (4%)
    all_gather x1, waiting for transfers between devices, body(): full_grad = lax.all_gather(grad_out, 'col', axis=1, tiled=True)  134 us
    reduce_scatter x1, waiting for transfers between devices, body(): lax.psum_scatter(holder, ('row', 'srv'), scatter_dimension=0, tiled=True)  97.9 us
    gather x10, local copies, waits for them, and re-layouts, tile_group(): right = jnp.take(grad_tiles, col_sel, axis=1)  42.1 us
    scatter-add x1, other arithmetic, body(): jnp.zeros((owner_count * CAP, BLK, BLK), jnp.float32).at[position]  27.2 us
    dot_general x10, matrix products, tile_group(): jnp.einsum('bmi,bmj->mij', left, right, preferred_element_type=jnp.float32)  14.3 us
    while x2, local copies, waits for them, and re-layouts, body(): lax.fori_loop(0, group_count, one_group, jnp.zeros((entries, BLK, BLK), j...  12.2 us
    dot_general x1, matrix products, body(): lax.dot_general(full_grad, lax.all_gather(weight, 'row', axis=1, tiled=Tr...  11.1 us
    another operation x2, local copies, waits for them, and re-layouts  8.52 us
  transfers between devices with their start and end apart: 3, of which 2 were waited for; matrix products, arithmetic and copies ran while one was open for 34% of the time, Pallas kernels for 0%

commit v1 on v0

v1 whole, which is shorter than its diff:
```python
import functools

import jax
import jax.numpy as jnp
from jax import lax
from jax.experimental import pallas as pl
from jax.experimental.pallas import tpu as pltpu
from jax.sharding import PartitionSpec as P

BLK = 128
CAP = 8
POWER = 9
TOP = 13.0
TAIL = 16
F32 = jnp.float32
BF16 = jnp.bfloat16

COLS = ((0, 0), (-1, 0), (1, 0), (0, 1), (-2, 0), (2, 0), (-3, 0), (3, 0),
        (4, 0), (-1, 1), (1, 1), (-2, 1), (2, 1), (-3, 1), (3, 1), (4, 1))
ROWS = ((0, 0), (1, 0), (0, -1), (1, -1), (0, 1), (1, 1), (0, 2), (1, 2))
DESTS = ((1, 0), (1, 1), (1, 3), (1, 2), (0, 1), (0, 3), (0, 2), (0, 0))


def z_shift(d):
    return [(z * 2 + h, ((z + d) % 8) * 2 + h) for z in range(8) for h in range(2)]


def row_shift(dx, dy):
    return [(l * 4 + y, (l ^ dx) * 4 + (y + dy) % 4) for l in range(2) for y in range(4)]


X_SWAP = [(z * 2 + h, z * 2 + 1 - h) for z in range(8) for h in range(2)]
CORE_SWAP = [(0, 1), (1, 0)]


def any_spec():
    return pl.BlockSpec(memory_space=pl.ANY)


def smem_spec():
    return pl.BlockSpec(memory_space=pltpu.SMEM)


def vmem_spec():
    return pl.BlockSpec(memory_space=pltpu.VMEM)


def params(mib):
    return pltpu.CompilerParams(vmem_limit_bytes=mib * 1024 * 1024)


def dense_kernel(count, first, where_ref, xt_ref, *refs):
    blocks = refs[:count]
    out, made, sems = refs[count + (0 if first else 1):]
    copies = []
    for j in range(count):
        acc = jnp.dot(xt_ref[...], blocks[j][...], preferred_element_type=F32)
        for cc in range(4):
            for rb in range(4):
                made[j, cc * 4 + rb] = acc[rb * BLK:(rb + 1) * BLK, cc * BLK:(cc + 1) * BLK]
        copy = pltpu.make_async_copy(made.at[j], out.at[where_ref[j]], sems.at[j])
        copy.start()
        copies.append(copy)
    for copy in copies:
        copy.wait()


def dense(total, where, xt, blocks):
    count = len(blocks)
    first = total is None
    args = [where, xt, *blocks] + ([] if first else [total])
    return pl.pallas_call(
        functools.partial(dense_kernel, count, first),
        out_shape=jax.ShapeDtypeStruct((16, 16, BLK, BLK), F32),
        in_specs=[smem_spec()] + [vmem_spec()] * (1 + count) + ([] if first else [any_spec()]),
        out_specs=any_spec(),
        scratch_shapes=[pltpu.VMEM((count, 16, BLK, BLK), F32), pltpu.SemaphoreType.DMA((count,))],
        input_output_aliases={} if first else {2 + count: 0},
        compiler_params=params(24),
        cost_estimate=pl.CostEstimate(
            flops=count * 2 * 512 ** 3, bytes_accessed=count * 3 * 512 * 1024, transcendentals=0),
    )(*args)


def pick_kernel(chunks, slot_ref, row_ref, total, out, sems):
    def place(i):
        return jnp.maximum(slot_ref[row_ref[i // CAP] * CAP + i % CAP], 0)

    def start(i, carry):
        pltpu.make_async_copy(total.at[place(i)], out.at[i], sems.at[i]).start()
        return carry

    def finish(i, carry):
        pltpu.make_async_copy(total.at[place(i)], out.at[i], sems.at[i]).wait()
        return carry

    lax.fori_loop(0, chunks * CAP, start, 0)
    lax.fori_loop(0, chunks * CAP, finish, 0)


def pick(slots, owners, total):
    chunks = owners.shape[0]
    return pl.pallas_call(
        functools.partial(pick_kernel, chunks),
        out_shape=jax.ShapeDtypeStruct((chunks * CAP, BLK, BLK), F32),
        in_specs=[smem_spec(), smem_spec(), any_spec()],
        out_specs=any_spec(),
        scratch_shapes=[pltpu.SemaphoreType.DMA((chunks * CAP,))],
        compiler_params=params(16),
        cost_estimate=pl.CostEstimate(
            flops=0, bytes_accessed=chunks * CAP * BLK * BLK * 8, transcendentals=0),
    )(slots, owners, total)


def code_kernel(coded, plain, slot_ref, row_ref, total, other, *refs):
    chunks = coded + plain
    outs = refs[:chunks]
    mine, theirs, my_sems, their_sems = refs[chunks:]

    def place(i):
        return jnp.maximum(slot_ref[row_ref[i // CAP] * CAP + i % CAP], 0)

    def mine_copy(i):
        return pltpu.make_async_copy(total.at[place(i)], mine.at[i], my_sems.at[i])

    def theirs_copy(m):
        part = pl.ds(m * CAP, CAP)
        return pltpu.make_async_copy(other.at[part], theirs.at[part], their_sems.at[m])

    def start(i, carry):
        mine_copy(i).start()
        return carry

    def finish(i, carry):
        mine_copy(i).wait()
        return carry

    for m in range(chunks):
        theirs_copy(m).start()
        lax.fori_loop(m * CAP, (m + 1) * CAP, start, 0)
    for m in range(chunks):
        theirs_copy(m).wait()
        lax.fori_loop(m * CAP, (m + 1) * CAP, finish, 0)
        most = jnp.zeros((1, BLK), F32)
        for t in range(CAP):
            i = m * CAP + t
            live = slot_ref[row_ref[m] * CAP + t] >= 0
            both = jnp.where(live, mine[i] + theirs[i], 0.0)
            if m >= coded:
                outs[m][t] = both
            else:
                mine[i] = both
                most = jnp.maximum(most, jnp.max(jnp.abs(both), axis=0, keepdims=True))
        if m < coded:
            level = jnp.ceil(jnp.log2(jnp.maximum(most, 1e-30)))
            scale = jnp.exp2(TOP - level)
            for t in range(CAP):
                v = mine[m * CAP + t] * scale
                v2 = v * v
                v4 = v2 * v2
                outs[m][t * BLK:(t + 1) * BLK, :] = (v4 * v4 * v).astype(BF16)
            outs[m][CAP * BLK:, :] = jnp.broadcast_to(level, (TAIL, BLK)).astype(BF16)


def code(slots, owners, total, other, coded):
    chunks = owners.shape[0]
    plain = chunks - coded
    return pl.pallas_call(
        functools.partial(code_kernel, coded, plain),
        out_shape=[jax.ShapeDtypeStruct((CAP * BLK + TAIL, BLK), BF16)] * coded
        + [jax.ShapeDtypeStruct((CAP, BLK, BLK), F32)] * plain,
        in_specs=[smem_spec(), smem_spec(), any_spec(), any_spec()],
        out_specs=[vmem_spec()] * chunks,
        scratch_shapes=[
            pltpu.VMEM((chunks * CAP, BLK, BLK), F32),
            pltpu.VMEM((chunks * CAP, BLK, BLK), F32),
            pltpu.SemaphoreType.DMA((chunks * CAP,)),
            pltpu.SemaphoreType.DMA((chunks,)),
        ],
        compiler_params=params(24),
        cost_estimate=pl.CostEstimate(
            flops=chunks * CAP * BLK * BLK * 8, bytes_accessed=chunks * CAP * BLK * BLK * 10,
            transcendentals=0),
    )(slots, owners, total, other)


def sum_kernel(own, *refs):
    arrived, out = refs[:-1], refs[-1]
    scales = []
    for ref in arrived:
        level = ref[CAP * BLK:CAP * BLK + TAIL, :].astype(F32)[0:1, :]
        scales.append(level - TOP)
    for t in range(CAP):
        acc = own[t]
        for ref, scale in zip(arrived, scales):
            y = ref[t * BLK:(t + 1) * BLK, :].astype(F32)
            size = jnp.exp2(jnp.log2(jnp.maximum(jnp.abs(y), 1e-37)) * (1.0 / POWER) + scale)
            size = jnp.where(jnp.abs(y) > 1e-37, size, 0.0)
            acc = acc + jnp.where(y < 0, -size, size)
        out[t] = acc


def total_sum(own, arrived):
    return pl.pallas_call(
        sum_kernel,
        out_shape=jax.ShapeDtypeStruct((CAP, BLK, BLK), F32),
        in_specs=[vmem_spec()] * (1 + len(arrived)),
        out_specs=vmem_spec(),
        compiler_params=params(24),
        cost_estimate=pl.CostEstimate(
            flops=8 * CAP * BLK * BLK * 8, bytes_accessed=8 * CAP * BLK * BLK * 2,
            transcendentals=0),
    )(own, *arrived)


def grad_kernel(row_of_ref, half_ref, mine, theirs, *refs):
    blocks = refs[:16]
    out, grads, weights, g_sems, w_sems = refs[16:]
    side = half_ref[0]
    core = half_ref[1]
    w_copies = [
        pltpu.make_async_copy(mine, weights.at[core], w_sems.at[0]),
        pltpu.make_async_copy(theirs, weights.at[1 - core], w_sems.at[1]),
    ]
    g_copies = [pltpu.make_async_copy(blocks[k], grads.at[k], g_sems.at[k]) for k in range(16)]
    for copy in w_copies + g_copies:
        copy.start()
    for copy in w_copies:
        copy.wait()
    acc = jnp.zeros((512, 512), F32)
    for k, (dz, dxh) in enumerate(COLS):
        g_copies[k].wait()
        row = row_of_ref[dz % 8]
        first = pl.multiple_of((side if dxh == 0 else 1 - side) * 512, 512)
        w = weights[:, row, :, pl.ds(first, 512)].reshape(512, 512)
        acc = acc + lax.dot_general(
            grads[k], w, (((1,), (1,)), ((), ())), preferred_element_type=F32)
    out[...] = acc.astype(BF16)


def grad_in_of(row_of, half, mine, theirs, blocks):
    return pl.pallas_call(
        grad_kernel,
        out_shape=jax.ShapeDtypeStruct((512, 512), BF16),
        in_specs=[smem_spec(), smem_spec()] + [any_spec()] * 18,
        out_specs=vmem_spec(),
        scratch_shapes=[
            pltpu.VMEM((16, 512, 512), BF16),
            pltpu.VMEM((2, 8, 256, 1024), BF16),
            pltpu.SemaphoreType.DMA((16,)),
            pltpu.SemaphoreType.DMA((2,)),
        ],
        compiler_params=params(40),
        cost_estimate=pl.CostEstimate(
            flops=2 * 512 * 512 * 8192, bytes_accessed=17 * 1024 * 1024, transcendentals=0),
    )(row_of, half, mine, theirs, *blocks)


def body(inputs, grad_out, weight, blocks, owner):
    row = lax.axis_index("row")
    col = lax.axis_index("col")
    core = lax.axis_index("srv")
    x_lo, y = row // 4, row % 4
    z, x_hi = col // 2, col % 2

    def up(v):
        return lax.ppermute(v, "col", z_shift(1))

    def down(v):
        return lax.ppermute(v, "col", z_shift(-1))

    def across(v):
        return lax.ppermute(v, "col", X_SWAP)

    def to_row(v, dx, dy):
        return lax.ppermute(v, "row", row_shift(dx, dy))

    def to_core(v):
        return lax.ppermute(v, "srv", CORE_SWAP)

    o0 = across(grad_out)
    a1, c1 = up(grad_out), down(grad_out)
    a2, c2 = up(a1), down(c1)
    oa2, oc2 = across(a2), across(c2)
    a3, c3 = up(a2), down(c2)
    f4 = jnp.concatenate([up(a3[:256]), down(c3[256:])], axis=0)
    o4 = across(f4)
    e1, f1 = up(o0), down(o0)
    e3, f3 = up(oa2), down(oc2)
    cols = [grad_out, a1, c1, o0, a2, c2, a3, c3, f4, e1, f1, oa2, oc2, e3, f3, o4]

    half = lax.dynamic_slice_in_dim(weight, core * 256, 256, 0)
    pair = jnp.concatenate([half, to_row(half, 1, 0)], axis=0)
    wa, wc = to_row(pair, 0, 1), to_row(pair, 0, -1)
    wd, we = to_row(wa[:256], 0, 1), to_row(wc[256:], 0, -1)
    w_mine = jnp.concatenate([pair, wa, wc, wd, we], axis=0).reshape(8, 256, 1024)
    w_theirs = to_core(w_mine)

    listed = blocks[0]
    owners = owner[0]
    live = listed[:, 0] >= 0
    order = jnp.arange(listed.shape[0], dtype=jnp.int32)
    same = owners[:, None] == owners[None, :]
    earlier = order[None, :] < order[:, None]
    rank = jnp.sum((same & earlier & live[None, :]).astype(jnp.int32), axis=1)
    position = jnp.where(live, owners * CAP + rank, -1)
    tile = jnp.where(live, listed[:, 1] * 4 + listed[:, 0] % 4, 0)
    fills = position[None, :] == order[:, None]
    slots = jnp.sum(jnp.where(fills, tile[None, :] + 1, 0), axis=1) - 1

    def col_index(first, last):
        return jnp.stack([((z + dz) % 8) * 2 + (x_hi ^ dxh) for dz, dxh in COLS[first:last]]).astype(jnp.int32)

    xt = inputs.T
    total = None
    for first, last in ((0, 1), (1, 4), (4, 6), (6, 8), (8, 13), (13, 16)):
        total = dense(total, col_index(first, last), xt, cols[first:last])
    total = total.reshape(256, BLK, BLK)

    dest_rows = [(x_lo ^ dx) * 4 + (y + dy) % 4 for dx, dy in DESTS]
    mine_owners = jnp.stack([r * 2 + core for r in dest_rows]).astype(jnp.int32)
    their_owners = jnp.stack([r * 2 + 1 - core for r in dest_rows]).astype(jnp.int32)
    other_far = to_core(pick(slots, their_owners[:4], total))
    other_near = to_core(pick(slots, their_owners[4:], total))
    far = code(slots, mine_owners[:4], total, other_far, 4)
    near = code(slots, mine_owners[4:], total, other_near, 3)
    coded = list(far) + list(near[:3])
    arrived = [to_row(v, dx, dy) for v, (dx, dy) in zip(coded, DESTS)]
    pushed = total_sum(near[3], arrived)

    row_ids = jnp.stack([(x_lo ^ dx) * 4 + (y + dy) % 4 for dx, dy in ROWS])
    wanted = (z + jnp.arange(8)) % 8
    row_of = jnp.argmax(row_ids[None, :] == wanted[:, None], axis=1).astype(jnp.int32)
    sides = jnp.stack([x_hi, core]).astype(jnp.int32)
    grad_in = grad_in_of(row_of, sides, w_mine, w_theirs, cols)
    return grad_in, pushed.reshape(1, CAP, BLK, BLK)


def solution(mesh):
    in_specs = (
        P(("row", "srv"), "col"),
        P(("row", "srv"), "col"),
        P("col", "row"),
        P("col", None, None),
        P("col", None),
    )
    out_specs = (P(("row", "srv"), "col"), P(("row", "srv"), "col", None, None))
    return jax.shard_map(body, mesh=mesh, in_specs=in_specs, out_specs=out_specs, check_vma=False)
```

time: 383 us -> 208 us (0.54)
  waiting for transfers between devices: 233 us -> 55.6 us
  starting transfers between devices: 0.12 us -> 52.7 us
  Pallas kernels: 0 us -> 42.2 us
  other arithmetic: 31.9 us -> 4.9 us
  matrix products: 25.4 us -> 0 us
  local copies, waits for them, and re-layouts: 74.4 us -> 50.4 us
  between operations: 14.4 us -> 1.21 us
    all_gather x2 -> x0, waiting for transfers between devices: 134 us -> none  [the longest x1 134 us: body(): full_grad = lax.all_gather(grad_out, 'col', axis=1, tiled=True)]
    reduce_scatter x1 -> x0, waiting for transfers between devices: 97.9 us -> none  [body(): lax.psum_scatter(holder, ('row', 'srv'), scatter_dimension=0, tiled=True)]
    ppermute x0 -> x31, waiting for transfers between devices: none -> 55.6 us  [the longest x12 26.2 us: to_row(): return lax.ppermute(v, 'row', row_shift(dx, dy))]
    ppermute x0 -> x31, starting transfers between devices: none -> 52.7 us  [the longest x12 18.1 us: to_row(): return lax.ppermute(v, 'row', row_shift(dx, dy))]
    gather x20 -> x0, local copies, waits for them, and re-layouts: 49.6 us -> none  [the longest x10 42.1 us: tile_group(): right = jnp.take(grad_tiles, col_sel, axis=1)]
    pallas_call x0 -> x12, Pallas kernels: none -> 42.2 us  [the longest x6 12.1 us: dense(): pl.pallas_call(functools.partial(dense_kernel, count, first), out_shape=j...]
    unnamed x2 -> x61, local copies, waits for them, and re-layouts: 3.3 us -> 44.1 us
    scatter-add x1 -> x0, other arithmetic: 27.2 us -> none  [body(): jnp.zeros((owner_count * CAP, BLK, BLK), jnp.float32).at[position]]
  transfers between devices with their start and end apart: 3 -> 31, of which waited for: 2 -> 11; matrix products, arithmetic and copies ran while one was open for 34% -> 9% of each run, Pallas kernels for 0% -> 16%
where the time goes in v1:
time: 208 us; the launch traced here: 207 us
  waiting for transfers between devices  55.6 us (27%)
  starting transfers between devices  52.7 us (25%)
  local copies, waits for them, and re-layouts  50.4 us (24%)
  Pallas kernels  42.2 us (20%)
  other arithmetic  4.9 us (2%)
    unnamed x61, local copies, waits for them, and re-layouts  44.1 us
    ppermute x12, waiting for transfers between devices, to_row(): return lax.ppermute(v, 'row', row_shift(dx, dy))  26.2 us
    ppermute x6, waiting for transfers between devices, up(): return lax.ppermute(v, 'col', z_shift(1))  18.9 us
    ppermute x12, starting transfers between devices, to_row(): return lax.ppermute(v, 'row', row_shift(dx, dy))  18.1 us
    ppermute x6, starting transfers between devices, down(): return lax.ppermute(v, 'col', z_shift(-1))  15.5 us
    pallas_call x6, Pallas kernels, dense(): pl.pallas_call(functools.partial(dense_kernel, count, first), out_shape=j...  12.1 us
    pallas_call x2, Pallas kernels, code(): pl.pallas_call(functools.partial(code_kernel, coded, plain), out_shape=[j...  11.9 us
    ppermute x6, waiting for transfers between devices, down(): return lax.ppermute(v, 'col', z_shift(-1))  10.5 us
  transfers between devices with their start and end apart: 31, of which 11 were waited for; matrix products, arithmetic and copies ran while one was open for 9% of the time, Pallas kernels for 16%

profile of v1, /device:TPU:1, one launch (start us, length us, event | category | flops | bytes accessed | tf_op | source)
XLA Modules:
  0.0 207.1 jit_solution(7977032868608899558)
XLA Ops:
  4.6 10.3 %collective-permute-done = bf16[256,1024]{1,0:T(8,128)(2,1)S(1)} collective-permute-done((bf16[256,1024]{1,0:T(8,128)(2,1)S(1)}, bf16[256,1024]{1,0:T(8,128)(2,1)S(1)}, u32[]{:S(2)}, u32[]{:S(2)}) %collective-permute-start) | collective-permute-done | bytes 524320 | tf_op jit(solution)/shard_map/ppermute | solution.py:276
  21.6 2.7 %collective-permute-start.8 = (bf16[512,512]{1,0:T(8,128)(2,1)}, bf16[512,512]{1,0:T(8,128)(2,1)S(1)}, u32[]{:S(2)}, u32[]{:S(2)}) collective-permute-start(bf16[512,512]{1,0:T(8,128)(2,1)} %refs_0_.3), channel_id=1, source_target_pairs={{0,2},{2,0},{4,6},{6,4},{8,10},{10,8},{12,14},{14,12},{16,18},{18,... | collective-permute-start | bytes 1572872 | tf_op jit(solution)/shard_map/ppermute | solution.py:273
  24.3 3.9 %collective-permute-start.7 = (bf16[512,512]{1,0:T(8,128)(2,1)}, bf16[512,512]{1,0:T(8,128)(2,1)S(1)}, u32[]{:S(2)}, u32[]{:S(2)}) collective-permute-start(bf16[512,512]{1,0:T(8,128)(2,1)} %refs_0_.3), channel_id=1, source_target_pairs={{0,28},{2,30},{4,0},{6,2},{8,4},{10,6},{12,8},{14,10},{16,12},{18,... | collective-permute-start | bytes 1572872 | tf_op jit(solution)/shard_map/ppermute | solution.py:270
  29.9 6.2 %collective-permute-done.6.refs_1_.refs_0_ = bf16[512,512]{1,0:T(8,128)(2,1)S(1)} collective-permute-done((bf16[512,512]{1,0:T(8,128)(2,1)}, bf16[512,512]{1,0:T(8,128)(2,1)S(1)}, u32[]{:S(2)}, u32[]{:S(2)}) %collective-permute-start.6) | collective-permute-done | bytes 524320 | tf_op jit(solution)/shard_map/ppermute | solution.py:267
  37.5 3.4 %collective-permute-start.10 = (bf16[512,512]{1,0:T(8,128)(2,1)S(1)}, bf16[512,512]{1,0:T(8,128)(2,1)S(1)}, u32[]{:S(2)}, u32[]{:S(2)}) collective-permute-start(bf16[512,512]{1,0:T(8,128)(2,1)S(1)} %collective-permute-done.7.refs_2_.refs_1_), channel_id=1, source_target_pairs={{0,28},{2,30},{4,0},{6,2},{8,4},{10,6},{12,8},{14,10},{16,12},{18,... | collective-permute-start | bytes 1572872 | tf_op jit(solution)/shard_map/ppermute | solution.py:270
  54.9 2.7 %collective-permute-start.17 = (bf16[512,512]{1,0:T(8,128)(2,1)S(1)}, bf16[512,512]{1,0:T(8,128)(2,1)}, u32[]{:S(2)}, u32[]{:S(2)}) collective-permute-start(bf16[512,512]{1,0:T(8,128)(2,1)S(1)} %collective-permute-done.9.refs_4_.refs_0_), channel_id=1, source_target_pairs={{0,2},{2,0},{4,6},{6,4},{8,10},{10,8},{12,14},{14,12},{16,18},{18,... | collective-permute-start | bytes 1572872 | tf_op jit(solution)/shard_map/ppermute | solution.py:273
  57.7 4.3 %collective-permute-start.12 = (bf16[512,512]{1,0:T(8,128)(2,1)}, bf16[512,512]{1,0:T(8,128)(2,1)S(1)}, u32[]{:S(2)}, u32[]{:S(2)}) collective-permute-start(bf16[512,512]{1,0:T(8,128)(2,1)} %copy-done.11), channel_id=1, source_target_pairs={{0,28},{2,30},{4,0},{6,2},{8,4},{10,6},{12,8},{14,10},{16,12},{18,... | collective-permute-start | bytes 1572872 | tf_op jit(solution)/shard_map/ppermute | solution.py:270
  64.8 3.6 %collective-permute-start.5 = (bf16[8,256,1024]{2,1,0:T(8,128)(2,1)}, bf16[8,256,1024]{2,1,0:T(8,128)(2,1)}, u32[]{:S(2)}, u32[]{:S(2)}) collective-permute-start(bf16[8,256,1024]{2,1,0:T(8,128)(2,1)} %bitcast.79), channel_id=1, source_target_pairs={{0,1},{1,0},{2,3},{3,2},{4,5},{5,4},{6,7},{7,6},{8,9},{9,8},{10,11... | collective-permute-start | bytes 12582920 | tf_op jit(solution)/shard_map/ppermute | solution.py:279
  68.4 2.8 %collective-permute-start.18 = (bf16[512,512]{1,0:T(8,128)(2,1)}, bf16[512,512]{1,0:T(8,128)(2,1)}, u32[]{:S(2)}, u32[]{:S(2)}) collective-permute-start(bf16[512,512]{1,0:T(8,128)(2,1)} %copy-done.11), channel_id=1, source_target_pairs={{0,2},{2,0},{4,6},{6,4},{8,10},{10,8},{12,14},{14,12},{16,18},{18,... | collective-permute-start | bytes 1572872 | tf_op jit(solution)/shard_map/ppermute | solution.py:273
  78.7 12.7 %collective-permute-done.13 = bf16[256,512]{1,0:T(8,128)(2,1)S(1)} collective-permute-done((bf16[256,512]{1,0:T(8,128)(2,1)}, bf16[256,512]{1,0:T(8,128)(2,1)S(1)}, u32[]{:S(2)}, u32[]{:S(2)}) %collective-permute-start.13) | collective-permute-done | bytes 262176 | tf_op jit(solution)/shard_map/ppermute | solution.py:267
  101.0 2.8 %collective-permute-done.16.refs_10_.refs_2_ = bf16[512,512]{1,0:T(8,128)(2,1)S(1)} collective-permute-done((bf16[512,512]{1,0:T(8,128)(2,1)S(1)}, bf16[512,512]{1,0:T(8,128)(2,1)S(1)}, u32[]{:S(2)}, u32[]{:S(2)}) %collective-permute-start.16) | collective-permute-done | bytes 524320 | tf_op jit(solution)/shard_map/ppermute | solution.py:270
  103.7 4.2 %shard_map.73.refs_3_ = f32[16,16,128,128]{3,2,1,0:T(8,128)S(1)} custom-call(s32[5]{0:T(128)S(1)} %stack.183.where_ref, bf16[512,512]{1,0:T(8,128)(2,1)S(1)} %bitcast.77, bf16[512,512]{1,0:T(8,128)(2,1)S(1)} %constant_dynamic-update-slice_fusion.6.refs_8_.refs_0_, ...), custom_call_target="tpu_custom_call", output_to_operand_aliasing={{}: (7, {})} | custom-call | flops 1342177280 | bytes 7864320 | tf_op jit(solution)/shard_map/pallas_call | solution.py:72
  107.9 7.0 %collective-permute-done.20.refs_14_.refs_1_ = bf16[512,512]{1,0:T(8,128)(2,1)S(1)} collective-permute-done((bf16[512,512]{1,0:T(8,128)(2,1)}, bf16[512,512]{1,0:T(8,128)(2,1)S(1)}, u32[]{:S(2)}, u32[]{:S(2)}) %collective-permute-start.20) | collective-permute-done | bytes 524320 | tf_op jit(solution)/shard_map/ppermute | solution.py:270
  119.7 3.8 %copy-done = f32[16,16,128,128]{3,2,1,0:T(8,128)} copy-done((f32[16,16,128,128]{3,2,1,0:T(8,128)}, f32[16,16,128,128]{3,2,1,0:T(8,128)S(1)}, u32[]{:S(2)}) %copy-start) | copy-done | bytes 16777240
  125.6 5.8 %copy-done.1 = f32[16,16,128,128]{3,2,1,0:T(8,128)S(1)} copy-done((f32[16,16,128,128]{3,2,1,0:T(8,128)S(1)}, f32[16,16,128,128]{3,2,1,0:T(8,128)}, u32[]{:S(2)}) %copy-start.1) | copy-done | bytes 16777240
  133.7 5.8 %copy-done.2 = f32[16,16,128,128]{3,2,1,0:T(8,128)S(1)} copy-done((f32[16,16,128,128]{3,2,1,0:T(8,128)S(1)}, f32[16,16,128,128]{3,2,1,0:T(8,128)}, u32[]{:S(2)}) %copy-start.2) | copy-done | bytes 16777240
  139.5 6.0 %shard_map.78 = (bf16[1040,128]{1,0:T(8,128)(2,1)}, bf16[1040,128]{1,0:T(8,128)(2,1)}, bf16[1040,128]{1,0:T(8,128)(2,1)}, bf16[1040,128]{1,0:T(8,128)(2,1)}) custom-call(s32[128]{0:T(128)S(1)} %broadcast_add_fusion.slot_ref, s32[4]{0:T(128)S(1)} %pad_add_fusion.7.row_ref, f32[256,128,128]{2,1,0:T(8,128)S(1)} %bitcast.71, ...), custom_call_target="tpu_custom_call" | custom-call | flops 4194304 | bytes 5242880 | tf_op jit(solution)/shard_map/pallas_call | solution.py:168
  145.9 3.6 %collective-permute-start.26 = (bf16[1040,128]{1,0:T(8,128)(2,1)}, bf16[1040,128]{1,0:T(8,128)(2,1)}, u32[]{:S(2)}, u32[]{:S(2)}) collective-permute-start(bf16[1040,128]{1,0:T(8,128)(2,1)} %get-tuple-element.15), channel_id=1, source_target_pairs={{0,224},{32,128},{64,160},{96,192},{128,96},{160,0},{192,32},{224,... | collective-permute-start | bytes 798728 | tf_op jit(solution)/shard_map/ppermute | solution.py:276
  149.6 5.8 %copy-done.3 = f32[16,16,128,128]{3,2,1,0:T(8,128)S(1)} copy-done((f32[16,16,128,128]{3,2,1,0:T(8,128)S(1)}, f32[16,16,128,128]{3,2,1,0:T(8,128)}, u32[]{:S(2)}) %copy-start.3) | copy-done | bytes 16777240
  155.4 5.9 %shard_map.76 = (bf16[1040,128]{1,0:T(8,128)(2,1)}, bf16[1040,128]{1,0:T(8,128)(2,1)}, bf16[1040,128]{1,0:T(8,128)(2,1)}, f32[8,128,128]{2,1,0:T(8,128)S(1)}) custom-call(s32[128]{0:T(128)S(1)} %broadcast_add_fusion.slot_ref, s32[4]{0:T(128)S(1)} %pad_add_fusion.1.row_ref, f32[256,128,128]{2,1,0:T(8,128)S(1)} %bitcast.72, ...), custom_call_target="tpu_custom_call" | custom-call | flops 4194304 | bytes 5242880 | tf_op jit(solution)/shard_map/pallas_call | solution.py:168
  170.6 5.9 %collective-permute-done.28.refs_4_ = bf16[1040,128]{1,0:T(8,128)(2,1)} collective-permute-done((bf16[1040,128]{1,0:T(8,128)(2,1)}, bf16[1040,128]{1,0:T(8,128)(2,1)}, u32[]{:S(2)}, u32[]{:S(2)}) %collective-permute-start.28) | collective-permute-done | bytes 266272 | tf_op jit(solution)/shard_map/ppermute | solution.py:276
  176.6 5.0 %collective-permute-done.29.refs_5_ = bf16[1040,128]{1,0:T(8,128)(2,1)} collective-permute-done((bf16[1040,128]{1,0:T(8,128)(2,1)}, bf16[1040,128]{1,0:T(8,128)(2,1)}, u32[]{:S(2)}, u32[]{:S(2)}) %collective-permute-start.29) | collective-permute-done | bytes 266272 | tf_op jit(solution)/shard_map/ppermute | solution.py:276
  183.9 3.7 %shard_map.79 = f32[8,128,128]{2,1,0:T(8,128)} custom-call(f32[8,128,128]{2,1,0:T(8,128)S(1)} %copy-done.25, bf16[1040,128]{1,0:T(8,128)(2,1)S(1)} %collective-permute-done.24.refs_0_, bf16[1040,128]{1,0:T(8,128)(2,1)} %collective-permute-done.25.refs_1_, bf16[1040,128]{1,0:T(8,128)(2,1)} %collective-permute-done.26.refs_2_, ...), custom_call_target="tpu_custom_call" | custom-call | flops 8388608 | bytes 2097152 | tf_op jit(solution)/shard_map/pallas_call | solution.py:204
  197.0 9.8 %shard_map.68 = bf16[512,512]{1,0:T(8,128)(2,1)} custom-call(s32[8]{0:T(128)S(1)} %get-tuple-element.11.row_of_ref, s32[2]{0:T(128)S(1)} %pad_add_fusion.half_ref, bf16[8,256,1024]{2,1,0:T(8,128)(2,1)S(1)} %bitcast.80, bf16[8,256,1024]{2,1,0:T(8,128)(2,1)} %collective-permute-done.5.theirs, bf16[512,512]{1,0:T(8,128)(2,1)S(1)} %copy-done.23, ...), custom_call_target="tpu_custom_call" | custom-call | flops 4294967296 | bytes 17825792 | tf_op jit(solution)/shard_map/pallas_call | solution.py:242
  (137 shorter events, 78.2 us)
Async XLA Ops:
  15.9 26.2 %collective-permute-start.1 = (bf16[512,1024]{1,0:T(8,128)(2,1)}, bf16[512,1024]{1,0:T(8,128)(2,1)}, u32[]{:S(2)}, u32[]{:S(2)}) collective-permute-start(bf16[512,1024]{1,0:T(8,128)(2,1)} %pad_maximum_fusion), channel_id=1, source_target_pairs={{0,32},{32,64},{64,96},{96,0},{128,160},{160,192},{192,224},{224,1... | collective-permute-start | bytes 3145736 | tf_op jit(solution)/shard_map/ppermute | solution.py:276
  18.5 25.7 %collective-permute-start.2 = (bf16[512,1024]{1,0:T(8,128)(2,1)}, bf16[512,1024]{1,0:T(8,128)(2,1)}, u32[]{:S(2)}, u32[]{:S(2)}) collective-permute-start(bf16[512,1024]{1,0:T(8,128)(2,1)} %pad_maximum_fusion), channel_id=1, source_target_pairs={{0,96},{32,0},{64,32},{96,64},{128,224},{160,128},{192,160},{224,1... | collective-permute-start | bytes 3145736 | tf_op jit(solution)/shard_map/ppermute | solution.py:276
  20.0 16.1 %collective-permute-start.6 = (bf16[512,512]{1,0:T(8,128)(2,1)}, bf16[512,512]{1,0:T(8,128)(2,1)S(1)}, u32[]{:S(2)}, u32[]{:S(2)}) collective-permute-start(bf16[512,512]{1,0:T(8,128)(2,1)} %refs_0_.3), channel_id=1, source_target_pairs={{0,4},{2,6},{4,8},{6,10},{8,12},{10,14},{12,16},{14,18},{16,20},{1... | collective-permute-start | bytes 1572872 | tf_op jit(solution)/shard_map/ppermute | solution.py:267
  21.6 46.8 %collective-permute-start.8 = (bf16[512,512]{1,0:T(8,128)(2,1)}, bf16[512,512]{1,0:T(8,128)(2,1)S(1)}, u32[]{:S(2)}, u32[]{:S(2)}) collective-permute-start(bf16[512,512]{1,0:T(8,128)(2,1)} %refs_0_.3), channel_id=1, source_target_pairs={{0,2},{2,0},{4,6},{6,4},{8,10},{10,8},{12,14},{14,12},{16,18},{18,... | collective-permute-start | bytes 1572872 | tf_op jit(solution)/shard_map/ppermute | solution.py:273
  37.5 17.4 %collective-permute-start.10 = (bf16[512,512]{1,0:T(8,128)(2,1)S(1)}, bf16[512,512]{1,0:T(8,128)(2,1)S(1)}, u32[]{:S(2)}, u32[]{:S(2)}) collective-permute-start(bf16[512,512]{1,0:T(8,128)(2,1)S(1)} %collective-permute-done.7.refs_2_.refs_1_), channel_id=1, source_target_pairs={{0,28},{2,30},{4,0},{6,2},{8,4},{10,6},{12,8},{14,10},{16,12},{18,... | collective-permute-start | bytes 1572872 | tf_op jit(solution)/shard_map/ppermute | solution.py:270
  45.3 18.5 %collective-permute-start.4 = (bf16[256,1024]{1,0:T(8,128)(2,1)S(1)}, bf16[256,1024]{1,0:T(8,128)(2,1)S(1)}, u32[]{:S(2)}, u32[]{:S(2)}) collective-permute-start(bf16[256,1024]{1,0:T(8,128)(2,1)S(1)} %slice.34), channel_id=1, source_target_pairs={{0,96},{32,0},{64,32},{96,64},{128,224},{160,128},{192,160},{224,1... | collective-permute-start | bytes 1572872 | tf_op jit(solution)/shard_map/ppermute | solution.py:276
  48.9 22.4 %collective-permute-start.11 = (bf16[512,512]{1,0:T(8,128)(2,1)S(1)}, bf16[512,512]{1,0:T(8,128)(2,1)S(1)}, u32[]{:S(2)}, u32[]{:S(2)}) collective-permute-start(bf16[512,512]{1,0:T(8,128)(2,1)S(1)} %collective-permute-done.9.refs_4_.refs_0_), channel_id=1, source_target_pairs={{0,4},{2,6},{4,8},{6,10},{8,12},{10,14},{12,16},{14,18},{16,20},{1... | collective-permute-start | bytes 1572872 | tf_op jit(solution)/shard_map/ppermute | solution.py:267
  54.9 18.0 %collective-permute-start.17 = (bf16[512,512]{1,0:T(8,128)(2,1)S(1)}, bf16[512,512]{1,0:T(8,128)(2,1)}, u32[]{:S(2)}, u32[]{:S(2)}) collective-permute-start(bf16[512,512]{1,0:T(8,128)(2,1)S(1)} %collective-permute-done.9.refs_4_.refs_0_), channel_id=1, source_target_pairs={{0,2},{2,0},{4,6},{6,4},{8,10},{10,8},{12,14},{14,12},{16,18},{18,... | collective-permute-start | bytes 1572872 | tf_op jit(solution)/shard_map/ppermute | solution.py:273
  64.8 122.8 %collective-permute-start.5 = (bf16[8,256,1024]{2,1,0:T(8,128)(2,1)}, bf16[8,256,1024]{2,1,0:T(8,128)(2,1)}, u32[]{:S(2)}, u32[]{:S(2)}) collective-permute-start(bf16[8,256,1024]{2,1,0:T(8,128)(2,1)} %bitcast.79), channel_id=1, source_target_pairs={{0,1},{1,0},{2,3},{3,2},{4,5},{5,4},{6,7},{7,6},{8,9},{9,8},{10,11... | collective-permute-start | bytes 12582920 | tf_op jit(solution)/shard_map/ppermute | solution.py:279
  68.4 23.1 %collective-permute-start.18 = (bf16[512,512]{1,0:T(8,128)(2,1)}, bf16[512,512]{1,0:T(8,128)(2,1)}, u32[]{:S(2)}, u32[]{:S(2)}) collective-permute-start(bf16[512,512]{1,0:T(8,128)(2,1)} %copy-done.11), channel_id=1, source_target_pairs={{0,2},{2,0},{4,6},{6,4},{8,10},{10,8},{12,14},{14,12},{16,18},{18,... | collective-permute-start | bytes 1572872 | tf_op jit(solution)/shard_map/ppermute | solution.py:273
  71.3 23.9 %collective-permute-start.15 = (bf16[512,512]{1,0:T(8,128)(2,1)S(1)}, bf16[512,512]{1,0:T(8,128)(2,1)}, u32[]{:S(2)}, u32[]{:S(2)}) collective-permute-start(bf16[512,512]{1,0:T(8,128)(2,1)S(1)} %collective-permute-done.8.refs_3_.refs_2_), channel_id=1, source_target_pairs={{0,4},{2,6},{4,8},{6,10},{8,12},{10,14},{12,16},{14,18},{16,20},{1... | collective-permute-start | bytes 1572872 | tf_op jit(solution)/shard_map/ppermute | solution.py:267
  72.1 19.3 %collective-permute-start.13 = (bf16[256,512]{1,0:T(8,128)(2,1)}, bf16[256,512]{1,0:T(8,128)(2,1)S(1)}, u32[]{:S(2)}, u32[]{:S(2)}) collective-permute-start(bf16[256,512]{1,0:T(8,128)(2,1)} %slice.35), channel_id=1, source_target_pairs={{0,4},{2,6},{4,8},{6,10},{8,12},{10,14},{12,16},{14,18},{16,20},{1... | collective-permute-start | bytes 786440 | tf_op jit(solution)/shard_map/ppermute | solution.py:267
  72.9 20.1 %collective-permute-start.14 = (bf16[256,512]{1,0:T(8,128)(2,1)}, bf16[256,512]{1,0:T(8,128)(2,1)}, u32[]{:S(2)}, u32[]{:S(2)}) collective-permute-start(bf16[256,512]{1,0:T(8,128)(2,1)} %slice.36), channel_id=1, source_target_pairs={{0,28},{2,30},{4,0},{6,2},{8,4},{10,6},{12,8},{14,10},{16,12},{18,... | collective-permute-start | bytes 786440 | tf_op jit(solution)/shard_map/ppermute | solution.py:270
  91.4 16.5 %collective-permute-start.19 = (bf16[512,512]{1,0:T(8,128)(2,1)}, bf16[512,512]{1,0:T(8,128)(2,1)S(1)}, u32[]{:S(2)}, u32[]{:S(2)}) collective-permute-start(bf16[512,512]{1,0:T(8,128)(2,1)} %collective-permute-done.17.refs_11_.refs_3_), channel_id=1, source_target_pairs={{0,4},{2,6},{4,8},{6,10},{8,12},{10,14},{12,16},{14,18},{16,20},{1... | collective-permute-start | bytes 1572872 | tf_op jit(solution)/shard_map/ppermute | solution.py:267
  93.0 22.0 %collective-permute-start.20 = (bf16[512,512]{1,0:T(8,128)(2,1)}, bf16[512,512]{1,0:T(8,128)(2,1)S(1)}, u32[]{:S(2)}, u32[]{:S(2)}) collective-permute-start(bf16[512,512]{1,0:T(8,128)(2,1)} %collective-permute-done.18.refs_12_.refs_4_), channel_id=1, source_target_pairs={{0,28},{2,30},{4,0},{6,2},{8,4},{10,6},{12,8},{14,10},{16,12},{18,... | collective-permute-start | bytes 1572872 | tf_op jit(solution)/shard_map/ppermute | solution.py:270
  95.2 19.8 %collective-permute-start.21 = (bf16[512,512]{1,0:T(8,128)(2,1)S(1)}, bf16[512,512]{1,0:T(8,128)(2,1)S(1)}, u32[]{:S(2)}, u32[]{:S(2)}) collective-permute-start(bf16[512,512]{1,0:T(8,128)(2,1)S(1)} %constant_dynamic-update-slice_fusion.6.refs_8_.refs_0_), channel_id=1, source_target_pairs={{0,2},{2,0},{4,6},{6,4},{8,10},{10,8},{12,14},{14,12},{16,18},{18,... | collective-permute-start | bytes 1572872 | tf_op jit(solution)/shard_map/ppermute | solution.py:273
  133.5 16.0 %collective-permute-start.22 = (f32[32,128,128]{2,1,0:T(8,128)}, f32[32,128,128]{2,1,0:T(8,128)}, u32[]{:S(2)}, u32[]{:S(2)}) collective-permute-start(f32[32,128,128]{2,1,0:T(8,128)} %shard_map.75), channel_id=1, source_target_pairs={{0,1},{1,0},{2,3},{3,2},{4,5},{5,4},{6,7},{7,6},{8,9},{9,8},{10,11... | collective-permute-start | bytes 6291464 | tf_op jit(solution)/shard_map/ppermute | solution.py:279
  145.5 16.6 %collective-permute-start.24 = (bf16[1040,128]{1,0:T(8,128)(2,1)}, bf16[1040,128]{1,0:T(8,128)(2,1)S(1)}, u32[]{:S(2)}, u32[]{:S(2)}) collective-permute-start(bf16[1040,128]{1,0:T(8,128)(2,1)} %get-tuple-element.13), channel_id=1, source_target_pairs={{0,128},{32,160},{64,192},{96,224},{128,0},{160,32},{192,64},{224,... | collective-permute-start | bytes 798728 | tf_op jit(solution)/shard_map/ppermute | solution.py:276
  145.9 16.7 %collective-permute-start.25 = (bf16[1040,128]{1,0:T(8,128)(2,1)}, bf16[1040,128]{1,0:T(8,128)(2,1)}, u32[]{:S(2)}, u32[]{:S(2)}) collective-permute-start(bf16[1040,128]{1,0:T(8,128)(2,1)} %get-tuple-element.14), channel_id=1, source_target_pairs={{0,160},{32,192},{64,224},{96,128},{128,32},{160,64},{192,96},{224... | collective-permute-start | bytes 798728 | tf_op jit(solution)/shard_map/ppermute | solution.py:276
  145.9 18.9 %collective-permute-start.26 = (bf16[1040,128]{1,0:T(8,128)(2,1)}, bf16[1040,128]{1,0:T(8,128)(2,1)}, u32[]{:S(2)}, u32[]{:S(2)}) collective-permute-start(bf16[1040,128]{1,0:T(8,128)(2,1)} %get-tuple-element.15), channel_id=1, source_target_pairs={{0,224},{32,128},{64,160},{96,192},{128,96},{160,0},{192,32},{224,... | collective-permute-start | bytes 798728 | tf_op jit(solution)/shard_map/ppermute | solution.py:276
  149.5 21.1 %collective-permute-start.27 = (bf16[1040,128]{1,0:T(8,128)(2,1)}, bf16[1040,128]{1,0:T(8,128)(2,1)}, u32[]{:S(2)}, u32[]{:S(2)}) collective-permute-start(bf16[1040,128]{1,0:T(8,128)(2,1)} %get-tuple-element.16), channel_id=1, source_target_pairs={{0,192},{32,224},{64,128},{96,160},{128,64},{160,96},{192,0},{224,... | collective-permute-start | bytes 798728 | tf_op jit(solution)/shard_map/ppermute | solution.py:276
  162.1 14.5 %collective-permute-start.28 = (bf16[1040,128]{1,0:T(8,128)(2,1)}, bf16[1040,128]{1,0:T(8,128)(2,1)}, u32[]{:S(2)}, u32[]{:S(2)}) collective-permute-start(bf16[1040,128]{1,0:T(8,128)(2,1)} %get-tuple-element.17), channel_id=1, source_target_pairs={{0,32},{32,64},{64,96},{96,0},{128,160},{160,192},{192,224},{224,1... | collective-permute-start | bytes 798728 | tf_op jit(solution)/shard_map/ppermute | solution.py:276
  162.6 18.9 %collective-permute-start.29 = (bf16[1040,128]{1,0:T(8,128)(2,1)}, bf16[1040,128]{1,0:T(8,128)(2,1)}, u32[]{:S(2)}, u32[]{:S(2)}) collective-permute-start(bf16[1040,128]{1,0:T(8,128)(2,1)} %get-tuple-element.18), channel_id=1, source_target_pairs={{0,96},{32,0},{64,32},{96,64},{128,224},{160,128},{192,160},{224,1... | collective-permute-start | bytes 798728 | tf_op jit(solution)/shard_map/ppermute | solution.py:276
  164.7 18.1 %collective-permute-start.30 = (bf16[1040,128]{1,0:T(8,128)(2,1)}, bf16[1040,128]{1,0:T(8,128)(2,1)}, u32[]{:S(2)}, u32[]{:S(2)}) collective-permute-start(bf16[1040,128]{1,0:T(8,128)(2,1)} %get-tuple-element.19), channel_id=1, source_target_pairs={{0,64},{32,96},{64,0},{96,32},{128,192},{160,224},{192,128},{224,1... | collective-permute-start | bytes 798728 | tf_op jit(solution)/shard_map/ppermute | solution.py:276
  (34 other events, 277.9 us)

commit v2 on v0

v2 whole, which is shorter than its diff:
```python
import functools

import jax
import jax.numpy as jnp
import numpy as np
from jax import lax
from jax.experimental import pallas as pl
from jax.experimental.pallas import tpu as pltpu
from jax.sharding import PartitionSpec as P

BLK = 128
CAP = 8
POWER = 9
TOP = 13.0
TAIL = 16
F32 = jnp.float32
BF16 = jnp.bfloat16

COLS = ((0, 0), (-1, 0), (1, 0), (-2, 0), (2, 0), (0, 1), (-3, 0), (3, 0), (-2, 1),
        (-4, 0), (-1, 1), (1, 1), (2, 1), (-3, 1), (3, 1), (-4, 1))
LAST = 13
DESTS = ((1, 0), (1, 1), (1, 3), (1, 2), (0, 2), (0, 1), (0, 3), (0, 0))
EARLY = 2
DENSE_MIB = PICK_MIB = CODE_MIB = GRAD_MIB = 20
COL_AT, ROW_AT, SIDE_AT, MINE_AT, THEIRS_AT, SLOT_AT = 0, 16, 48, 50, 58, 66


def z_shift(d):
    return [((z * 2 + h) * 2 + c, (((z + (1 - 2 * c) * d) % 8) * 2 + h) * 2 + c)
            for z in range(8) for h in range(2) for c in range(2)]


def y_shift(d):
    return [((l * 4 + y) * 2 + c, (l * 4 + (y + (1 - 2 * c) * d) % 4) * 2 + c)
            for l in range(2) for y in range(4) for c in range(2)]


def row_shift(dx, dy):
    return [(l * 4 + y, (l ^ dx) * 4 + (y + dy) % 4) for l in range(2) for y in range(4)]


X_SWAP = [(z * 2 + h, z * 2 + 1 - h) for z in range(8) for h in range(2)]
CORE_SWAP = [(0, 1), (1, 0)]


def hbm_spec():
    return pl.BlockSpec(memory_space=pltpu.HBM)


def smem_spec():
    return pl.BlockSpec(memory_space=pltpu.SMEM)


def vmem_spec():
    return pl.BlockSpec(memory_space=pltpu.VMEM)


def params(mib):
    return pltpu.CompilerParams(vmem_limit_bytes=mib * 1024 * 1024)


def dense_kernel(count, place, first, table, xt_ref, *refs):
    blocks = refs[:count]
    out = refs[count + (0 if first else 1)]
    for j in range(count):
        acc = jnp.dot(xt_ref[...], blocks[j][...], preferred_element_type=F32)
        at = table[COL_AT + place + j] * 16
        for cc in range(4):
            for rb in range(4):
                out[at + cc * 4 + rb] = acc[rb * BLK:(rb + 1) * BLK, cc * BLK:(cc + 1) * BLK]


def dense(total, table, xt, blocks, place):
    count = len(blocks)
    first = total is None
    args = [table, xt, *blocks] + ([] if first else [total])
    return pl.pallas_call(
        functools.partial(dense_kernel, count, place, first),
        out_shape=jax.ShapeDtypeStruct((256, BLK, BLK), F32),
        in_specs=[smem_spec(), vmem_spec()] + [vmem_spec()] * count + ([] if first else [vmem_spec()]),
        out_specs=vmem_spec(),
        input_output_aliases={} if first else {2 + count: 0},
        compiler_params=params(DENSE_MIB),
        cost_estimate=pl.CostEstimate(
            flops=count * 2 * 512 ** 3, bytes_accessed=count * 3 * 512 * 1024, transcendentals=0),
    )(*args)


def slot_tile(table, owner_at, i):
    return table[SLOT_AT + table[owner_at + i // CAP] * CAP + i % CAP]


def pick_kernel(first, chunks, table, total, out):
    for i in range(chunks * CAP):
        out[i] = total[jnp.maximum(slot_tile(table, THEIRS_AT + first, i), 0)]


def pick(table, first, last, total):
    chunks = last - first
    return pl.pallas_call(
        functools.partial(pick_kernel, first, chunks),
        out_shape=jax.ShapeDtypeStruct((chunks * CAP, BLK, BLK), F32),
        in_specs=[smem_spec(), vmem_spec()],
        out_specs=vmem_spec(),
        compiler_params=params(PICK_MIB),
        cost_estimate=pl.CostEstimate(
            flops=0, bytes_accessed=chunks * CAP * BLK * BLK * 8, transcendentals=0),
    )(table, total)


def code_kernel(at, coded, plain, table, total, other, *refs):
    chunks = coded + plain
    outs, held = refs[:chunks], refs[chunks]
    for m in range(chunks):
        most = jnp.zeros((1, BLK), F32)
        for t in range(CAP):
            i = m * CAP + t
            tile = slot_tile(table, MINE_AT + at, i)
            both = jnp.where(tile >= 0, total[jnp.maximum(tile, 0)] + other[i], 0.0)
            if m >= coded:
                outs[m][t] = both
            else:
                held[t] = both
                most = jnp.maximum(most, jnp.max(jnp.abs(both), axis=0, keepdims=True))
        if m < coded:
            level = jnp.ceil(jnp.log2(jnp.maximum(most, 1e-30)))
            scale = jnp.exp2(TOP - level)
            for t in range(CAP):
                v = held[t] * scale
                v2 = v * v
                v4 = v2 * v2
                outs[m][t * BLK:(t + 1) * BLK, :] = (v4 * v4 * v).astype(BF16)
            outs[m][CAP * BLK:, :] = jnp.broadcast_to(level, (TAIL, BLK)).astype(BF16)


def code(table, first, last, total, other, plain):
    chunks = last - first
    coded = chunks - plain
    return pl.pallas_call(
        functools.partial(code_kernel, first, coded, plain),
        out_shape=[jax.ShapeDtypeStruct((CAP * BLK + TAIL, BLK), BF16)] * coded
        + [jax.ShapeDtypeStruct((CAP, BLK, BLK), F32)] * plain,
        in_specs=[smem_spec(), vmem_spec(), vmem_spec()],
        out_specs=[vmem_spec()] * chunks,
        scratch_shapes=[pltpu.VMEM((CAP, BLK, BLK), F32)],
        compiler_params=params(CODE_MIB),
        cost_estimate=pl.CostEstimate(
            flops=chunks * CAP * BLK * BLK * 8, bytes_accessed=chunks * CAP * BLK * BLK * 10,
            transcendentals=0),
    )(table, total, other)


def sum_kernel(own, *refs):
    arrived, out = refs[:-1], refs[-1]
    scales = []
    for ref in arrived:
        level = ref[CAP * BLK:CAP * BLK + TAIL, :].astype(F32)[0:1, :]
        scales.append(level - TOP)
    for t in range(CAP):
        acc = own[t]
        for ref, scale in zip(arrived, scales):
            y = ref[t * BLK:(t + 1) * BLK, :].astype(F32)
            size = jnp.exp2(jnp.log2(jnp.maximum(jnp.abs(y), 1e-37)) * (1.0 / POWER) + scale)
            size = jnp.where(jnp.abs(y) > 1e-37, size, 0.0)
            acc = acc + jnp.where(y < 0, -size, size)
        out[t] = acc


def total_sum(own, arrived):
    return pl.pallas_call(
        sum_kernel,
        out_shape=jax.ShapeDtypeStruct((CAP, BLK, BLK), F32),
        in_specs=[vmem_spec()] * (1 + len(arrived)),
        out_specs=vmem_spec(),
        compiler_params=params(24),
        cost_estimate=pl.CostEstimate(
            flops=8 * CAP * BLK * BLK * 8, bytes_accessed=8 * CAP * BLK * BLK * 2,
            transcendentals=0),
    )(own, *arrived)


def grad_kernel(ids, has_sum, last, table, *refs):
    count = len(ids)
    blocks, parts = refs[:count], refs[count:count + 8]
    refs = refs[count + 8:]
    before = refs[0] if has_sum else None
    out, weights, total = refs[1 if has_sum else 0:]
    side = table[SIDE_AT]
    core = table[SIDE_AT + 1]
    for k in range(8):
        weights[core if k < 4 else 1 - core, (k % 4) * 512:(k % 4 + 1) * 512, :] = parts[k][...]
    for k, place in enumerate(ids):
        dxh = COLS[place][1]
        first = pl.multiple_of((side if dxh == 0 else 1 - side) * 512, 512)
        for h in range(2):
            row = pl.multiple_of(table[ROW_AT + h * 16 + place] * 256, 256)
            made = lax.dot_general(
                blocks[k][...], weights[h, pl.ds(row, 256), pl.ds(first, 512)],
                (((1,), (1,)), ((), ())), preferred_element_type=F32)
            cols = slice(h * 256, (h + 1) * 256)
            if k > 0:
                made = made + total[:, cols]
            elif has_sum:
                made = made + before[:, cols]
            if k < count - 1:
                total[:, cols] = made
            else:
                out[:, cols] = made.astype(out.dtype)


def grad_sum(table, ids, blocks, parts, before, last):
    count = len(ids)
    has_sum = before is not None
    return pl.pallas_call(
        functools.partial(grad_kernel, tuple(ids), has_sum, last),
        out_shape=jax.ShapeDtypeStruct((512, 512), BF16 if last else F32),
        in_specs=[smem_spec()] + [vmem_spec()] * (count + 8 + has_sum),
        out_specs=vmem_spec(),
        scratch_shapes=[pltpu.VMEM((2, 2048, 1024), BF16), pltpu.VMEM((512, 512), F32)],
        compiler_params=params(GRAD_MIB),
        cost_estimate=pl.CostEstimate(
            flops=2 * 512 ** 3 * count, bytes_accessed=(8 + count) * 1024 * 1024, transcendentals=0),
    )(table, *blocks, *parts, *([before] if has_sum else []))


def body(inputs, grad_out, weight, blocks, owner):
    row = lax.axis_index("row")
    col = lax.axis_index("col")
    core = lax.axis_index("srv")
    x_lo, y = row // 4, row % 4
    z, x_hi = col // 2, col % 2

    sign = 1 - 2 * core

    def ahead(v):
        return lax.ppermute(v, ("col", "srv"), z_shift(1))

    def back(v):
        return lax.ppermute(v, ("col", "srv"), z_shift(-1))

    def across(v):
        return lax.ppermute(v, "col", X_SWAP)

    def around(v):
        return lax.ppermute(v, ("row", "srv"), y_shift(1))

    def to_row(v, dx, dy):
        return lax.ppermute(v, "row", row_shift(dx, dy))

    def to_core(v):
        return lax.ppermute(v, "srv", CORE_SWAP)

    together = lax.optimization_barrier

    listed = blocks[0]
    owners = owner[0]
    live = listed[:, 0] >= 0
    order = jnp.arange(listed.shape[0], dtype=jnp.int32)
    same = owners[:, None] == owners[None, :]
    earlier = order[None, :] < order[:, None]
    rank = jnp.sum((same & earlier & live[None, :]).astype(jnp.int32), axis=1)
    position = jnp.where(live, owners * CAP + rank, -1)
    tile = jnp.where(live, listed[:, 1] * 4 + listed[:, 0] % 4, 0)
    fills = position[None, :] == order[:, None]
    slots = jnp.sum(jnp.where(fills, tile[None, :] + 1, 0), axis=1) - 1

    z_of = (z + sign * np.array([dz for dz, _ in COLS])) % 8
    col_of = z_of * 2 + (x_hi ^ np.array([dxh for _, dxh in COLS]))
    found = []
    for h in range(2):
        turn = np.array([t for t in range(4) for _ in range(2)])
        ids = (x_lo ^ np.array([dx for _ in range(4) for dx in range(2)])) * 4 + (y - (1 - 2 * h) * turn) % 4
        hit = ids[None, :] == z_of[:, None]
        found.append(jnp.sum(jnp.where(hit, np.arange(8)[None, :], 0), axis=1))
    dest = (x_lo ^ np.array([dx for dx, _ in DESTS])) * 4 + (y + np.array([dy for _, dy in DESTS])) % 4
    table = jnp.concatenate([
        v.astype(jnp.int32)
        for v in (col_of, *found, x_hi[None], core[None], dest * 2 + core, dest * 2 + 1 - core, slots)])
    xt = inputs.T

    half = lax.dynamic_slice_in_dim(weight, core * 256, 256, 0)
    far_half, r1, f1, table, xt = together(
        (to_row(half, 1, 0), back(grad_out), ahead(grad_out), table, xt))

    pair = jnp.concatenate([half, far_half], axis=0)
    total = dense(None, table, xt, [grad_out, f1, r1], 0)
    s0, w1, o0, r2, f2, total = together(
        (to_core(pair), around(pair), across(grad_out), back(r1), ahead(f1), total))

    total = dense(total, table, xt, [f2, r2, o0], 3)
    s1, w2, of2, r3, f3, total = together(
        (to_core(w1), around(w1), across(f2), back(r2), ahead(f2), total))

    total = dense(total, table, xt, [f3, r3, of2], 6)
    w3, or2, or1, of1, f4, total = together(
        (around(w2), across(r2), back(o0), ahead(o0), ahead(f3), total))

    total = dense(total, table, xt, [f4, of1, or1, or2], 9)
    s3, s2, of4, or3, of3, total = together(
        (to_core(w3), to_core(w2), across(f4), back(or2), ahead(of2), total))

    total = dense(total, table, xt, [of3, or3, of4], LAST)
    parts = [pair, w1, w2, w3, s0, s1, s2, s3]
    cols = [grad_out, f1, r1, f2, r2, o0, f3, r3, of2, f4, of1, or1, or2, of3, or3, of4]

    other_late = to_core(pick(table, EARLY, 8, total))
    other_early = to_core(pick(table, 0, EARLY, total))
    early = code(table, 0, EARLY, total, other_early, 0)
    late = code(table, EARLY, 8, total, other_late, 1)
    coded = list(early) + list(late[:-1])
    arrived = [to_row(v, dx, dy) for v, (dx, dy) in zip(coded, DESTS)]
    own, grad_table = together((late[-1], table))
    grad_in = grad_sum(grad_table, range(16), cols, parts, None, True)
    *arrived, grad_in = together((*arrived, grad_in))
    pushed = total_sum(own, arrived)
    return grad_in, pushed.reshape(1, CAP, BLK, BLK)


def solution(mesh):
    in_specs = (
        P(("row", "srv"), "col"),
        P(("row", "srv"), "col"),
        P("col", "row"),
        P("col", None, None),
        P("col", None),
    )
    out_specs = (P(("row", "srv"), "col"), P(("row", "srv"), "col", None, None))
    return jax.shard_map(body, mesh=mesh, in_specs=in_specs, out_specs=out_specs, check_vma=False)
```

time: 383 us -> 145 us (0.38)
  waiting for transfers between devices: 233 us -> 69.6 us
  local copies, waits for them, and re-layouts: 74.4 us -> 2.43 us
  starting transfers between devices: 0.12 us -> 45.6 us
  other arithmetic: 31.9 us -> 5.79 us
  matrix products: 25.4 us -> 0 us
  Pallas kernels: 0 us -> 20.5 us
  between operations: 14.4 us -> 0.8 us
    all_gather x2 -> x0, waiting for transfers between devices: 134 us -> none  [the longest x1 134 us: body(): full_grad = lax.all_gather(grad_out, 'col', axis=1, tiled=True)]
    reduce_scatter x1 -> x0, waiting for transfers between devices: 97.9 us -> none  [body(): lax.psum_scatter(holder, ('row', 'srv'), scatter_dimension=0, tiled=True)]
    ppermute x0 -> x32, waiting for transfers between devices: none -> 69.6 us  [the longest x4 21.8 us: across(): return lax.ppermute(v, 'col', X_SWAP)]
    gather x20 -> x0, local copies, waits for them, and re-layouts: 49.6 us -> none  [the longest x10 42.1 us: tile_group(): right = jnp.take(grad_tiles, col_sel, axis=1)]
    ppermute x0 -> x32, starting transfers between devices: none -> 45.6 us  [the longest x6 18.6 us: ahead(): return lax.ppermute(v, ('col', 'srv'), z_shift(1))]
    scatter-add x1 -> x0, other arithmetic: 27.2 us -> none  [body(): jnp.zeros((owner_count * CAP, BLK, BLK), jnp.float32).at[position]]
    dot_general x11 -> x0, matrix products: 25.4 us -> none  [the longest x10 14.3 us: tile_group(): jnp.einsum('bmi,bmj->mij', left, right, preferred_element_type=jnp.float32)]
    pallas_call x0 -> x11, Pallas kernels: none -> 20.5 us  [the longest x5 7.92 us: dense(): pl.pallas_call(functools.partial(dense_kernel, count, place, first), out_...]
  transfers between devices with their start and end apart: 3 -> 32, of which waited for: 2 -> 15; matrix products, arithmetic and copies ran while one was open for 34% -> 4% of each run, Pallas kernels for 0% -> 11%
where the time goes in v2:
time: 145 us
  waiting for transfers between devices  69.6 us (48%)
  starting transfers between devices  45.6 us (31%)
  Pallas kernels  20.5 us (14%)
  other arithmetic  5.79 us (4%)
  local copies, waits for them, and re-layouts  2.43 us (2%)
    ppermute x4, waiting for transfers between devices, across(): return lax.ppermute(v, 'col', X_SWAP)  21.8 us
    ppermute x8, waiting for transfers between devices, to_row(): return lax.ppermute(v, 'row', row_shift(dx, dy))  21.2 us
    ppermute x6, starting transfers between devices, ahead(): return lax.ppermute(v, ('col', 'srv'), z_shift(1))  18.6 us
    ppermute x6, waiting for transfers between devices, ahead(): return lax.ppermute(v, ('col', 'srv'), z_shift(1))  16.4 us
    ppermute x8, starting transfers between devices, to_row(): return lax.ppermute(v, 'row', row_shift(dx, dy))  9.69 us
    pallas_call x5, Pallas kernels, dense(): pl.pallas_call(functools.partial(dense_kernel, count, place, first), out_...  7.92 us
    pallas_call x1, Pallas kernels, grad_sum(): pl.pallas_call(functools.partial(grad_kernel, tuple(ids), has_sum, last),...  6.41 us
    ppermute x3, starting transfers between devices, around(): return lax.ppermute(v, ('row', 'srv'), y_shift(1))  6.23 us
  transfers between devices with their start and end apart: 32, of which 15 were waited for; matrix products, arithmetic and copies ran while one was open for 4% of the time, Pallas kernels for 11%

profile of v2, /device:TPU:1, one launch (start us, length us, event | category | flops | bytes accessed | tf_op | source)
XLA Modules:
  0.0 144.7 jit_solution(18196877995051163152)
XLA Ops:
  0.6 6.5 %collective-permute-start.2 = (bf16[512,512]{1,0:T(8,128)(2,1)}, bf16[512,512]{1,0:T(8,128)(2,1)S(1)}, u32[]{:S(2)}, u32[]{:S(2)}) collective-permute-start(bf16[512,512]{1,0:T(8,128)(2,1)} %refs_0_.3), channel_id=1, source_target_pairs={{0,4},{1,29},{2,6},{3,31},{4,8},{5,1},{6,10},{7,3},{8,12},{9,5},{1... | collective-permute-start | bytes 1572872 | tf_op jit(solution)/shard_map/ppermute | solution.py:236
  14.5 5.2 %collective-permute-done = bf16[256,1024]{1,0:T(8,128)(2,1)} collective-permute-done((bf16[256,1024]{1,0:T(8,128)(2,1)S(1)}, bf16[256,1024]{1,0:T(8,128)(2,1)}, u32[]{:S(2)}, u32[]{:S(2)}) %collective-permute-start) | collective-permute-done | bytes 524320 | tf_op jit(solution)/shard_map/ppermute | solution.py:248
  21.5 2.8 %collective-permute-start.4 = (bf16[512,1024]{1,0:T(8,128)(2,1)S(1)}, bf16[512,1024]{1,0:T(8,128)(2,1)S(1)}, u32[]{:S(2)}, u32[]{:S(2)}) collective-permute-start(bf16[512,1024]{1,0:T(8,128)(2,1)S(1)} %pad_maximum_fusion.refs_16_), channel_id=1, source_target_pairs={{0,32},{1,97},{32,64},{33,1},{64,96},{65,33},{96,0},{97,65},{128,1... | collective-permute-start | bytes 3145736 | tf_op jit(solution)/shard_map/ppermute | solution.py:245
  24.5 2.7 %collective-permute-start.5 = (bf16[512,512]{1,0:T(8,128)(2,1)}, bf16[512,512]{1,0:T(8,128)(2,1)S(1)}, u32[]{:S(2)}, u32[]{:S(2)}) collective-permute-start(bf16[512,512]{1,0:T(8,128)(2,1)} %refs_0_.3), channel_id=1, source_target_pairs={{0,2},{2,0},{4,6},{6,4},{8,10},{10,8},{12,14},{14,12},{16,18},{18,... | collective-permute-start | bytes 1572872 | tf_op jit(solution)/shard_map/ppermute | solution.py:242
  27.2 3.0 %collective-permute-start.7 = (bf16[512,512]{1,0:T(8,128)(2,1)S(1)}, bf16[512,512]{1,0:T(8,128)(2,1)S(1)}, u32[]{:S(2)}, u32[]{:S(2)}) collective-permute-start(bf16[512,512]{1,0:T(8,128)(2,1)S(1)} %collective-permute-done.2.refs_1_), channel_id=1, source_target_pairs={{0,4},{1,29},{2,6},{3,31},{4,8},{5,1},{6,10},{7,3},{8,12},{9,5},{1... | collective-permute-start | bytes 1572872 | tf_op jit(solution)/shard_map/ppermute | solution.py:236
  32.8 6.5 %collective-permute-done.5.refs_2_.refs_5_ = bf16[512,512]{1,0:T(8,128)(2,1)S(1)} collective-permute-done((bf16[512,512]{1,0:T(8,128)(2,1)}, bf16[512,512]{1,0:T(8,128)(2,1)S(1)}, u32[]{:S(2)}, u32[]{:S(2)}) %collective-permute-start.5) | collective-permute-done | bytes 524320 | tf_op jit(solution)/shard_map/ppermute | solution.py:242
  44.4 2.8 %collective-permute-start.12 = (bf16[512,512]{1,0:T(8,128)(2,1)S(1)}, bf16[512,512]{1,0:T(8,128)(2,1)S(1)}, u32[]{:S(2)}, u32[]{:S(2)}) collective-permute-start(bf16[512,512]{1,0:T(8,128)(2,1)S(1)} %collective-permute-done.7.refs_0_.refs_3_), channel_id=1, source_target_pairs={{0,4},{1,29},{2,6},{3,31},{4,8},{5,1},{6,10},{7,3},{8,12},{9,5},{1... | collective-permute-start | bytes 1572872 | tf_op jit(solution)/shard_map/ppermute | solution.py:236
  49.2 8.1 %collective-permute-done.12.refs_0_.refs_6_ = bf16[512,512]{1,0:T(8,128)(2,1)S(1)} collective-permute-done((bf16[512,512]{1,0:T(8,128)(2,1)S(1)}, bf16[512,512]{1,0:T(8,128)(2,1)S(1)}, u32[]{:S(2)}, u32[]{:S(2)}) %collective-permute-start.12) | collective-permute-done | bytes 524320 | tf_op jit(solution)/shard_map/ppermute | solution.py:236
  57.3 2.7 %collective-permute-done.10.refs_2_.refs_8_ = bf16[512,512]{1,0:T(8,128)(2,1)S(1)} collective-permute-done((bf16[512,512]{1,0:T(8,128)(2,1)S(1)}, bf16[512,512]{1,0:T(8,128)(2,1)S(1)}, u32[]{:S(2)}, u32[]{:S(2)}) %collective-permute-start.10) | collective-permute-done | bytes 524320 | tf_op jit(solution)/shard_map/ppermute | solution.py:242
  62.1 2.4 %collective-permute-start.16 = (bf16[512,512]{1,0:T(8,128)(2,1)S(1)}, bf16[512,512]{1,0:T(8,128)(2,1)S(1)}, u32[]{:S(2)}, u32[]{:S(2)}) collective-permute-start(bf16[512,512]{1,0:T(8,128)(2,1)S(1)} %collective-permute-done.5.refs_2_.refs_5_), channel_id=1, source_target_pairs={{0,4},{1,29},{2,6},{3,31},{4,8},{5,1},{6,10},{7,3},{8,12},{9,5},{1... | collective-permute-start | bytes 1572872 | tf_op jit(solution)/shard_map/ppermute | solution.py:236
  64.5 2.7 %collective-permute-start.17 = (bf16[512,512]{1,0:T(8,128)(2,1)S(1)}, bf16[512,512]{1,0:T(8,128)(2,1)S(1)}, u32[]{:S(2)}, u32[]{:S(2)}) collective-permute-start(bf16[512,512]{1,0:T(8,128)(2,1)S(1)} %collective-permute-done.12.refs_0_.refs_6_), channel_id=1, source_target_pairs={{0,4},{1,29},{2,6},{3,31},{4,8},{5,1},{6,10},{7,3},{8,12},{9,5},{1... | collective-permute-start | bytes 1572872 | tf_op jit(solution)/shard_map/ppermute | solution.py:236
  68.7 7.4 %collective-permute-done.14.refs_3_.refs_12_ = bf16[512,512]{1,0:T(8,128)(2,1)S(1)} collective-permute-done((bf16[512,512]{1,0:T(8,128)(2,1)S(1)}, bf16[512,512]{1,0:T(8,128)(2,1)S(1)}, u32[]{:S(2)}, u32[]{:S(2)}) %collective-permute-start.14) | collective-permute-done | bytes 524320 | tf_op jit(solution)/shard_map/ppermute | solution.py:242
  76.2 3.6 %collective-permute-done.15.refs_2_.refs_11_ = bf16[512,512]{1,0:T(8,128)(2,1)S(1)} collective-permute-done((bf16[512,512]{1,0:T(8,128)(2,1)S(1)}, bf16[512,512]{1,0:T(8,128)(2,1)S(1)}, u32[]{:S(2)}, u32[]{:S(2)}) %collective-permute-start.15) | collective-permute-done | bytes 524320 | tf_op jit(solution)/shard_map/ppermute | solution.py:239
  85.0 2.2 %collective-permute-start.20 = (bf16[512,512]{1,0:T(8,128)(2,1)S(1)}, bf16[512,512]{1,0:T(8,128)(2,1)S(1)}, u32[]{:S(2)}, u32[]{:S(2)}) collective-permute-start(bf16[512,512]{1,0:T(8,128)(2,1)S(1)} %collective-permute-done.17.refs_0_.refs_9_), channel_id=1, source_target_pairs={{0,2},{2,0},{4,6},{6,4},{8,10},{10,8},{12,14},{14,12},{16,18},{18,... | collective-permute-start | bytes 1572872 | tf_op jit(solution)/shard_map/ppermute | solution.py:242
  89.5 4.8 %collective-permute-done.22.refs_0_.refs_13_ = bf16[512,512]{1,0:T(8,128)(2,1)S(1)} collective-permute-done((bf16[512,512]{1,0:T(8,128)(2,1)S(1)}, bf16[512,512]{1,0:T(8,128)(2,1)S(1)}, u32[]{:S(2)}, u32[]{:S(2)}) %collective-permute-start.22) | collective-permute-done | bytes 524320 | tf_op jit(solution)/shard_map/ppermute | solution.py:236
  94.4 5.1 %collective-permute-done.20.refs_2_.refs_15_ = bf16[512,512]{1,0:T(8,128)(2,1)S(1)} collective-permute-done((bf16[512,512]{1,0:T(8,128)(2,1)S(1)}, bf16[512,512]{1,0:T(8,128)(2,1)S(1)}, u32[]{:S(2)}, u32[]{:S(2)}) %collective-permute-start.20) | collective-permute-done | bytes 524320 | tf_op jit(solution)/shard_map/ppermute | solution.py:242
  103.2 5.9 %collective-permute-done.23.other = f32[16,128,128]{2,1,0:T(8,128)S(1)} collective-permute-done((f32[16,128,128]{2,1,0:T(8,128)S(1)}, f32[16,128,128]{2,1,0:T(8,128)S(1)}, u32[]{:S(2)}, u32[]{:S(2)}) %collective-permute-start.23) | collective-permute-done | bytes 1048608 | tf_op jit(solution)/shard_map/ppermute | solution.py:251
  112.9 3.3 %collective-permute-start.27 = (bf16[1040,128]{1,0:T(8,128)(2,1)S(1)}, bf16[1040,128]{1,0:T(8,128)(2,1)S(1)}, u32[]{:S(2)}, u32[]{:S(2)}) collective-permute-start(bf16[1040,128]{1,0:T(8,128)(2,1)S(1)} %get-tuple-element.76), channel_id=1, source_target_pairs={{0,224},{32,128},{64,160},{96,192},{128,96},{160,0},{192,32},{224,... | collective-permute-start | bytes 798728 | tf_op jit(solution)/shard_map/ppermute | solution.py:248
  116.9 2.5 %collective-permute-start.29 = (bf16[1040,128]{1,0:T(8,128)(2,1)S(1)}, bf16[1040,128]{1,0:T(8,128)(2,1)S(1)}, u32[]{:S(2)}, u32[]{:S(2)}) collective-permute-start(bf16[1040,128]{1,0:T(8,128)(2,1)S(1)} %get-tuple-element.78), channel_id=1, source_target_pairs={{0,64},{32,96},{64,0},{96,32},{128,192},{160,224},{192,128},{224,1... | collective-permute-start | bytes 798728 | tf_op jit(solution)/shard_map/ppermute | solution.py:248
  119.4 5.3 %collective-permute-done.25.refs_1_ = bf16[1040,128]{1,0:T(8,128)(2,1)S(1)} collective-permute-done((bf16[1040,128]{1,0:T(8,128)(2,1)S(1)}, bf16[1040,128]{1,0:T(8,128)(2,1)S(1)}, u32[]{:S(2)}, u32[]{:S(2)}) %collective-permute-start.25) | collective-permute-done | bytes 266272 | tf_op jit(solution)/shard_map/ppermute | solution.py:248
  125.2 6.4 %shard_map.167 = bf16[512,512]{1,0:T(8,128)(2,1)} custom-call(s32[194]{0:T(256)S(1)} %concatenate.6.table, bf16[512,512]{1,0:T(8,128)(2,1)S(1)} %copy-done.2, bf16[512,512]{1,0:T(8,128)(2,1)S(1)} %collective-permute-done.2.refs_1_, bf16[512,512]{1,0:T(8,128)(2,1)S(1)} %collective-permute-done.1.refs_2_, ...), custom_call_target="tpu_custom_call" | custom-call | flops 4294967296 | bytes 25165824 | tf_op jit(solution)/shard_map/pallas_call | solution.py:214
  131.6 5.6 %collective-permute-done.28.refs_3_ = bf16[1040,128]{1,0:T(8,128)(2,1)S(1)} collective-permute-done((bf16[1040,128]{1,0:T(8,128)(2,1)S(1)}, bf16[1040,128]{1,0:T(8,128)(2,1)S(1)}, u32[]{:S(2)}, u32[]{:S(2)}) %collective-permute-start.28) | collective-permute-done | bytes 266272 | tf_op jit(solution)/shard_map/ppermute | solution.py:248
  137.2 5.1 %collective-permute-done.30.refs_5_ = bf16[1040,128]{1,0:T(8,128)(2,1)S(1)} collective-permute-done((bf16[1040,128]{1,0:T(8,128)(2,1)S(1)}, bf16[1040,128]{1,0:T(8,128)(2,1)S(1)}, u32[]{:S(2)}, u32[]{:S(2)}) %collective-permute-start.30) | collective-permute-done | bytes 266272 | tf_op jit(solution)/shard_map/ppermute | solution.py:248
  142.3 2.3 %shard_map.168 = f32[8,128,128]{2,1,0:T(8,128)} custom-call(f32[8,128,128]{2,1,0:T(8,128)S(1)} %get-tuple-element.88.own, bf16[1040,128]{1,0:T(8,128)(2,1)S(1)} %collective-permute-done.24.refs_0_, bf16[1040,128]{1,0:T(8,128)(2,1)S(1)} %collective-permute-done.25.refs_1_, bf16[1040,128]{1,0:T(8,128)(2,1)S(1)} %collective-permute-done.27.refs_2_, ...), custom_call_target="tpu_custom_call" | custom-call | flops 8388608 | bytes 2097152 | tf_op jit(solution)/shard_map/pallas_call | solution.py:170
  (71 shorter events, 38.8 us)
Async XLA Ops:
  0.6 19.1 %collective-permute-start.2 = (bf16[512,512]{1,0:T(8,128)(2,1)}, bf16[512,512]{1,0:T(8,128)(2,1)S(1)}, u32[]{:S(2)}, u32[]{:S(2)}) collective-permute-start(bf16[512,512]{1,0:T(8,128)(2,1)} %refs_0_.3), channel_id=1, source_target_pairs={{0,4},{1,29},{2,6},{3,31},{4,8},{5,1},{6,10},{7,3},{8,12},{9,5},{1... | collective-permute-start | bytes 1572872 | tf_op jit(solution)/shard_map/ppermute | solution.py:236
  7.1 13.3 %collective-permute-start.1 = (bf16[512,512]{1,0:T(8,128)(2,1)}, bf16[512,512]{1,0:T(8,128)(2,1)S(1)}, u32[]{:S(2)}, u32[]{:S(2)}) collective-permute-start(bf16[512,512]{1,0:T(8,128)(2,1)} %refs_0_.3), channel_id=1, source_target_pairs={{0,28},{1,5},{2,30},{3,7},{4,0},{5,9},{6,2},{7,11},{8,4},{9,13},{1... | collective-permute-start | bytes 1572872 | tf_op jit(solution)/shard_map/ppermute | solution.py:239
  21.5 19.2 %collective-permute-start.4 = (bf16[512,1024]{1,0:T(8,128)(2,1)S(1)}, bf16[512,1024]{1,0:T(8,128)(2,1)S(1)}, u32[]{:S(2)}, u32[]{:S(2)}) collective-permute-start(bf16[512,1024]{1,0:T(8,128)(2,1)S(1)} %pad_maximum_fusion.refs_16_), channel_id=1, source_target_pairs={{0,32},{1,97},{32,64},{33,1},{64,96},{65,33},{96,0},{97,65},{128,1... | collective-permute-start | bytes 3145736 | tf_op jit(solution)/shard_map/ppermute | solution.py:245
  24.3 16.4 %collective-permute-start.3 = (bf16[512,1024]{1,0:T(8,128)(2,1)S(1)}, bf16[512,1024]{1,0:T(8,128)(2,1)S(1)}, u32[]{:S(2)}, u32[]{:S(2)}) collective-permute-start(bf16[512,1024]{1,0:T(8,128)(2,1)S(1)} %pad_maximum_fusion.refs_16_), channel_id=1, source_target_pairs={{0,1},{1,0},{2,3},{3,2},{4,5},{5,4},{6,7},{7,6},{8,9},{9,8},{10,11... | collective-permute-start | bytes 3145736 | tf_op jit(solution)/shard_map/ppermute | solution.py:251
  24.5 14.9 %collective-permute-start.5 = (bf16[512,512]{1,0:T(8,128)(2,1)}, bf16[512,512]{1,0:T(8,128)(2,1)S(1)}, u32[]{:S(2)}, u32[]{:S(2)}) collective-permute-start(bf16[512,512]{1,0:T(8,128)(2,1)} %refs_0_.3), channel_id=1, source_target_pairs={{0,2},{2,0},{4,6},{6,4},{8,10},{10,8},{12,14},{14,12},{16,18},{18,... | collective-permute-start | bytes 1572872 | tf_op jit(solution)/shard_map/ppermute | solution.py:242
  27.2 13.5 %collective-permute-start.7 = (bf16[512,512]{1,0:T(8,128)(2,1)S(1)}, bf16[512,512]{1,0:T(8,128)(2,1)S(1)}, u32[]{:S(2)}, u32[]{:S(2)}) collective-permute-start(bf16[512,512]{1,0:T(8,128)(2,1)S(1)} %collective-permute-done.2.refs_1_), channel_id=1, source_target_pairs={{0,4},{1,29},{2,6},{3,31},{4,8},{5,1},{6,10},{7,3},{8,12},{9,5},{1... | collective-permute-start | bytes 1572872 | tf_op jit(solution)/shard_map/ppermute | solution.py:236
  40.7 19.3 %collective-permute-start.9 = (bf16[512,1024]{1,0:T(8,128)(2,1)S(1)}, bf16[512,1024]{1,0:T(8,128)(2,1)S(1)}, u32[]{:S(2)}, u32[]{:S(2)}) collective-permute-start(bf16[512,1024]{1,0:T(8,128)(2,1)S(1)} %collective-permute-done.4.refs_17_), channel_id=1, source_target_pairs={{0,32},{1,97},{32,64},{33,1},{64,96},{65,33},{96,0},{97,65},{128,1... | collective-permute-start | bytes 3145736 | tf_op jit(solution)/shard_map/ppermute | solution.py:245
  42.3 17.7 %collective-permute-start.8 = (bf16[512,1024]{1,0:T(8,128)(2,1)S(1)}, bf16[512,1024]{1,0:T(8,128)(2,1)S(1)}, u32[]{:S(2)}, u32[]{:S(2)}) collective-permute-start(bf16[512,1024]{1,0:T(8,128)(2,1)S(1)} %collective-permute-done.4.refs_17_), channel_id=1, source_target_pairs={{0,1},{1,0},{2,3},{3,2},{4,5},{5,4},{6,7},{7,6},{8,9},{9,8},{10,11... | collective-permute-start | bytes 3145736 | tf_op jit(solution)/shard_map/ppermute | solution.py:251
  44.4 12.9 %collective-permute-start.12 = (bf16[512,512]{1,0:T(8,128)(2,1)S(1)}, bf16[512,512]{1,0:T(8,128)(2,1)S(1)}, u32[]{:S(2)}, u32[]{:S(2)}) collective-permute-start(bf16[512,512]{1,0:T(8,128)(2,1)S(1)} %collective-permute-done.7.refs_0_.refs_3_), channel_id=1, source_target_pairs={{0,4},{1,29},{2,6},{3,31},{4,8},{5,1},{6,10},{7,3},{8,12},{9,5},{1... | collective-permute-start | bytes 1572872 | tf_op jit(solution)/shard_map/ppermute | solution.py:236
  47.1 12.9 %collective-permute-start.10 = (bf16[512,512]{1,0:T(8,128)(2,1)S(1)}, bf16[512,512]{1,0:T(8,128)(2,1)S(1)}, u32[]{:S(2)}, u32[]{:S(2)}) collective-permute-start(bf16[512,512]{1,0:T(8,128)(2,1)S(1)} %collective-permute-done.7.refs_0_.refs_3_), channel_id=1, source_target_pairs={{0,2},{2,0},{4,6},{6,4},{8,10},{10,8},{12,14},{14,12},{16,18},{18,... | collective-permute-start | bytes 1572872 | tf_op jit(solution)/shard_map/ppermute | solution.py:242
  60.0 21.9 %collective-permute-start.13 = (bf16[512,1024]{1,0:T(8,128)(2,1)S(1)}, bf16[512,1024]{1,0:T(8,128)(2,1)S(1)}, u32[]{:S(2)}, u32[]{:S(2)}) collective-permute-start(bf16[512,1024]{1,0:T(8,128)(2,1)S(1)} %collective-permute-done.9.refs_18_), channel_id=1, source_target_pairs={{0,32},{1,97},{32,64},{33,1},{64,96},{65,33},{96,0},{97,65},{128,1... | collective-permute-start | bytes 3145736 | tf_op jit(solution)/shard_map/ppermute | solution.py:245
  61.8 14.4 %collective-permute-start.14 = (bf16[512,512]{1,0:T(8,128)(2,1)S(1)}, bf16[512,512]{1,0:T(8,128)(2,1)S(1)}, u32[]{:S(2)}, u32[]{:S(2)}) collective-permute-start(bf16[512,512]{1,0:T(8,128)(2,1)S(1)} %collective-permute-done.6.refs_1_.refs_4_), channel_id=1, source_target_pairs={{0,2},{2,0},{4,6},{6,4},{8,10},{10,8},{12,14},{14,12},{16,18},{18,... | collective-permute-start | bytes 1572872 | tf_op jit(solution)/shard_map/ppermute | solution.py:242
  62.1 14.1 %collective-permute-start.16 = (bf16[512,512]{1,0:T(8,128)(2,1)S(1)}, bf16[512,512]{1,0:T(8,128)(2,1)S(1)}, u32[]{:S(2)}, u32[]{:S(2)}) collective-permute-start(bf16[512,512]{1,0:T(8,128)(2,1)S(1)} %collective-permute-done.5.refs_2_.refs_5_), channel_id=1, source_target_pairs={{0,4},{1,29},{2,6},{3,31},{4,8},{5,1},{6,10},{7,3},{8,12},{9,5},{1... | collective-permute-start | bytes 1572872 | tf_op jit(solution)/shard_map/ppermute | solution.py:236
  64.5 15.2 %collective-permute-start.15 = (bf16[512,512]{1,0:T(8,128)(2,1)S(1)}, bf16[512,512]{1,0:T(8,128)(2,1)S(1)}, u32[]{:S(2)}, u32[]{:S(2)}) collective-permute-start(bf16[512,512]{1,0:T(8,128)(2,1)S(1)} %collective-permute-done.5.refs_2_.refs_5_), channel_id=1, source_target_pairs={{0,28},{1,5},{2,30},{3,7},{4,0},{5,9},{6,2},{7,11},{8,4},{9,13},{1... | collective-permute-start | bytes 1572872 | tf_op jit(solution)/shard_map/ppermute | solution.py:239
  64.5 17.4 %collective-permute-start.17 = (bf16[512,512]{1,0:T(8,128)(2,1)S(1)}, bf16[512,512]{1,0:T(8,128)(2,1)S(1)}, u32[]{:S(2)}, u32[]{:S(2)}) collective-permute-start(bf16[512,512]{1,0:T(8,128)(2,1)S(1)} %collective-permute-done.12.refs_0_.refs_6_), channel_id=1, source_target_pairs={{0,4},{1,29},{2,6},{3,31},{4,8},{5,1},{6,10},{7,3},{8,12},{9,5},{1... | collective-permute-start | bytes 1572872 | tf_op jit(solution)/shard_map/ppermute | solution.py:236
  76.2 18.2 %collective-permute-start.19 = (bf16[512,1024]{1,0:T(8,128)(2,1)S(1)}, bf16[512,1024]{1,0:T(8,128)(2,1)S(1)}, u32[]{:S(2)}, u32[]{:S(2)}) collective-permute-start(bf16[512,1024]{1,0:T(8,128)(2,1)S(1)} %collective-permute-done.9.refs_18_), channel_id=1, source_target_pairs={{0,1},{1,0},{2,3},{3,2},{4,5},{5,4},{6,7},{7,6},{8,9},{9,8},{10,11... | collective-permute-start | bytes 3145736 | tf_op jit(solution)/shard_map/ppermute | solution.py:251
  81.9 17.6 %collective-permute-start.18 = (bf16[512,1024]{1,0:T(8,128)(2,1)S(1)}, bf16[512,1024]{1,0:T(8,128)(2,1)S(1)}, u32[]{:S(2)}, u32[]{:S(2)}) collective-permute-start(bf16[512,1024]{1,0:T(8,128)(2,1)S(1)} %collective-permute-done.13.refs_19_), channel_id=1, source_target_pairs={{0,1},{1,0},{2,3},{3,2},{4,5},{5,4},{6,7},{7,6},{8,9},{9,8},{10,11... | collective-permute-start | bytes 3145736 | tf_op jit(solution)/shard_map/ppermute | solution.py:251
  85.0 14.5 %collective-permute-start.20 = (bf16[512,512]{1,0:T(8,128)(2,1)S(1)}, bf16[512,512]{1,0:T(8,128)(2,1)S(1)}, u32[]{:S(2)}, u32[]{:S(2)}) collective-permute-start(bf16[512,512]{1,0:T(8,128)(2,1)S(1)} %collective-permute-done.17.refs_0_.refs_9_), channel_id=1, source_target_pairs={{0,2},{2,0},{4,6},{6,4},{8,10},{10,8},{12,14},{14,12},{16,18},{18,... | collective-permute-start | bytes 1572872 | tf_op jit(solution)/shard_map/ppermute | solution.py:242
  111.0 13.6 %collective-permute-start.25 = (bf16[1040,128]{1,0:T(8,128)(2,1)S(1)}, bf16[1040,128]{1,0:T(8,128)(2,1)S(1)}, u32[]{:S(2)}, u32[]{:S(2)}) collective-permute-start(bf16[1040,128]{1,0:T(8,128)(2,1)S(1)} %get-tuple-element.75), channel_id=1, source_target_pairs={{0,160},{32,192},{64,224},{96,128},{128,32},{160,64},{192,96},{224... | collective-permute-start | bytes 798728 | tf_op jit(solution)/shard_map/ppermute | solution.py:248
  112.9 18.7 %collective-permute-start.27 = (bf16[1040,128]{1,0:T(8,128)(2,1)S(1)}, bf16[1040,128]{1,0:T(8,128)(2,1)S(1)}, u32[]{:S(2)}, u32[]{:S(2)}) collective-permute-start(bf16[1040,128]{1,0:T(8,128)(2,1)S(1)} %get-tuple-element.76), channel_id=1, source_target_pairs={{0,224},{32,128},{64,160},{96,192},{128,96},{160,0},{192,32},{224,... | collective-permute-start | bytes 798728 | tf_op jit(solution)/shard_map/ppermute | solution.py:248
  116.2 21.0 %collective-permute-start.28 = (bf16[1040,128]{1,0:T(8,128)(2,1)S(1)}, bf16[1040,128]{1,0:T(8,128)(2,1)S(1)}, u32[]{:S(2)}, u32[]{:S(2)}) collective-permute-start(bf16[1040,128]{1,0:T(8,128)(2,1)S(1)} %get-tuple-element.77), channel_id=1, source_target_pairs={{0,192},{32,224},{64,128},{96,160},{128,64},{160,96},{192,0},{224,... | collective-permute-start | bytes 798728 | tf_op jit(solution)/shard_map/ppermute | solution.py:248
  116.9 20.2 %collective-permute-start.29 = (bf16[1040,128]{1,0:T(8,128)(2,1)S(1)}, bf16[1040,128]{1,0:T(8,128)(2,1)S(1)}, u32[]{:S(2)}, u32[]{:S(2)}) collective-permute-start(bf16[1040,128]{1,0:T(8,128)(2,1)S(1)} %get-tuple-element.78), channel_id=1, source_target_pairs={{0,64},{32,96},{64,0},{96,32},{128,192},{160,224},{192,128},{224,1... | collective-permute-start | bytes 798728 | tf_op jit(solution)/shard_map/ppermute | solution.py:248
  119.4 22.9 %collective-permute-start.30 = (bf16[1040,128]{1,0:T(8,128)(2,1)S(1)}, bf16[1040,128]{1,0:T(8,128)(2,1)S(1)}, u32[]{:S(2)}, u32[]{:S(2)}) collective-permute-start(bf16[1040,128]{1,0:T(8,128)(2,1)S(1)} %get-tuple-element.79), channel_id=1, source_target_pairs={{0,32},{32,64},{64,96},{96,0},{128,160},{160,192},{192,224},{224,1... | collective-permute-start | bytes 798728 | tf_op jit(solution)/shard_map/ppermute | solution.py:248
  124.7 17.7 %collective-permute-start.31 = (bf16[1040,128]{1,0:T(8,128)(2,1)S(1)}, bf16[1040,128]{1,0:T(8,128)(2,1)S(1)}, u32[]{:S(2)}, u32[]{:S(2)}) collective-permute-start(bf16[1040,128]{1,0:T(8,128)(2,1)S(1)} %get-tuple-element.80), channel_id=1, source_target_pairs={{0,96},{32,0},{64,32},{96,64},{128,224},{160,128},{192,160},{224,1... | collective-permute-start | bytes 798728 | tf_op jit(solution)/shard_map/ppermute | solution.py:248
  (11 other events, 115.4 us)

commit v3 on v2

--- a/solution.py
+++ b/solution.py
@@ -19,7 +19,7 @@
 COLS = ((0, 0), (-1, 0), (1, 0), (-2, 0), (2, 0), (0, 1), (-3, 0), (3, 0), (-2, 1),
         (-4, 0), (-1, 1), (1, 1), (2, 1), (-3, 1), (3, 1), (-4, 1))
 LAST = 13
-DESTS = ((1, 0), (1, 1), (1, 3), (1, 2), (0, 2), (0, 1), (0, 3), (0, 0))
+DESTS = ((1, 2), (1, 1), (1, 3), (1, 0), (0, 2), (0, 1), (0, 3), (0, 0))
 EARLY = 2
 DENSE_MIB = PICK_MIB = CODE_MIB = GRAD_MIB = 20
 COL_AT, ROW_AT, SIDE_AT, MINE_AT, THEIRS_AT, SLOT_AT = 0, 16, 48, 50, 58, 66
@@ -150,14 +150,14 @@
     )(table, total, other)
 
 
-def sum_kernel(own, *refs):
+def sum_kernel(before, *refs):
     arrived, out = refs[:-1], refs[-1]
     scales = []
     for ref in arrived:
         level = ref[CAP * BLK:CAP * BLK + TAIL, :].astype(F32)[0:1, :]
         scales.append(level - TOP)
     for t in range(CAP):
-        acc = own[t]
+        acc = before[t]
         for ref, scale in zip(arrived, scales):
             y = ref[t * BLK:(t + 1) * BLK, :].astype(F32)
             size = jnp.exp2(jnp.log2(jnp.maximum(jnp.abs(y), 1e-37)) * (1.0 / POWER) + scale)
@@ -166,29 +166,31 @@
         out[t] = acc
 
 
-def total_sum(own, arrived):
+def add_coded(before, arrived):
+    count = len(arrived)
     return pl.pallas_call(
         sum_kernel,
         out_shape=jax.ShapeDtypeStruct((CAP, BLK, BLK), F32),
-        in_specs=[vmem_spec()] * (1 + len(arrived)),
-        out_specs=vmem_spec(),
-        compiler_params=params(24),
-        cost_estimate=pl.CostEstimate(
-            flops=8 * CAP * BLK * BLK * 8, bytes_accessed=8 * CAP * BLK * BLK * 2,
+        in_specs=[vmem_spec()] * (1 + count),
+        out_specs=vmem_spec(),
+        compiler_params=params(20),
+        cost_estimate=pl.CostEstimate(
+            flops=count * CAP * BLK * BLK * 8, bytes_accessed=count * CAP * BLK * BLK * 2,
             transcendentals=0),
-    )(own, *arrived)
+    )(before, *arrived)
 
 
 def grad_kernel(ids, has_sum, last, table, *refs):
     count = len(ids)
-    blocks, parts = refs[:count], refs[count:count + 8]
-    refs = refs[count + 8:]
+    blocks, parts = refs[:count], refs[count:count + 4]
+    refs = refs[count + 4:]
     before = refs[0] if has_sum else None
     out, weights, total = refs[1 if has_sum else 0:]
     side = table[SIDE_AT]
     core = table[SIDE_AT + 1]
-    for k in range(8):
-        weights[core if k < 4 else 1 - core, (k % 4) * 512:(k % 4 + 1) * 512, :] = parts[k][...]
+    for k in range(4):
+        rows = slice(0, 1536) if k % 2 == 0 else slice(1536, 2048)
+        weights[core if k < 2 else 1 - core, rows, :] = parts[k][...]
     for k, place in enumerate(ids):
         dxh = COLS[place][1]
         first = pl.multiple_of((side if dxh == 0 else 1 - side) * 512, 512)
@@ -214,13 +216,33 @@
     return pl.pallas_call(
         functools.partial(grad_kernel, tuple(ids), has_sum, last),
         out_shape=jax.ShapeDtypeStruct((512, 512), BF16 if last else F32),
-        in_specs=[smem_spec()] + [vmem_spec()] * (count + 8 + has_sum),
+        in_specs=[smem_spec()] + [vmem_spec()] * (count + 4 + has_sum),
         out_specs=vmem_spec(),
         scratch_shapes=[pltpu.VMEM((2, 2048, 1024), BF16), pltpu.VMEM((512, 512), F32)],
         compiler_params=params(GRAD_MIB),
         cost_estimate=pl.CostEstimate(
             flops=2 * 512 ** 3 * count, bytes_accessed=(8 + count) * 1024 * 1024, transcendentals=0),
     )(table, *blocks, *parts, *([before] if has_sum else []))
+
+
+def join_kernel(*refs):
+    first = 0
+    for part in refs[:-1]:
+        refs[-1][first:first + part.shape[0], :] = part[...]
+        first += part.shape[0]
+
+
+def join(parts):
+    rows = sum(part.shape[0] for part in parts)
+    return pl.pallas_call(
+        join_kernel,
+        out_shape=jax.ShapeDtypeStruct((rows, parts[0].shape[1]), parts[0].dtype),
+        in_specs=[vmem_spec()] * len(parts),
+        out_specs=vmem_spec(),
+        compiler_params=params(20),
+        cost_estimate=pl.CostEstimate(
+            flops=0, bytes_accessed=4 * rows * parts[0].shape[1], transcendentals=0),
+    )(*parts)
 
 
 def body(inputs, grad_out, weight, blocks, owner):
@@ -279,40 +301,41 @@
     xt = inputs.T
 
     half = lax.dynamic_slice_in_dim(weight, core * 256, 256, 0)
-    far_half, r1, f1, table, xt = together(
-        (to_row(half, 1, 0), back(grad_out), ahead(grad_out), table, xt))
+    o0 = across(grad_out)
+    r1, f1, table, xt, half = together((back(grad_out), ahead(grad_out), table, xt, half))
+
+    total = dense(None, table, xt, [grad_out, f1, r1], 0)
+    o0, far_half, r2, f2, total = together((o0, to_row(half, 1, 0), back(r1), ahead(f1), total))
 
     pair = jnp.concatenate([half, far_half], axis=0)
-    total = dense(None, table, xt, [grad_out, f1, r1], 0)
-    s0, w1, o0, r2, f2, total = together(
-        (to_core(pair), around(pair), across(grad_out), back(r1), ahead(f1), total))
-
     total = dense(total, table, xt, [f2, r2, o0], 3)
-    s1, w2, of2, r3, f3, total = together(
-        (to_core(w1), around(w1), across(f2), back(r2), ahead(f2), total))
+    w1, of2, of1, r3, f3, total = together(
+        (around(pair), across(f2), ahead(o0), back(r2), ahead(f2), total))
 
     total = dense(total, table, xt, [f3, r3, of2], 6)
-    w3, or2, or1, of1, f4, total = together(
-        (around(w2), across(r2), back(o0), ahead(o0), ahead(f3), total))
+    w2, or2, or1, f4, total = together((around(w1), across(r2), back(o0), ahead(f3), total))
 
     total = dense(total, table, xt, [f4, of1, or1, or2], 9)
-    s3, s2, of4, or3, of3, total = together(
-        (to_core(w3), to_core(w2), across(f4), back(or2), ahead(of2), total))
+    mine = join([pair, w1, w2])
+    w3, theirs, of4, or3, of3, total = together(
+        (around(w2), to_core(mine), across(f4), back(or2), ahead(of2), total))
 
     total = dense(total, table, xt, [of3, or3, of4], LAST)
-    parts = [pair, w1, w2, w3, s0, s1, s2, s3]
     cols = [grad_out, f1, r1, f2, r2, o0, f3, r3, of2, f4, of1, or1, or2, of3, or3, of4]
 
-    other_late = to_core(pick(table, EARLY, 8, total))
     other_early = to_core(pick(table, 0, EARLY, total))
     early = code(table, 0, EARLY, total, other_early, 0)
-    late = code(table, EARLY, 8, total, other_late, 1)
+    *early, w3, late_table = together((*early, w3, table))
+    other_late = to_core(pick(late_table, EARLY, 8, total))
+    parts = [mine, w3, theirs, to_core(w3)]
+    late = code(late_table, EARLY, 8, total, other_late, 1)
     coded = list(early) + list(late[:-1])
     arrived = [to_row(v, dx, dy) for v, (dx, dy) in zip(coded, DESTS)]
-    own, grad_table = together((late[-1], table))
+    own, grad_table = together((late[-1], late_table))
     grad_in = grad_sum(grad_table, range(16), cols, parts, None, True)
-    *arrived, grad_in = together((*arrived, grad_in))
-    pushed = total_sum(own, arrived)
+    first, second, grad_in = together((arrived[0], arrived[1], grad_in))
+    pushed = add_coded(own, [first, second, arrived[2], arrived[3]])
+    pushed = add_coded(pushed, arrived[4:])
     return grad_in, pushed.reshape(1, CAP, BLK, BLK)
 
 

time: 145 us -> 135 us (0.931)
  waiting for transfers between devices: 69.6 us -> 60.8 us
    ppermute x4, waiting for transfers between devices: 21.8 us -> 7.46 us  [across(): return lax.ppermute(v, 'col', X_SWAP)]
    ppermute x6, waiting for transfers between devices: 16.4 us -> 24.8 us  [ahead(): return lax.ppermute(v, ('col', 'srv'), z_shift(1))]
    ppermute x8, waiting for transfers between devices: 21.2 us -> 16.5 us  [to_row(): return lax.ppermute(v, 'row', row_shift(dx, dy))]
    ppermute x5, waiting for transfers between devices: 4.22 us -> 7.42 us  [back(): return lax.ppermute(v, ('col', 'srv'), z_shift(-1))]
    ppermute x4, starting transfers between devices: 5.76 us -> 8.36 us  [across(): return lax.ppermute(v, 'col', X_SWAP)]
    ppermute x6 -> x4, starting transfers between devices: 4.81 us -> 2.31 us  [to_core(): return lax.ppermute(v, 'srv', CORE_SWAP)]
    ppermute x3, starting transfers between devices: 6.23 us -> 4.45 us  [around(): return lax.ppermute(v, ('row', 'srv'), y_shift(1))]
    ppermute x6 -> x4, waiting for transfers between devices: 5.93 us -> 4.62 us  [to_core(): return lax.ppermute(v, 'srv', CORE_SWAP)]
  transfers between devices with their start and end apart: 32 -> 30, of which waited for: 15 -> 18; matrix products, arithmetic and copies ran while one was open for 4% -> 5% of each run, Pallas kernels for 11% -> 11%
where the time goes in v3:
time: 135 us
  waiting for transfers between devices  60.8 us (45%)
  starting transfers between devices  44.7 us (33%)
  Pallas kernels  20.9 us (15%)
  other arithmetic  4.68 us (3%)
  local copies, waits for them, and re-layouts  2.63 us (2%)
    ppermute x6, waiting for transfers between devices, ahead(): return lax.ppermute(v, ('col', 'srv'), z_shift(1))  24.8 us
    ppermute x6, starting transfers between devices, ahead(): return lax.ppermute(v, ('col', 'srv'), z_shift(1))  17.7 us
    ppermute x8, waiting for transfers between devices, to_row(): return lax.ppermute(v, 'row', row_shift(dx, dy))  16.5 us
    ppermute x8, starting transfers between devices, to_row(): return lax.ppermute(v, 'row', row_shift(dx, dy))  10.5 us
    ppermute x4, starting transfers between devices, across(): return lax.ppermute(v, 'col', X_SWAP)  8.36 us
    pallas_call x5, Pallas kernels, dense(): pl.pallas_call(functools.partial(dense_kernel, count, place, first), out_...  7.92 us
    ppermute x4, waiting for transfers between devices, across(): return lax.ppermute(v, 'col', X_SWAP)  7.46 us
    ppermute x5, waiting for transfers between devices, back(): return lax.ppermute(v, ('col', 'srv'), z_shift(-1))  7.42 us
  transfers between devices with their start and end apart: 30, of which 18 were waited for; matrix products, arithmetic and copies ran while one was open for 5% of the time, Pallas kernels for 11%

profile of v3, /device:TPU:1, one launch (start us, length us, event | category | flops | bytes accessed | tf_op | source)
XLA Modules:
  0.0 134.6 jit_solution(1817556604508331823)
XLA Ops:
  0.6 3.7 %collective-permute-start.2 = (bf16[512,512]{1,0:T(8,128)(2,1)}, bf16[512,512]{1,0:T(8,128)(2,1)S(1)}, u32[]{:S(2)}, u32[]{:S(2)}) collective-permute-start(bf16[512,512]{1,0:T(8,128)(2,1)} %refs_0_.3), channel_id=1, source_target_pairs={{0,2},{2,0},{4,6},{6,4},{8,10},{10,8},{12,14},{14,12},{16,18},{18,... | collective-permute-start | bytes 1572872 | tf_op jit(solution)/shard_map/ppermute | solution.py:264
  4.3 5.6 %collective-permute-start.1 = (bf16[512,512]{1,0:T(8,128)(2,1)}, bf16[512,512]{1,0:T(8,128)(2,1)S(1)}, u32[]{:S(2)}, u32[]{:S(2)}) collective-permute-start(bf16[512,512]{1,0:T(8,128)(2,1)} %refs_0_.3), channel_id=1, source_target_pairs={{0,4},{1,29},{2,6},{3,31},{4,8},{5,1},{6,10},{7,3},{8,12},{9,5},{1... | collective-permute-start | bytes 1572872 | tf_op jit(solution)/shard_map/ppermute | solution.py:258
  16.0 4.5 %collective-permute-done.1.refs_1_ = bf16[512,512]{1,0:T(8,128)(2,1)S(1)} collective-permute-done((bf16[512,512]{1,0:T(8,128)(2,1)}, bf16[512,512]{1,0:T(8,128)(2,1)S(1)}, u32[]{:S(2)}, u32[]{:S(2)}) %collective-permute-start.1) | collective-permute-done | bytes 524320 | tf_op jit(solution)/shard_map/ppermute | solution.py:258
  20.5 3.0 %collective-permute-done.refs_2_ = bf16[512,512]{1,0:T(8,128)(2,1)S(1)} collective-permute-done((bf16[512,512]{1,0:T(8,128)(2,1)}, bf16[512,512]{1,0:T(8,128)(2,1)S(1)}, u32[]{:S(2)}, u32[]{:S(2)}) %collective-permute-start) | collective-permute-done | bytes 524320 | tf_op jit(solution)/shard_map/ppermute | solution.py:261
  23.8 2.7 %collective-permute-start.5 = (bf16[512,512]{1,0:T(8,128)(2,1)S(1)}, bf16[512,512]{1,0:T(8,128)(2,1)S(1)}, u32[]{:S(2)}, u32[]{:S(2)}) collective-permute-start(bf16[512,512]{1,0:T(8,128)(2,1)S(1)} %collective-permute-done.1.refs_1_), channel_id=1, source_target_pairs={{0,4},{1,29},{2,6},{3,31},{4,8},{5,1},{6,10},{7,3},{8,12},{9,5},{1... | collective-permute-start | bytes 1572872 | tf_op jit(solution)/shard_map/ppermute | solution.py:258
  29.1 7.9 %collective-permute-done.3 = bf16[256,1024]{1,0:T(8,128)(2,1)S(1)} collective-permute-done((bf16[256,1024]{1,0:T(8,128)(2,1)S(1)}, bf16[256,1024]{1,0:T(8,128)(2,1)S(1)}, u32[]{:S(2)}, u32[]{:S(2)}) %collective-permute-start.3) | collective-permute-done | bytes 524320 | tf_op jit(solution)/shard_map/ppermute | solution.py:270
  38.0 2.8 %collective-permute-start.6 = (bf16[512,1024]{1,0:T(8,128)(2,1)S(1)}, bf16[512,1024]{1,0:T(8,128)(2,1)S(1)}, u32[]{:S(2)}, u32[]{:S(2)}) collective-permute-start(bf16[512,1024]{1,0:T(8,128)(2,1)S(1)} %constant_dynamic-update-slice_fusion.refs_0_), channel_id=1, source_target_pairs={{0,32},{1,97},{32,64},{33,1},{64,96},{65,33},{96,0},{97,65},{128,1... | collective-permute-start | bytes 3145736 | tf_op jit(solution)/shard_map/ppermute | solution.py:267
  40.8 3.4 %collective-permute-start.10 = (bf16[512,512]{1,0:T(8,128)(2,1)S(1)}, bf16[512,512]{1,0:T(8,128)(2,1)S(1)}, u32[]{:S(2)}, u32[]{:S(2)}) collective-permute-start(bf16[512,512]{1,0:T(8,128)(2,1)S(1)} %collective-permute-done.5.refs_0_.refs_3_), channel_id=1, source_target_pairs={{0,4},{1,29},{2,6},{3,31},{4,8},{5,1},{6,10},{7,3},{8,12},{9,5},{1... | collective-permute-start | bytes 1572872 | tf_op jit(solution)/shard_map/ppermute | solution.py:258
  48.9 4.7 %collective-permute-done.10.refs_0_.refs_6_ = bf16[512,512]{1,0:T(8,128)(2,1)S(1)} collective-permute-done((bf16[512,512]{1,0:T(8,128)(2,1)S(1)}, bf16[512,512]{1,0:T(8,128)(2,1)S(1)}, u32[]{:S(2)}, u32[]{:S(2)}) %collective-permute-start.10) | collective-permute-done | bytes 524320 | tf_op jit(solution)/shard_map/ppermute | solution.py:258
  53.6 3.0 %collective-permute-done.7.refs_2_.refs_8_ = bf16[512,512]{1,0:T(8,128)(2,1)S(1)} collective-permute-done((bf16[512,512]{1,0:T(8,128)(2,1)S(1)}, bf16[512,512]{1,0:T(8,128)(2,1)S(1)}, u32[]{:S(2)}, u32[]{:S(2)}) %collective-permute-start.7) | collective-permute-done | bytes 524320 | tf_op jit(solution)/shard_map/ppermute | solution.py:264
  56.6 4.9 %collective-permute-done.8.refs_1_.refs_10_ = bf16[512,512]{1,0:T(8,128)(2,1)S(1)} collective-permute-done((bf16[512,512]{1,0:T(8,128)(2,1)S(1)}, bf16[512,512]{1,0:T(8,128)(2,1)S(1)}, u32[]{:S(2)}, u32[]{:S(2)}) %collective-permute-start.8) | collective-permute-done | bytes 524320 | tf_op jit(solution)/shard_map/ppermute | solution.py:258
  63.8 3.1 %collective-permute-start.14 = (bf16[512,512]{1,0:T(8,128)(2,1)S(1)}, bf16[512,512]{1,0:T(8,128)(2,1)S(1)}, u32[]{:S(2)}, u32[]{:S(2)}) collective-permute-start(bf16[512,512]{1,0:T(8,128)(2,1)S(1)} %collective-permute-done.10.refs_0_.refs_6_), channel_id=1, source_target_pairs={{0,4},{1,29},{2,6},{3,31},{4,8},{5,1},{6,10},{7,3},{8,12},{9,5},{1... | collective-permute-start | bytes 1572872 | tf_op jit(solution)/shard_map/ppermute | solution.py:258
  68.5 4.4 %collective-permute-done.13.refs_2_.refs_11_ = bf16[512,512]{1,0:T(8,128)(2,1)S(1)} collective-permute-done((bf16[512,512]{1,0:T(8,128)(2,1)S(1)}, bf16[512,512]{1,0:T(8,128)(2,1)S(1)}, u32[]{:S(2)}, u32[]{:S(2)}) %collective-permute-start.13) | collective-permute-done | bytes 524320 | tf_op jit(solution)/shard_map/ppermute | solution.py:261
  73.8 3.4 %collective-permute-done.14.refs_0_.refs_9_ = bf16[512,512]{1,0:T(8,128)(2,1)S(1)} collective-permute-done((bf16[512,512]{1,0:T(8,128)(2,1)S(1)}, bf16[512,512]{1,0:T(8,128)(2,1)S(1)}, u32[]{:S(2)}, u32[]{:S(2)}) %collective-permute-start.14) | collective-permute-done | bytes 524320 | tf_op jit(solution)/shard_map/ppermute | solution.py:258
  80.1 2.9 %collective-permute-start.19 = (bf16[512,512]{1,0:T(8,128)(2,1)S(1)}, bf16[512,512]{1,0:T(8,128)(2,1)S(1)}, u32[]{:S(2)}, u32[]{:S(2)}) collective-permute-start(bf16[512,512]{1,0:T(8,128)(2,1)S(1)} %collective-permute-done.7.refs_2_.refs_8_), channel_id=1, source_target_pairs={{0,4},{1,29},{2,6},{3,31},{4,8},{5,1},{6,10},{7,3},{8,12},{9,5},{1... | collective-permute-start | bytes 1572872 | tf_op jit(solution)/shard_map/ppermute | solution.py:258
  86.1 6.4 %collective-permute-done.19.refs_0_.refs_13_ = bf16[512,512]{1,0:T(8,128)(2,1)S(1)} collective-permute-done((bf16[512,512]{1,0:T(8,128)(2,1)S(1)}, bf16[512,512]{1,0:T(8,128)(2,1)S(1)}, u32[]{:S(2)}, u32[]{:S(2)}) %collective-permute-start.19) | collective-permute-done | bytes 524320 | tf_op jit(solution)/shard_map/ppermute | solution.py:258
  92.5 3.5 %collective-permute-done.17.refs_2_.refs_15_ = bf16[512,512]{1,0:T(8,128)(2,1)S(1)} collective-permute-done((bf16[512,512]{1,0:T(8,128)(2,1)S(1)}, bf16[512,512]{1,0:T(8,128)(2,1)S(1)}, u32[]{:S(2)}, u32[]{:S(2)}) %collective-permute-start.17) | collective-permute-done | bytes 524320 | tf_op jit(solution)/shard_map/ppermute | solution.py:264
  98.4 2.6 %collective-permute-done.20.other = f32[16,128,128]{2,1,0:T(8,128)S(1)} collective-permute-done((f32[16,128,128]{2,1,0:T(8,128)S(1)}, f32[16,128,128]{2,1,0:T(8,128)S(1)}, u32[]{:S(2)}, u32[]{:S(2)}) %collective-permute-start.20) | collective-permute-done | bytes 1048608 | tf_op jit(solution)/shard_map/ppermute | solution.py:273
  106.5 2.0 %collective-permute-done.23.other = f32[48,128,128]{2,1,0:T(8,128)S(1)} collective-permute-done((f32[48,128,128]{2,1,0:T(8,128)S(1)}, f32[48,128,128]{2,1,0:T(8,128)S(1)}, u32[]{:S(2)}, u32[]{:S(2)}) %collective-permute-start.23) | collective-permute-done | bytes 3145760 | tf_op jit(solution)/shard_map/ppermute | solution.py:273
  110.0 2.4 %collective-permute-start.25 = (bf16[1040,128]{1,0:T(8,128)(2,1)S(1)}, bf16[1040,128]{1,0:T(8,128)(2,1)S(1)}, u32[]{:S(2)}, u32[]{:S(2)}) collective-permute-start(bf16[1040,128]{1,0:T(8,128)(2,1)S(1)} %get-tuple-element.85), channel_id=1, source_target_pairs={{0,224},{32,128},{64,160},{96,192},{128,96},{160,0},{192,32},{224,... | collective-permute-start | bytes 798728 | tf_op jit(solution)/shard_map/ppermute | solution.py:270
  114.9 4.4 %collective-permute-done.22.refs_1_ = bf16[1040,128]{1,0:T(8,128)(2,1)S(1)} collective-permute-done((bf16[1040,128]{1,0:T(8,128)(2,1)S(1)}, bf16[1040,128]{1,0:T(8,128)(2,1)S(1)}, u32[]{:S(2)}, u32[]{:S(2)}) %collective-permute-start.22) | collective-permute-done | bytes 266272 | tf_op jit(solution)/shard_map/ppermute | solution.py:270
  119.3 2.7 %collective-permute-start.29 = (bf16[1040,128]{1,0:T(8,128)(2,1)S(1)}, bf16[1040,128]{1,0:T(8,128)(2,1)S(1)}, u32[]{:S(2)}, u32[]{:S(2)}) collective-permute-start(bf16[1040,128]{1,0:T(8,128)(2,1)S(1)} %get-tuple-element.89), channel_id=1, source_target_pairs={{0,96},{32,0},{64,32},{96,64},{128,224},{160,128},{192,160},{224,1... | collective-permute-start | bytes 798728 | tf_op jit(solution)/shard_map/ppermute | solution.py:270
  122.0 6.6 %shard_map.168 = bf16[512,512]{1,0:T(8,128)(2,1)} custom-call(s32[194]{0:T(256)S(1)} %concatenate.6.table, bf16[512,512]{1,0:T(8,128)(2,1)S(1)} %copy-done.4, bf16[512,512]{1,0:T(8,128)(2,1)S(1)} %collective-permute-done.1.refs_1_, bf16[512,512]{1,0:T(8,128)(2,1)S(1)} %collective-permute-done.refs_2_, ...), custom_call_target="tpu_custom_call" | custom-call | flops 4294967296 | bytes 25165824 | tf_op jit(solution)/shard_map/pallas_call | solution.py:216
  131.2 1.9 %collective-permute-done.29.refs_2_ = bf16[1040,128]{1,0:T(8,128)(2,1)S(1)} collective-permute-done((bf16[1040,128]{1,0:T(8,128)(2,1)S(1)}, bf16[1040,128]{1,0:T(8,128)(2,1)S(1)}, u32[]{:S(2)}, u32[]{:S(2)}) %collective-permute-start.29) | collective-permute-done | bytes 266272 | tf_op jit(solution)/shard_map/ppermute | solution.py:270
  (86 shorter events, 41.4 us)
Async XLA Ops:
  0.6 28.4 %collective-permute-start.2 = (bf16[512,512]{1,0:T(8,128)(2,1)}, bf16[512,512]{1,0:T(8,128)(2,1)S(1)}, u32[]{:S(2)}, u32[]{:S(2)}) collective-permute-start(bf16[512,512]{1,0:T(8,128)(2,1)} %refs_0_.3), channel_id=1, source_target_pairs={{0,2},{2,0},{4,6},{6,4},{8,10},{10,8},{12,14},{14,12},{16,18},{18,... | collective-permute-start | bytes 1572872 | tf_op jit(solution)/shard_map/ppermute | solution.py:264
  4.3 16.2 %collective-permute-start.1 = (bf16[512,512]{1,0:T(8,128)(2,1)}, bf16[512,512]{1,0:T(8,128)(2,1)S(1)}, u32[]{:S(2)}, u32[]{:S(2)}) collective-permute-start(bf16[512,512]{1,0:T(8,128)(2,1)} %refs_0_.3), channel_id=1, source_target_pairs={{0,4},{1,29},{2,6},{3,31},{4,8},{5,1},{6,10},{7,3},{8,12},{9,5},{1... | collective-permute-start | bytes 1572872 | tf_op jit(solution)/shard_map/ppermute | solution.py:258
  9.9 13.6 %collective-permute-start = (bf16[512,512]{1,0:T(8,128)(2,1)}, bf16[512,512]{1,0:T(8,128)(2,1)S(1)}, u32[]{:S(2)}, u32[]{:S(2)}) collective-permute-start(bf16[512,512]{1,0:T(8,128)(2,1)} %refs_0_.3), channel_id=1, source_target_pairs={{0,28},{1,5},{2,30},{3,7},{4,0},{5,9},{6,2},{7,11},{8,4},{9,13},{1... | collective-permute-start | bytes 1572872 | tf_op jit(solution)/shard_map/ppermute | solution.py:261
  23.4 13.5 %collective-permute-start.3 = (bf16[256,1024]{1,0:T(8,128)(2,1)S(1)}, bf16[256,1024]{1,0:T(8,128)(2,1)S(1)}, u32[]{:S(2)}, u32[]{:S(2)}) collective-permute-start(bf16[256,1024]{1,0:T(8,128)(2,1)S(1)} %constant_dynamic-slice_fusion), channel_id=1, source_target_pairs={{0,128},{32,160},{64,192},{96,224},{128,0},{160,32},{192,64},{224,... | collective-permute-start | bytes 1572872 | tf_op jit(solution)/shard_map/ppermute | solution.py:270
  23.8 13.2 %collective-permute-start.4 = (bf16[512,512]{1,0:T(8,128)(2,1)S(1)}, bf16[512,512]{1,0:T(8,128)(2,1)S(1)}, u32[]{:S(2)}, u32[]{:S(2)}) collective-permute-start(bf16[512,512]{1,0:T(8,128)(2,1)S(1)} %collective-permute-done.refs_2_), channel_id=1, source_target_pairs={{0,28},{1,5},{2,30},{3,7},{4,0},{5,9},{6,2},{7,11},{8,4},{9,13},{1... | collective-permute-start | bytes 1572872 | tf_op jit(solution)/shard_map/ppermute | solution.py:261
  23.8 14.2 %collective-permute-start.5 = (bf16[512,512]{1,0:T(8,128)(2,1)S(1)}, bf16[512,512]{1,0:T(8,128)(2,1)S(1)}, u32[]{:S(2)}, u32[]{:S(2)}) collective-permute-start(bf16[512,512]{1,0:T(8,128)(2,1)S(1)} %collective-permute-done.1.refs_1_), channel_id=1, source_target_pairs={{0,4},{1,29},{2,6},{3,31},{4,8},{5,1},{6,10},{7,3},{8,12},{9,5},{1... | collective-permute-start | bytes 1572872 | tf_op jit(solution)/shard_map/ppermute | solution.py:258
  38.0 23.6 %collective-permute-start.6 = (bf16[512,1024]{1,0:T(8,128)(2,1)S(1)}, bf16[512,1024]{1,0:T(8,128)(2,1)S(1)}, u32[]{:S(2)}, u32[]{:S(2)}) collective-permute-start(bf16[512,1024]{1,0:T(8,128)(2,1)S(1)} %constant_dynamic-update-slice_fusion.refs_0_), channel_id=1, source_target_pairs={{0,32},{1,97},{32,64},{33,1},{64,96},{65,33},{96,0},{97,65},{128,1... | collective-permute-start | bytes 3145736 | tf_op jit(solution)/shard_map/ppermute | solution.py:267
  40.8 12.8 %collective-permute-start.10 = (bf16[512,512]{1,0:T(8,128)(2,1)S(1)}, bf16[512,512]{1,0:T(8,128)(2,1)S(1)}, u32[]{:S(2)}, u32[]{:S(2)}) collective-permute-start(bf16[512,512]{1,0:T(8,128)(2,1)S(1)} %collective-permute-done.5.refs_0_.refs_3_), channel_id=1, source_target_pairs={{0,4},{1,29},{2,6},{3,31},{4,8},{5,1},{6,10},{7,3},{8,12},{9,5},{1... | collective-permute-start | bytes 1572872 | tf_op jit(solution)/shard_map/ppermute | solution.py:258
  44.2 12.4 %collective-permute-start.7 = (bf16[512,512]{1,0:T(8,128)(2,1)S(1)}, bf16[512,512]{1,0:T(8,128)(2,1)S(1)}, u32[]{:S(2)}, u32[]{:S(2)}) collective-permute-start(bf16[512,512]{1,0:T(8,128)(2,1)S(1)} %collective-permute-done.5.refs_0_.refs_3_), channel_id=1, source_target_pairs={{0,2},{2,0},{4,6},{6,4},{8,10},{10,8},{12,14},{14,12},{16,18},{18,... | collective-permute-start | bytes 1572872 | tf_op jit(solution)/shard_map/ppermute | solution.py:264
  45.9 15.6 %collective-permute-start.8 = (bf16[512,512]{1,0:T(8,128)(2,1)S(1)}, bf16[512,512]{1,0:T(8,128)(2,1)S(1)}, u32[]{:S(2)}, u32[]{:S(2)}) collective-permute-start(bf16[512,512]{1,0:T(8,128)(2,1)S(1)} %collective-permute-done.2.refs_2_.refs_5_), channel_id=1, source_target_pairs={{0,4},{1,29},{2,6},{3,31},{4,8},{5,1},{6,10},{7,3},{8,12},{9,5},{1... | collective-permute-start | bytes 1572872 | tf_op jit(solution)/shard_map/ppermute | solution.py:258
  45.9 15.6 %collective-permute-start.9 = (bf16[512,512]{1,0:T(8,128)(2,1)S(1)}, bf16[512,512]{1,0:T(8,128)(2,1)S(1)}, u32[]{:S(2)}, u32[]{:S(2)}) collective-permute-start(bf16[512,512]{1,0:T(8,128)(2,1)S(1)} %collective-permute-done.4.refs_1_.refs_4_), channel_id=1, source_target_pairs={{0,28},{1,5},{2,30},{3,7},{4,0},{5,9},{6,2},{7,11},{8,4},{9,13},{1... | collective-permute-start | bytes 1572872 | tf_op jit(solution)/shard_map/ppermute | solution.py:261
  61.5 15.6 %collective-permute-start.11 = (bf16[512,1024]{1,0:T(8,128)(2,1)S(1)}, bf16[512,1024]{1,0:T(8,128)(2,1)S(1)}, u32[]{:S(2)}, u32[]{:S(2)}) collective-permute-start(bf16[512,1024]{1,0:T(8,128)(2,1)S(1)} %collective-permute-done.6.refs_1_), channel_id=1, source_target_pairs={{0,32},{1,97},{32,64},{33,1},{64,96},{65,33},{96,0},{97,65},{128,1... | collective-permute-start | bytes 3145736 | tf_op jit(solution)/shard_map/ppermute | solution.py:267
  63.8 13.4 %collective-permute-start.14 = (bf16[512,512]{1,0:T(8,128)(2,1)S(1)}, bf16[512,512]{1,0:T(8,128)(2,1)S(1)}, u32[]{:S(2)}, u32[]{:S(2)}) collective-permute-start(bf16[512,512]{1,0:T(8,128)(2,1)S(1)} %collective-permute-done.10.refs_0_.refs_6_), channel_id=1, source_target_pairs={{0,4},{1,29},{2,6},{3,31},{4,8},{5,1},{6,10},{7,3},{8,12},{9,5},{1... | collective-permute-start | bytes 1572872 | tf_op jit(solution)/shard_map/ppermute | solution.py:258
  77.4 18.6 %collective-permute-start.16 = (bf16[1536,1024]{1,0:T(8,128)(2,1)S(1)}, bf16[1536,1024]{1,0:T(8,128)(2,1)S(1)}, u32[]{:S(2)}, u32[]{:S(2)}) collective-permute-start(bf16[1536,1024]{1,0:T(8,128)(2,1)S(1)} %shard_map.161.refs_16_), channel_id=1, source_target_pairs={{0,1},{1,0},{2,3},{3,2},{4,5},{5,4},{6,7},{7,6},{8,9},{9,8},{10,11... | collective-permute-start | bytes 9437192 | tf_op jit(solution)/shard_map/ppermute | solution.py:273
  79.0 17.0 %collective-permute-start.15 = (bf16[512,1024]{1,0:T(8,128)(2,1)S(1)}, bf16[512,1024]{1,0:T(8,128)(2,1)S(1)}, u32[]{:S(2)}, u32[]{:S(2)}) collective-permute-start(bf16[512,1024]{1,0:T(8,128)(2,1)S(1)} %collective-permute-done.11.refs_2_), channel_id=1, source_target_pairs={{0,32},{1,97},{32,64},{33,1},{64,96},{65,33},{96,0},{97,65},{128,1... | collective-permute-start | bytes 3145736 | tf_op jit(solution)/shard_map/ppermute | solution.py:267
  80.1 12.3 %collective-permute-start.19 = (bf16[512,512]{1,0:T(8,128)(2,1)S(1)}, bf16[512,512]{1,0:T(8,128)(2,1)S(1)}, u32[]{:S(2)}, u32[]{:S(2)}) collective-permute-start(bf16[512,512]{1,0:T(8,128)(2,1)S(1)} %collective-permute-done.7.refs_2_.refs_8_), channel_id=1, source_target_pairs={{0,4},{1,29},{2,6},{3,31},{4,8},{5,1},{6,10},{7,3},{8,12},{9,5},{1... | collective-permute-start | bytes 1572872 | tf_op jit(solution)/shard_map/ppermute | solution.py:258
  83.0 13.0 %collective-permute-start.17 = (bf16[512,512]{1,0:T(8,128)(2,1)S(1)}, bf16[512,512]{1,0:T(8,128)(2,1)S(1)}, u32[]{:S(2)}, u32[]{:S(2)}) collective-permute-start(bf16[512,512]{1,0:T(8,128)(2,1)S(1)} %collective-permute-done.14.refs_0_.refs_9_), channel_id=1, source_target_pairs={{0,2},{2,0},{4,6},{6,4},{8,10},{10,8},{12,14},{14,12},{16,18},{18,... | collective-permute-start | bytes 1572872 | tf_op jit(solution)/shard_map/ppermute | solution.py:264
  103.0 16.3 %collective-permute-start.24 = (bf16[512,1024]{1,0:T(8,128)(2,1)S(1)}, bf16[512,1024]{1,0:T(8,128)(2,1)S(1)}, u32[]{:S(2)}, u32[]{:S(2)}) collective-permute-start(bf16[512,1024]{1,0:T(8,128)(2,1)S(1)} %collective-permute-done.15.refs_17_), channel_id=1, source_target_pairs={{0,1},{1,0},{2,3},{3,2},{4,5},{5,4},{6,7},{7,6},{8,9},{9,8},{10,11... | collective-permute-start | bytes 3145736 | tf_op jit(solution)/shard_map/ppermute | solution.py:273
  104.9 14.4 %collective-permute-start.22 = (bf16[1040,128]{1,0:T(8,128)(2,1)S(1)}, bf16[1040,128]{1,0:T(8,128)(2,1)S(1)}, u32[]{:S(2)}, u32[]{:S(2)}) collective-permute-start(bf16[1040,128]{1,0:T(8,128)(2,1)S(1)} %get-tuple-element.75), channel_id=1, source_target_pairs={{0,160},{32,192},{64,224},{96,128},{128,32},{160,64},{192,96},{224... | collective-permute-start | bytes 798728 | tf_op jit(solution)/shard_map/ppermute | solution.py:270
  110.0 18.6 %collective-permute-start.25 = (bf16[1040,128]{1,0:T(8,128)(2,1)S(1)}, bf16[1040,128]{1,0:T(8,128)(2,1)S(1)}, u32[]{:S(2)}, u32[]{:S(2)}) collective-permute-start(bf16[1040,128]{1,0:T(8,128)(2,1)S(1)} %get-tuple-element.85), channel_id=1, source_target_pairs={{0,224},{32,128},{64,160},{96,192},{128,96},{160,0},{192,32},{224,... | collective-permute-start | bytes 798728 | tf_op jit(solution)/shard_map/ppermute | solution.py:270
  112.4 17.9 %collective-permute-start.26 = (bf16[1040,128]{1,0:T(8,128)(2,1)S(1)}, bf16[1040,128]{1,0:T(8,128)(2,1)S(1)}, u32[]{:S(2)}, u32[]{:S(2)}) collective-permute-start(bf16[1040,128]{1,0:T(8,128)(2,1)S(1)} %get-tuple-element.86), channel_id=1, source_target_pairs={{0,128},{32,160},{64,192},{96,224},{128,0},{160,32},{192,64},{224,... | collective-permute-start | bytes 798728 | tf_op jit(solution)/shard_map/ppermute | solution.py:270
  113.6 17.6 %collective-permute-start.27 = (bf16[1040,128]{1,0:T(8,128)(2,1)S(1)}, bf16[1040,128]{1,0:T(8,128)(2,1)S(1)}, u32[]{:S(2)}, u32[]{:S(2)}) collective-permute-start(bf16[1040,128]{1,0:T(8,128)(2,1)S(1)} %get-tuple-element.87), channel_id=1, source_target_pairs={{0,64},{32,96},{64,0},{96,32},{128,192},{160,224},{192,128},{224,1... | collective-permute-start | bytes 798728 | tf_op jit(solution)/shard_map/ppermute | solution.py:270
  119.3 11.9 %collective-permute-start.28 = (bf16[1040,128]{1,0:T(8,128)(2,1)S(1)}, bf16[1040,128]{1,0:T(8,128)(2,1)S(1)}, u32[]{:S(2)}, u32[]{:S(2)}) collective-permute-start(bf16[1040,128]{1,0:T(8,128)(2,1)S(1)} %get-tuple-element.88), channel_id=1, source_target_pairs={{0,32},{32,64},{64,96},{96,0},{128,160},{160,192},{192,224},{224,1... | collective-permute-start | bytes 798728 | tf_op jit(solution)/shard_map/ppermute | solution.py:270
  119.3 13.8 %collective-permute-start.29 = (bf16[1040,128]{1,0:T(8,128)(2,1)S(1)}, bf16[1040,128]{1,0:T(8,128)(2,1)S(1)}, u32[]{:S(2)}, u32[]{:S(2)}) collective-permute-start(bf16[1040,128]{1,0:T(8,128)(2,1)S(1)} %get-tuple-element.89), channel_id=1, source_target_pairs={{0,96},{32,0},{64,32},{96,64},{128,224},{160,128},{192,160},{224,1... | collective-permute-start | bytes 798728 | tf_op jit(solution)/shard_map/ppermute | solution.py:270
  (17 other events, 219.4 us)

commit v4 on v3

--- a/solution.py
+++ b/solution.py
@@ -21,7 +21,8 @@
 LAST = 13
 DESTS = ((1, 2), (1, 1), (1, 3), (1, 0), (0, 2), (0, 1), (0, 3), (0, 0))
 EARLY = 2
-DENSE_MIB = PICK_MIB = CODE_MIB = GRAD_MIB = 20
+PHASE_FLOPS = 30 * 10 ** 9
+DENSE_MIB = PICK_MIB = CODE_MIB = GRAD_MIB = 10
 COL_AT, ROW_AT, SIDE_AT, MINE_AT, THEIRS_AT, SLOT_AT = 0, 16, 48, 50, 58, 66
 
 
@@ -82,7 +83,7 @@
         input_output_aliases={} if first else {2 + count: 0},
         compiler_params=params(DENSE_MIB),
         cost_estimate=pl.CostEstimate(
-            flops=count * 2 * 512 ** 3, bytes_accessed=count * 3 * 512 * 1024, transcendentals=0),
+            flops=PHASE_FLOPS, bytes_accessed=count * 3 * 512 * 1024, transcendentals=0),
     )(*args)
 
 
@@ -173,56 +174,46 @@
         out_shape=jax.ShapeDtypeStruct((CAP, BLK, BLK), F32),
         in_specs=[vmem_spec()] * (1 + count),
         out_specs=vmem_spec(),
-        compiler_params=params(20),
+        compiler_params=params(10),
         cost_estimate=pl.CostEstimate(
             flops=count * CAP * BLK * BLK * 8, bytes_accessed=count * CAP * BLK * BLK * 2,
             transcendentals=0),
     )(before, *arrived)
 
 
-def grad_kernel(ids, has_sum, last, table, *refs):
+def grad_kernel(ids, table, *refs):
     count = len(ids)
-    blocks, parts = refs[:count], refs[count:count + 4]
-    refs = refs[count + 4:]
-    before = refs[0] if has_sum else None
-    out, weights, total = refs[1 if has_sum else 0:]
+    blocks, mine, theirs, out, total = refs[:count], *refs[count:]
     side = table[SIDE_AT]
     core = table[SIDE_AT + 1]
-    for k in range(4):
-        rows = slice(0, 1536) if k % 2 == 0 else slice(1536, 2048)
-        weights[core if k < 2 else 1 - core, rows, :] = parts[k][...]
     for k, place in enumerate(ids):
         dxh = COLS[place][1]
         first = pl.multiple_of((side if dxh == 0 else 1 - side) * 512, 512)
-        for h in range(2):
-            row = pl.multiple_of(table[ROW_AT + h * 16 + place] * 256, 256)
+        for part, half in enumerate((core, 1 - core)):
+            rows = pl.multiple_of(table[ROW_AT + half * 16 + place] * 256, 256)
+            weights = (mine, theirs)[part][pl.ds(rows, 256), pl.ds(first, 512)]
             made = lax.dot_general(
-                blocks[k][...], weights[h, pl.ds(row, 256), pl.ds(first, 512)],
-                (((1,), (1,)), ((), ())), preferred_element_type=F32)
-            cols = slice(h * 256, (h + 1) * 256)
+                blocks[k][...], weights, (((1,), (1,)), ((), ())), preferred_element_type=F32)
             if k > 0:
-                made = made + total[:, cols]
-            elif has_sum:
-                made = made + before[:, cols]
+                made = made + total[part]
             if k < count - 1:
-                total[:, cols] = made
+                total[part] = made
             else:
-                out[:, cols] = made.astype(out.dtype)
-
-
-def grad_sum(table, ids, blocks, parts, before, last):
+                out[:, pl.ds(pl.multiple_of(half * 256, 256), 256)] = made.astype(out.dtype)
+
+
+def grad_sum(table, ids, blocks, parts):
     count = len(ids)
-    has_sum = before is not None
-    return pl.pallas_call(
-        functools.partial(grad_kernel, tuple(ids), has_sum, last),
-        out_shape=jax.ShapeDtypeStruct((512, 512), BF16 if last else F32),
-        in_specs=[smem_spec()] + [vmem_spec()] * (count + 4 + has_sum),
-        out_specs=vmem_spec(),
-        scratch_shapes=[pltpu.VMEM((2, 2048, 1024), BF16), pltpu.VMEM((512, 512), F32)],
+    return pl.pallas_call(
+        functools.partial(grad_kernel, tuple(ids)),
+        out_shape=jax.ShapeDtypeStruct((512, 512), BF16),
+        in_specs=[smem_spec()] + [vmem_spec()] * (count + 2),
+        out_specs=vmem_spec(),
+        scratch_shapes=[pltpu.VMEM((2, 512, 256), F32)],
         compiler_params=params(GRAD_MIB),
         cost_estimate=pl.CostEstimate(
             flops=2 * 512 ** 3 * count, bytes_accessed=(8 + count) * 1024 * 1024, transcendentals=0),
-    )(table, *blocks, *parts, *([before] if has_sum else []))
+    )(table, *blocks, *parts)
 
 
 def join_kernel(*refs):
@@ -239,9 +230,9 @@
         out_shape=jax.ShapeDtypeStruct((rows, parts[0].shape[1]), parts[0].dtype),
         in_specs=[vmem_spec()] * len(parts),
         out_specs=vmem_spec(),
-        compiler_params=params(20),
-        cost_estimate=pl.CostEstimate(
-            flops=0, bytes_accessed=4 * rows * parts[0].shape[1], transcendentals=0),
+        compiler_params=params(10),
+        cost_estimate=pl.CostEstimate(
+            flops=0, bytes_accessed=0, transcendentals=0),
     )(*parts)
 
 
@@ -301,38 +292,45 @@
     xt = inputs.T
 
     half = lax.dynamic_slice_in_dim(weight, core * 256, 256, 0)
-    o0 = across(grad_out)
-    r1, f1, table, xt, half = together((back(grad_out), ahead(grad_out), table, xt, half))
-
-    total = dense(None, table, xt, [grad_out, f1, r1], 0)
-    o0, far_half, r2, f2, total = together((o0, to_row(half, 1, 0), back(r1), ahead(f1), total))
-
-    pair = jnp.concatenate([half, far_half], axis=0)
-    total = dense(total, table, xt, [f2, r2, o0], 3)
-    w1, of2, of1, r3, f3, total = together(
-        (around(pair), across(f2), ahead(o0), back(r2), ahead(f2), total))
-
-    total = dense(total, table, xt, [f3, r3, of2], 6)
-    w2, or2, or1, f4, total = together((around(w1), across(r2), back(o0), ahead(f3), total))
-
-    total = dense(total, table, xt, [f4, of1, or1, or2], 9)
-    mine = join([pair, w1, w2])
-    w3, theirs, of4, or3, of3, total = together(
-        (around(w2), to_core(mine), across(f4), back(or2), ahead(of2), total))
+    far_half = to_row(half, 1, 0)
+    r1, f1, own, table, xt = together((back(grad_out), ahead(grad_out), grad_out, table, xt))
+
+    near_half, far_half, own, now = together((half, far_half, own, table))
+    o0 = across(own)
+    pair = join([near_half, far_half])
+    w1 = around(pair)
+    total = dense(None, now, xt, [grad_out, f1, r1], 0)
+    o0, r2, f2, total = together((o0, back(r1), ahead(f1), total))
+
+    w1, now = together((w1, table))
+    w2 = around(w1)
+    total = dense(total, now, xt, [f2, r2, o0], 3)
+    of2, of1, r3, f3, total = together((across(f2), ahead(o0), back(r2), ahead(f2), total))
+
+    w2, now = together((w2, table))
+    w3 = around(w2)
+    total = dense(total, now, xt, [f3, r3, of2], 6)
+    or2, or1, f4, total = together((across(r2), back(o0), ahead(f3), total))
+
+    w3, now = together((w3, table))
+    mine = join([pair, w1, w2, w3])
+    theirs = to_core(mine)
+    total = dense(total, now, xt, [f4, of1, or1, or2], 9)
+    of4, or3, of3, total = together((across(f4), back(or2), ahead(of2), total))
 
     total = dense(total, table, xt, [of3, or3, of4], LAST)
     cols = [grad_out, f1, r1, f2, r2, o0, f3, r3, of2, f4, of1, or1, or2, of3, or3, of4]
 
     other_early = to_core(pick(table, 0, EARLY, total))
     early = code(table, 0, EARLY, total, other_early, 0)
-    *early, w3, late_table = together((*early, w3, table))
+    *early, theirs, late_table = together((*early, theirs, table))
     other_late = to_core(pick(late_table, EARLY, 8, total))
-    parts = [mine, w3, theirs, to_core(w3)]
+    parts = [mine, theirs]
     late = code(late_table, EARLY, 8, total, other_late, 1)
     coded = list(early) + list(late[:-1])
     arrived = [to_row(v, dx, dy) for v, (dx, dy) in zip(coded, DESTS)]
     own, grad_table = together((late[-1], late_table))
-    grad_in = grad_sum(grad_table, range(16), cols, parts, None, True)
+    grad_in = grad_sum(grad_table, range(16), cols, parts)
     first, second, grad_in = together((arrived[0], arrived[1], grad_in))
     pushed = add_coded(own, [first, second, arrived[2], arrived[3]])
     pushed = add_coded(pushed, arrived[4:])

time: 135 us -> 126 us (0.933)
  waiting for transfers between devices: 60.8 us -> 45.6 us
  starting transfers between devices: 44.7 us -> 50.6 us
    ppermute x6, waiting for transfers between devices: 24.8 us -> 6.74 us  [ahead(): return lax.ppermute(v, ('col', 'srv'), z_shift(1))]
    ppermute x4 -> x3, starting transfers between devices: 2.31 us -> 6.6 us  [to_core(): return lax.ppermute(v, 'srv', CORE_SWAP)]
    ppermute x3, starting transfers between devices: 4.45 us -> 8.28 us  [around(): return lax.ppermute(v, ('row', 'srv'), y_shift(1))]
    ppermute x4, waiting for transfers between devices: 7.46 us -> 11.2 us  [across(): return lax.ppermute(v, 'col', X_SWAP)]
    ppermute x8, waiting for transfers between devices: 16.5 us -> 12.9 us  [to_row(): return lax.ppermute(v, 'row', row_shift(dx, dy))]
    ppermute x6, starting transfers between devices: 17.7 us -> 15.5 us  [ahead(): return lax.ppermute(v, ('col', 'srv'), z_shift(1))]
    ppermute x5, waiting for transfers between devices: 7.42 us -> 9.52 us  [back(): return lax.ppermute(v, ('col', 'srv'), z_shift(-1))]
    ppermute x3, waiting for transfers between devices: 0.01 us -> 1.89 us  [around(): return lax.ppermute(v, ('row', 'srv'), y_shift(1))]
  transfers between devices with their start and end apart: 30 -> 29, of which waited for: 18 -> 16; matrix products, arithmetic and copies ran while one was open for 5% -> 5% of each run, Pallas kernels for 11% -> 15%
where the time goes in v4:
time: 126 us; the launch traced here: 125 us
  starting transfers between devices  50.6 us (40%)
  waiting for transfers between devices  45.6 us (36%)
  Pallas kernels  21.4 us (17%)
  other arithmetic  4.67 us (4%)
  local copies, waits for them, and re-layouts  2.43 us (2%)
    ppermute x6, starting transfers between devices, ahead(): return lax.ppermute(v, ('col', 'srv'), z_shift(1))  15.5 us
    ppermute x8, waiting for transfers between devices, to_row(): return lax.ppermute(v, 'row', row_shift(dx, dy))  12.9 us
    ppermute x4, waiting for transfers between devices, across(): return lax.ppermute(v, 'col', X_SWAP)  11.2 us
    ppermute x8, starting transfers between devices, to_row(): return lax.ppermute(v, 'row', row_shift(dx, dy))  10.5 us
    ppermute x5, waiting for transfers between devices, back(): return lax.ppermute(v, ('col', 'srv'), z_shift(-1))  9.52 us
    ppermute x3, starting transfers between devices, around(): return lax.ppermute(v, ('row', 'srv'), y_shift(1))  8.28 us
    pallas_call x5, Pallas kernels, dense(): pl.pallas_call(functools.partial(dense_kernel, count, place, first), out_...  7.91 us
    ppermute x4, starting transfers between devices, across(): return lax.ppermute(v, 'col', X_SWAP)  7.05 us
  transfers between devices with their start and end apart: 29, of which 16 were waited for; matrix products, arithmetic and copies ran while one was open for 5% of the time, Pallas kernels for 15%

profile of v4, /device:TPU:1, one launch (start us, length us, event | category | flops | bytes accessed | tf_op | source)
XLA Modules:
  0.0 125.4 jit_solution(6730412469058058774)
XLA Ops:
  0.6 2.5 %collective-permute-start = (bf16[512,512]{1,0:T(8,128)(2,1)}, bf16[512,512]{1,0:T(8,128)(2,1)S(1)}, u32[]{:S(2)}, u32[]{:S(2)}) collective-permute-start(bf16[512,512]{1,0:T(8,128)(2,1)} %refs_0_.3), channel_id=1, source_target_pairs={{0,28},{1,5},{2,30},{3,7},{4,0},{5,9},{6,2},{7,11},{8,4},{9,13},{1... | collective-permute-start | bytes 1572872 | tf_op jit(solution)/shard_map/ppermute | solution.py:252
  3.2 4.0 %collective-permute-start.1 = (bf16[512,512]{1,0:T(8,128)(2,1)}, bf16[512,512]{1,0:T(8,128)(2,1)S(1)}, u32[]{:S(2)}, u32[]{:S(2)}) collective-permute-start(bf16[512,512]{1,0:T(8,128)(2,1)} %refs_0_.3), channel_id=1, source_target_pairs={{0,4},{1,29},{2,6},{3,31},{4,8},{5,1},{6,10},{7,3},{8,12},{9,5},{1... | collective-permute-start | bytes 1572872 | tf_op jit(solution)/shard_map/ppermute | solution.py:249
  15.7 2.6 %collective-permute-done.1.refs_1_ = bf16[512,512]{1,0:T(8,128)(2,1)S(1)} collective-permute-done((bf16[512,512]{1,0:T(8,128)(2,1)}, bf16[512,512]{1,0:T(8,128)(2,1)S(1)}, u32[]{:S(2)}, u32[]{:S(2)}) %collective-permute-start.1) | collective-permute-done | bytes 524320 | tf_op jit(solution)/shard_map/ppermute | solution.py:249
  20.0 2.7 %collective-permute-start.3 = (bf16[512,512]{1,0:T(8,128)(2,1)}, bf16[512,512]{1,0:T(8,128)(2,1)S(1)}, u32[]{:S(2)}, u32[]{:S(2)}) collective-permute-start(bf16[512,512]{1,0:T(8,128)(2,1)} %refs_0_.3), channel_id=1, source_target_pairs={{0,2},{2,0},{4,6},{6,4},{8,10},{10,8},{12,14},{14,12},{16,18},{18,... | collective-permute-start | bytes 1572872 | tf_op jit(solution)/shard_map/ppermute | solution.py:255
  22.8 2.7 %collective-permute-start.5 = (bf16[512,512]{1,0:T(8,128)(2,1)S(1)}, bf16[512,512]{1,0:T(8,128)(2,1)S(1)}, u32[]{:S(2)}, u32[]{:S(2)}) collective-permute-start(bf16[512,512]{1,0:T(8,128)(2,1)S(1)} %collective-permute-done.1.refs_1_), channel_id=1, source_target_pairs={{0,4},{1,29},{2,6},{3,31},{4,8},{5,1},{6,10},{7,3},{8,12},{9,5},{1... | collective-permute-start | bytes 1572872 | tf_op jit(solution)/shard_map/ppermute | solution.py:249
  26.6 2.8 %collective-permute-start.12 = (bf16[512,1024]{1,0:T(8,128)(2,1)S(1)}, bf16[512,1024]{1,0:T(8,128)(2,1)S(1)}, u32[]{:S(2)}, u32[]{:S(2)}) collective-permute-start(bf16[512,1024]{1,0:T(8,128)(2,1)S(1)} %shard_map.159.refs_0_), channel_id=1, source_target_pairs={{0,32},{1,97},{32,64},{33,1},{64,96},{65,33},{96,0},{97,65},{128,1... | collective-permute-start | bytes 3145736 | tf_op jit(solution)/shard_map/ppermute | solution.py:258
  33.7 2.3 %collective-permute-done.5.refs_0_.refs_3_ = bf16[512,512]{1,0:T(8,128)(2,1)S(1)} collective-permute-done((bf16[512,512]{1,0:T(8,128)(2,1)S(1)}, bf16[512,512]{1,0:T(8,128)(2,1)S(1)}, u32[]{:S(2)}, u32[]{:S(2)}) %collective-permute-start.5) | collective-permute-done | bytes 524320 | tf_op jit(solution)/shard_map/ppermute | solution.py:249
  36.0 3.4 %collective-permute-start.11 = (bf16[512,512]{1,0:T(8,128)(2,1)S(1)}, bf16[512,512]{1,0:T(8,128)(2,1)S(1)}, u32[]{:S(2)}, u32[]{:S(2)}) collective-permute-start(bf16[512,512]{1,0:T(8,128)(2,1)S(1)} %collective-permute-done.5.refs_0_.refs_3_), channel_id=1, source_target_pairs={{0,4},{1,29},{2,6},{3,31},{4,8},{5,1},{6,10},{7,3},{8,12},{9,5},{1... | collective-permute-start | bytes 1572872 | tf_op jit(solution)/shard_map/ppermute | solution.py:249
  39.6 2.7 %collective-permute-start.9 = (bf16[512,512]{1,0:T(8,128)(2,1)S(1)}, bf16[512,512]{1,0:T(8,128)(2,1)S(1)}, u32[]{:S(2)}, u32[]{:S(2)}) collective-permute-start(bf16[512,512]{1,0:T(8,128)(2,1)S(1)} %collective-permute-done.3.refs_2_.refs_5_), channel_id=1, source_target_pairs={{0,4},{1,29},{2,6},{3,31},{4,8},{5,1},{6,10},{7,3},{8,12},{9,5},{1... | collective-permute-start | bytes 1572872 | tf_op jit(solution)/shard_map/ppermute | solution.py:249
  42.3 2.7 %collective-permute-start.14 = (bf16[512,1024]{1,0:T(8,128)(2,1)S(1)}, bf16[512,1024]{1,0:T(8,128)(2,1)S(1)}, u32[]{:S(2)}, u32[]{:S(2)}) collective-permute-start(bf16[512,1024]{1,0:T(8,128)(2,1)S(1)} %collective-permute-done.12.refs_1_), channel_id=1, source_target_pairs={{0,32},{1,97},{32,64},{33,1},{64,96},{65,33},{96,0},{97,65},{128,1... | collective-permute-start | bytes 3145736 | tf_op jit(solution)/shard_map/ppermute | solution.py:258
  46.5 8.2 %collective-permute-done.10.refs_1_.refs_7_ = bf16[512,512]{1,0:T(8,128)(2,1)S(1)} collective-permute-done((bf16[512,512]{1,0:T(8,128)(2,1)S(1)}, bf16[512,512]{1,0:T(8,128)(2,1)S(1)}, u32[]{:S(2)}, u32[]{:S(2)}) %collective-permute-start.10) | collective-permute-done | bytes 524320 | tf_op jit(solution)/shard_map/ppermute | solution.py:252
  54.7 2.8 %collective-permute-start.6 = (bf16[512,512]{1,0:T(8,128)(2,1)S(1)}, bf16[512,512]{1,0:T(8,128)(2,1)S(1)}, u32[]{:S(2)}, u32[]{:S(2)}) collective-permute-start(bf16[512,512]{1,0:T(8,128)(2,1)S(1)} %collective-permute-done.4.refs_1_.refs_4_), channel_id=1, source_target_pairs={{0,2},{2,0},{4,6},{6,4},{8,10},{10,8},{12,14},{14,12},{16,18},{18,... | collective-permute-start | bytes 1572872 | tf_op jit(solution)/shard_map/ppermute | solution.py:255
  57.6 2.7 %collective-permute-start.13 = (bf16[512,512]{1,0:T(8,128)(2,1)S(1)}, bf16[512,512]{1,0:T(8,128)(2,1)S(1)}, u32[]{:S(2)}, u32[]{:S(2)}) collective-permute-start(bf16[512,512]{1,0:T(8,128)(2,1)S(1)} %collective-permute-done.11.refs_0_.refs_6_), channel_id=1, source_target_pairs={{0,4},{1,29},{2,6},{3,31},{4,8},{5,1},{6,10},{7,3},{8,12},{9,5},{1... | collective-permute-start | bytes 1572872 | tf_op jit(solution)/shard_map/ppermute | solution.py:249
  60.3 2.7 %collective-permute-start.18 = (bf16[512,1024]{1,0:T(8,128)(2,1)S(1)}, bf16[512,1024]{1,0:T(8,128)(2,1)S(1)}, u32[]{:S(2)}, u32[]{:S(2)}) collective-permute-start(bf16[512,1024]{1,0:T(8,128)(2,1)S(1)} %collective-permute-done.14.refs_2_), channel_id=1, source_target_pairs={{0,32},{1,97},{32,64},{33,1},{64,96},{65,33},{96,0},{97,65},{128,1... | collective-permute-start | bytes 3145736 | tf_op jit(solution)/shard_map/ppermute | solution.py:258
  64.6 5.2 %collective-permute-done.6.refs_3_.refs_12_ = bf16[512,512]{1,0:T(8,128)(2,1)S(1)} collective-permute-done((bf16[512,512]{1,0:T(8,128)(2,1)S(1)}, bf16[512,512]{1,0:T(8,128)(2,1)S(1)}, u32[]{:S(2)}, u32[]{:S(2)}) %collective-permute-start.6) | collective-permute-done | bytes 524320 | tf_op jit(solution)/shard_map/ppermute | solution.py:255
  75.1 3.3 %collective-permute-start.20 = (bf16[2048,1024]{1,0:T(8,128)(2,1)S(1)}, bf16[2048,1024]{1,0:T(8,128)(2,1)S(1)}, u32[]{:S(2)}, u32[]{:S(2)}) collective-permute-start(bf16[2048,1024]{1,0:T(8,128)(2,1)S(1)} %shard_map.166.refs_16_), channel_id=1, source_target_pairs={{0,1},{1,0},{2,3},{3,2},{4,5},{5,4},{6,7},{7,6},{8,9},{9,8},{10,11... | collective-permute-start | bytes 12582920 | tf_op jit(solution)/shard_map/ppermute | solution.py:264
  80.2 4.6 %collective-permute-done.15.refs_2_.refs_15_ = bf16[512,512]{1,0:T(8,128)(2,1)S(1)} collective-permute-done((bf16[512,512]{1,0:T(8,128)(2,1)S(1)}, bf16[512,512]{1,0:T(8,128)(2,1)S(1)}, u32[]{:S(2)}, u32[]{:S(2)}) %collective-permute-start.15) | collective-permute-done | bytes 524320 | tf_op jit(solution)/shard_map/ppermute | solution.py:255
  87.0 2.8 %collective-permute-start.19 = (f32[16,128,128]{2,1,0:T(8,128)S(1)}, f32[16,128,128]{2,1,0:T(8,128)S(1)}, u32[]{:S(2)}, u32[]{:S(2)}) collective-permute-start(f32[16,128,128]{2,1,0:T(8,128)S(1)} %shard_map.164), channel_id=1, source_target_pairs={{0,1},{1,0},{2,3},{3,2},{4,5},{5,4},{6,7},{7,6},{8,9},{9,8},{10,11... | collective-permute-start | bytes 3145736 | tf_op jit(solution)/shard_map/ppermute | solution.py:264
  89.8 2.3 %collective-permute-done.19.other = f32[16,128,128]{2,1,0:T(8,128)S(1)} collective-permute-done((f32[16,128,128]{2,1,0:T(8,128)S(1)}, f32[16,128,128]{2,1,0:T(8,128)S(1)}, u32[]{:S(2)}, u32[]{:S(2)}) %collective-permute-start.19) | collective-permute-done | bytes 1048608 | tf_op jit(solution)/shard_map/ppermute | solution.py:264
  94.3 2.9 %collective-permute-start.21 = (bf16[1040,128]{1,0:T(8,128)(2,1)S(1)}, bf16[1040,128]{1,0:T(8,128)(2,1)S(1)}, u32[]{:S(2)}, u32[]{:S(2)}) collective-permute-start(bf16[1040,128]{1,0:T(8,128)(2,1)S(1)} %get-tuple-element.85), channel_id=1, source_target_pairs={{0,192},{32,224},{64,128},{96,160},{128,64},{160,96},{192,0},{224,... | collective-permute-start | bytes 798728 | tf_op jit(solution)/shard_map/ppermute | solution.py:261
  101.1 2.8 %collective-permute-start.24 = (bf16[1040,128]{1,0:T(8,128)(2,1)S(1)}, bf16[1040,128]{1,0:T(8,128)(2,1)S(1)}, u32[]{:S(2)}, u32[]{:S(2)}) collective-permute-start(bf16[1040,128]{1,0:T(8,128)(2,1)S(1)} %get-tuple-element.95), channel_id=1, source_target_pairs={{0,224},{32,128},{64,160},{96,192},{128,96},{160,0},{192,32},{224,... | collective-permute-start | bytes 798728 | tf_op jit(solution)/shard_map/ppermute | solution.py:261
  106.1 5.1 %collective-permute-done.22.refs_1_ = bf16[1040,128]{1,0:T(8,128)(2,1)S(1)} collective-permute-done((bf16[1040,128]{1,0:T(8,128)(2,1)S(1)}, bf16[1040,128]{1,0:T(8,128)(2,1)S(1)}, u32[]{:S(2)}, u32[]{:S(2)}) %collective-permute-start.22) | collective-permute-done | bytes 266272 | tf_op jit(solution)/shard_map/ppermute | solution.py:261
  111.2 5.9 %shard_map.169 = bf16[512,512]{1,0:T(8,128)(2,1)} custom-call(s32[194]{0:T(256)S(1)} %concatenate.3.table, bf16[512,512]{1,0:T(8,128)(2,1)S(1)} %copy-done.2, bf16[512,512]{1,0:T(8,128)(2,1)S(1)} %collective-permute-done.1.refs_1_, bf16[512,512]{1,0:T(8,128)(2,1)S(1)} %collective-permute-done.refs_2_, ...), custom_call_target="tpu_custom_call" | custom-call | flops 4294967296 | bytes 25165824 | tf_op jit(solution)/shard_map/pallas_call | solution.py:207
  117.2 5.8 %collective-permute-done.25.refs_3_ = bf16[1040,128]{1,0:T(8,128)(2,1)S(1)} collective-permute-done((bf16[1040,128]{1,0:T(8,128)(2,1)S(1)}, bf16[1040,128]{1,0:T(8,128)(2,1)S(1)}, u32[]{:S(2)}, u32[]{:S(2)}) %collective-permute-start.25) | collective-permute-done | bytes 266272 | tf_op jit(solution)/shard_map/ppermute | solution.py:261
  (67 shorter events, 39.0 us)
Async XLA Ops:
  0.6 15.0 %collective-permute-start = (bf16[512,512]{1,0:T(8,128)(2,1)}, bf16[512,512]{1,0:T(8,128)(2,1)S(1)}, u32[]{:S(2)}, u32[]{:S(2)}) collective-permute-start(bf16[512,512]{1,0:T(8,128)(2,1)} %refs_0_.3), channel_id=1, source_target_pairs={{0,28},{1,5},{2,30},{3,7},{4,0},{5,9},{6,2},{7,11},{8,4},{9,13},{1... | collective-permute-start | bytes 1572872 | tf_op jit(solution)/shard_map/ppermute | solution.py:252
  3.2 15.0 %collective-permute-start.1 = (bf16[512,512]{1,0:T(8,128)(2,1)}, bf16[512,512]{1,0:T(8,128)(2,1)S(1)}, u32[]{:S(2)}, u32[]{:S(2)}) collective-permute-start(bf16[512,512]{1,0:T(8,128)(2,1)} %refs_0_.3), channel_id=1, source_target_pairs={{0,4},{1,29},{2,6},{3,31},{4,8},{5,1},{6,10},{7,3},{8,12},{9,5},{1... | collective-permute-start | bytes 1572872 | tf_op jit(solution)/shard_map/ppermute | solution.py:249
  7.3 12.8 %collective-permute-start.2 = (bf16[256,1024]{1,0:T(8,128)(2,1)S(1)}, bf16[256,1024]{1,0:T(8,128)(2,1)}, u32[]{:S(2)}, u32[]{:S(2)}) collective-permute-start(bf16[256,1024]{1,0:T(8,128)(2,1)S(1)} %constant_dynamic-slice_fusion.refs_0_), channel_id=1, source_target_pairs={{0,128},{32,160},{64,192},{96,224},{128,0},{160,32},{192,64},{224,... | collective-permute-start | bytes 1572872 | tf_op jit(solution)/shard_map/ppermute | solution.py:261
  20.0 13.4 %collective-permute-start.3 = (bf16[512,512]{1,0:T(8,128)(2,1)}, bf16[512,512]{1,0:T(8,128)(2,1)S(1)}, u32[]{:S(2)}, u32[]{:S(2)}) collective-permute-start(bf16[512,512]{1,0:T(8,128)(2,1)} %refs_0_.3), channel_id=1, source_target_pairs={{0,2},{2,0},{4,6},{6,4},{8,10},{10,8},{12,14},{14,12},{16,18},{18,... | collective-permute-start | bytes 1572872 | tf_op jit(solution)/shard_map/ppermute | solution.py:255
  22.8 13.2 %collective-permute-start.5 = (bf16[512,512]{1,0:T(8,128)(2,1)S(1)}, bf16[512,512]{1,0:T(8,128)(2,1)S(1)}, u32[]{:S(2)}, u32[]{:S(2)}) collective-permute-start(bf16[512,512]{1,0:T(8,128)(2,1)S(1)} %collective-permute-done.1.refs_1_), channel_id=1, source_target_pairs={{0,4},{1,29},{2,6},{3,31},{4,8},{5,1},{6,10},{7,3},{8,12},{9,5},{1... | collective-permute-start | bytes 1572872 | tf_op jit(solution)/shard_map/ppermute | solution.py:249
  26.6 15.7 %collective-permute-start.12 = (bf16[512,1024]{1,0:T(8,128)(2,1)S(1)}, bf16[512,1024]{1,0:T(8,128)(2,1)S(1)}, u32[]{:S(2)}, u32[]{:S(2)}) collective-permute-start(bf16[512,1024]{1,0:T(8,128)(2,1)S(1)} %shard_map.159.refs_0_), channel_id=1, source_target_pairs={{0,32},{1,97},{32,64},{33,1},{64,96},{65,33},{96,0},{97,65},{128,1... | collective-permute-start | bytes 3145736 | tf_op jit(solution)/shard_map/ppermute | solution.py:258
  36.0 21.6 %collective-permute-start.11 = (bf16[512,512]{1,0:T(8,128)(2,1)S(1)}, bf16[512,512]{1,0:T(8,128)(2,1)S(1)}, u32[]{:S(2)}, u32[]{:S(2)}) collective-permute-start(bf16[512,512]{1,0:T(8,128)(2,1)S(1)} %collective-permute-done.5.refs_0_.refs_3_), channel_id=1, source_target_pairs={{0,4},{1,29},{2,6},{3,31},{4,8},{5,1},{6,10},{7,3},{8,12},{9,5},{1... | collective-permute-start | bytes 1572872 | tf_op jit(solution)/shard_map/ppermute | solution.py:249
  39.4 18.2 %collective-permute-start.8 = (bf16[512,512]{1,0:T(8,128)(2,1)S(1)}, bf16[512,512]{1,0:T(8,128)(2,1)S(1)}, u32[]{:S(2)}, u32[]{:S(2)}) collective-permute-start(bf16[512,512]{1,0:T(8,128)(2,1)S(1)} %collective-permute-done.5.refs_0_.refs_3_), channel_id=1, source_target_pairs={{0,2},{2,0},{4,6},{6,4},{8,10},{10,8},{12,14},{14,12},{16,18},{18,... | collective-permute-start | bytes 1572872 | tf_op jit(solution)/shard_map/ppermute | solution.py:255
  39.6 15.1 %collective-permute-start.10 = (bf16[512,512]{1,0:T(8,128)(2,1)S(1)}, bf16[512,512]{1,0:T(8,128)(2,1)S(1)}, u32[]{:S(2)}, u32[]{:S(2)}) collective-permute-start(bf16[512,512]{1,0:T(8,128)(2,1)S(1)} %collective-permute-done.4.refs_1_.refs_4_), channel_id=1, source_target_pairs={{0,28},{1,5},{2,30},{3,7},{4,0},{5,9},{6,2},{7,11},{8,4},{9,13},{1... | collective-permute-start | bytes 1572872 | tf_op jit(solution)/shard_map/ppermute | solution.py:252
  39.6 18.0 %collective-permute-start.9 = (bf16[512,512]{1,0:T(8,128)(2,1)S(1)}, bf16[512,512]{1,0:T(8,128)(2,1)S(1)}, u32[]{:S(2)}, u32[]{:S(2)}) collective-permute-start(bf16[512,512]{1,0:T(8,128)(2,1)S(1)} %collective-permute-done.3.refs_2_.refs_5_), channel_id=1, source_target_pairs={{0,4},{1,29},{2,6},{3,31},{4,8},{5,1},{6,10},{7,3},{8,12},{9,5},{1... | collective-permute-start | bytes 1572872 | tf_op jit(solution)/shard_map/ppermute | solution.py:249
  42.3 18.1 %collective-permute-start.14 = (bf16[512,1024]{1,0:T(8,128)(2,1)S(1)}, bf16[512,1024]{1,0:T(8,128)(2,1)S(1)}, u32[]{:S(2)}, u32[]{:S(2)}) collective-permute-start(bf16[512,1024]{1,0:T(8,128)(2,1)S(1)} %collective-permute-done.12.refs_1_), channel_id=1, source_target_pairs={{0,32},{1,97},{32,64},{33,1},{64,96},{65,33},{96,0},{97,65},{128,1... | collective-permute-start | bytes 3145736 | tf_op jit(solution)/shard_map/ppermute | solution.py:258
  54.7 15.0 %collective-permute-start.6 = (bf16[512,512]{1,0:T(8,128)(2,1)S(1)}, bf16[512,512]{1,0:T(8,128)(2,1)S(1)}, u32[]{:S(2)}, u32[]{:S(2)}) collective-permute-start(bf16[512,512]{1,0:T(8,128)(2,1)S(1)} %collective-permute-done.4.refs_1_.refs_4_), channel_id=1, source_target_pairs={{0,2},{2,0},{4,6},{6,4},{8,10},{10,8},{12,14},{14,12},{16,18},{18,... | collective-permute-start | bytes 1572872 | tf_op jit(solution)/shard_map/ppermute | solution.py:255
  57.6 12.2 %collective-permute-start.7 = (bf16[512,512]{1,0:T(8,128)(2,1)S(1)}, bf16[512,512]{1,0:T(8,128)(2,1)S(1)}, u32[]{:S(2)}, u32[]{:S(2)}) collective-permute-start(bf16[512,512]{1,0:T(8,128)(2,1)S(1)} %collective-permute-done.3.refs_2_.refs_5_), channel_id=1, source_target_pairs={{0,28},{1,5},{2,30},{3,7},{4,0},{5,9},{6,2},{7,11},{8,4},{9,13},{1... | collective-permute-start | bytes 1572872 | tf_op jit(solution)/shard_map/ppermute | solution.py:252
  57.6 14.1 %collective-permute-start.13 = (bf16[512,512]{1,0:T(8,128)(2,1)S(1)}, bf16[512,512]{1,0:T(8,128)(2,1)S(1)}, u32[]{:S(2)}, u32[]{:S(2)}) collective-permute-start(bf16[512,512]{1,0:T(8,128)(2,1)S(1)} %collective-permute-done.11.refs_0_.refs_6_), channel_id=1, source_target_pairs={{0,4},{1,29},{2,6},{3,31},{4,8},{5,1},{6,10},{7,3},{8,12},{9,5},{1... | collective-permute-start | bytes 1572872 | tf_op jit(solution)/shard_map/ppermute | solution.py:249
  60.2 20.0 %collective-permute-start.17 = (bf16[512,512]{1,0:T(8,128)(2,1)S(1)}, bf16[512,512]{1,0:T(8,128)(2,1)S(1)}, u32[]{:S(2)}, u32[]{:S(2)}) collective-permute-start(bf16[512,512]{1,0:T(8,128)(2,1)S(1)} %collective-permute-done.8.refs_2_.refs_8_), channel_id=1, source_target_pairs={{0,4},{1,29},{2,6},{3,31},{4,8},{5,1},{6,10},{7,3},{8,12},{9,5},{1... | collective-permute-start | bytes 1572872 | tf_op jit(solution)/shard_map/ppermute | solution.py:249
  60.3 14.5 %collective-permute-start.18 = (bf16[512,1024]{1,0:T(8,128)(2,1)S(1)}, bf16[512,1024]{1,0:T(8,128)(2,1)S(1)}, u32[]{:S(2)}, u32[]{:S(2)}) collective-permute-start(bf16[512,1024]{1,0:T(8,128)(2,1)S(1)} %collective-permute-done.14.refs_2_), channel_id=1, source_target_pairs={{0,32},{1,97},{32,64},{33,1},{64,96},{65,33},{96,0},{97,65},{128,1... | collective-permute-start | bytes 3145736 | tf_op jit(solution)/shard_map/ppermute | solution.py:258
  71.7 13.1 %collective-permute-start.15 = (bf16[512,512]{1,0:T(8,128)(2,1)S(1)}, bf16[512,512]{1,0:T(8,128)(2,1)S(1)}, u32[]{:S(2)}, u32[]{:S(2)}) collective-permute-start(bf16[512,512]{1,0:T(8,128)(2,1)S(1)} %collective-permute-done.13.refs_0_.refs_9_), channel_id=1, source_target_pairs={{0,2},{2,0},{4,6},{6,4},{8,10},{10,8},{12,14},{14,12},{16,18},{18,... | collective-permute-start | bytes 1572872 | tf_op jit(solution)/shard_map/ppermute | solution.py:255
  75.1 17.9 %collective-permute-start.20 = (bf16[2048,1024]{1,0:T(8,128)(2,1)S(1)}, bf16[2048,1024]{1,0:T(8,128)(2,1)S(1)}, u32[]{:S(2)}, u32[]{:S(2)}) collective-permute-start(bf16[2048,1024]{1,0:T(8,128)(2,1)S(1)} %shard_map.166.refs_16_), channel_id=1, source_target_pairs={{0,1},{1,0},{2,3},{3,2},{4,5},{5,4},{6,7},{7,6},{8,9},{9,8},{10,11... | collective-permute-start | bytes 12582920 | tf_op jit(solution)/shard_map/ppermute | solution.py:264
  97.2 14.0 %collective-permute-start.22 = (bf16[1040,128]{1,0:T(8,128)(2,1)S(1)}, bf16[1040,128]{1,0:T(8,128)(2,1)S(1)}, u32[]{:S(2)}, u32[]{:S(2)}) collective-permute-start(bf16[1040,128]{1,0:T(8,128)(2,1)S(1)} %get-tuple-element.86), channel_id=1, source_target_pairs={{0,160},{32,192},{64,224},{96,128},{128,32},{160,64},{192,96},{224... | collective-permute-start | bytes 798728 | tf_op jit(solution)/shard_map/ppermute | solution.py:261
  101.1 16.2 %collective-permute-start.24 = (bf16[1040,128]{1,0:T(8,128)(2,1)S(1)}, bf16[1040,128]{1,0:T(8,128)(2,1)S(1)}, u32[]{:S(2)}, u32[]{:S(2)}) collective-permute-start(bf16[1040,128]{1,0:T(8,128)(2,1)S(1)} %get-tuple-element.95), channel_id=1, source_target_pairs={{0,224},{32,128},{64,160},{96,192},{128,96},{160,0},{192,32},{224,... | collective-permute-start | bytes 798728 | tf_op jit(solution)/shard_map/ppermute | solution.py:261
  103.9 19.2 %collective-permute-start.25 = (bf16[1040,128]{1,0:T(8,128)(2,1)S(1)}, bf16[1040,128]{1,0:T(8,128)(2,1)S(1)}, u32[]{:S(2)}, u32[]{:S(2)}) collective-permute-start(bf16[1040,128]{1,0:T(8,128)(2,1)S(1)} %get-tuple-element.96), channel_id=1, source_target_pairs={{0,128},{32,160},{64,192},{96,224},{128,0},{160,32},{192,64},{224,... | collective-permute-start | bytes 798728 | tf_op jit(solution)/shard_map/ppermute | solution.py:261
  105.0 18.9 %collective-permute-start.26 = (bf16[1040,128]{1,0:T(8,128)(2,1)S(1)}, bf16[1040,128]{1,0:T(8,128)(2,1)S(1)}, u32[]{:S(2)}, u32[]{:S(2)}) collective-permute-start(bf16[1040,128]{1,0:T(8,128)(2,1)S(1)} %get-tuple-element.97), channel_id=1, source_target_pairs={{0,64},{32,96},{64,0},{96,32},{128,192},{160,224},{192,128},{224,1... | collective-permute-start | bytes 798728 | tf_op jit(solution)/shard_map/ppermute | solution.py:261
  105.4 18.5 %collective-permute-start.27 = (bf16[1040,128]{1,0:T(8,128)(2,1)S(1)}, bf16[1040,128]{1,0:T(8,128)(2,1)S(1)}, u32[]{:S(2)}, u32[]{:S(2)}) collective-permute-start(bf16[1040,128]{1,0:T(8,128)(2,1)S(1)} %get-tuple-element.98), channel_id=1, source_target_pairs={{0,32},{32,64},{64,96},{96,0},{128,160},{160,192},{192,224},{224,1... | collective-permute-start | bytes 798728 | tf_op jit(solution)/shard_map/ppermute | solution.py:261
  111.2 12.8 %collective-permute-start.28 = (bf16[1040,128]{1,0:T(8,128)(2,1)S(1)}, bf16[1040,128]{1,0:T(8,128)(2,1)S(1)}, u32[]{:S(2)}, u32[]{:S(2)}) collective-permute-start(bf16[1040,128]{1,0:T(8,128)(2,1)S(1)} %get-tuple-element.99), channel_id=1, source_target_pairs={{0,96},{32,0},{64,32},{96,64},{128,224},{160,128},{192,160},{224,1... | collective-permute-start | bytes 798728 | tf_op jit(solution)/shard_map/ppermute | solution.py:261
  (8 other events, 70.6 us)

commit v5 on v4

--- a/solution.py
+++ b/solution.py
@@ -19,8 +19,9 @@
 COLS = ((0, 0), (-1, 0), (1, 0), (-2, 0), (2, 0), (0, 1), (-3, 0), (3, 0), (-2, 1),
         (-4, 0), (-1, 1), (1, 1), (2, 1), (-3, 1), (3, 1), (-4, 1))
 LAST = 13
-DESTS = ((1, 2), (1, 1), (1, 3), (1, 0), (0, 2), (0, 1), (0, 3), (0, 0))
-EARLY = 2
+DESTS = ((1, 2), (1, 1), (1, 3), (0, 1), (0, 3), (1, 0), (0, 2), (0, 0))
+EARLY = 3
+DENSE_MIB = PICK_MIB = CODE_MIB = GRAD_MIB = 10
 PHASE_FLOPS = 30 * 10 ** 9
 DENSE_MIB = PICK_MIB = CODE_MIB = GRAD_MIB = 10
 COL_AT, ROW_AT, SIDE_AT, MINE_AT, THEIRS_AT, SLOT_AT = 0, 16, 48, 50, 58, 66
@@ -107,6 +108,32 @@
         cost_estimate=pl.CostEstimate(
             flops=0, bytes_accessed=chunks * CAP * BLK * BLK * 8, transcendentals=0),
     )(table, total)
+
+
+def encode(held, most, out):
+    level = jnp.ceil(jnp.log2(jnp.maximum(most, 1e-30)))
+    scale = jnp.exp2(TOP - level)
+    for t in range(CAP):
+        v = held[t] * scale
+        v2 = v * v
+        v4 = v2 * v2
+        out[t * BLK:(t + 1) * BLK, :] = (v4 * v4 * v).astype(BF16)
+    out[CAP * BLK:, :] = jnp.broadcast_to(level, (TAIL, BLK)).astype(BF16)
+
+
+def scale_of(ref):
+    return ref[CAP * BLK:CAP * BLK + TAIL, :].astype(F32)[0:1, :] - TOP
+
+
+def decode(ref, t, scale):
+    y = ref[t * BLK:(t + 1) * BLK, :].astype(F32)
+    size = jnp.exp2(jnp.log2(jnp.maximum(jnp.abs(y), 1e-37)) * (1.0 / POWER) + scale)
+    size = jnp.where(jnp.abs(y) > 1e-37, size, 0.0)
+    return jnp.where(y < 0, -size, size)
+
+
+def largest(most, tile):
+    return jnp.maximum(most, jnp.max(jnp.abs(tile), axis=0, keepdims=True))
 
 
 def code_kernel(at, coded, plain, table, total, other, *refs):
@@ -122,16 +149,9 @@
                 outs[m][t] = both
             else:
                 held[t] = both
-                most = jnp.maximum(most, jnp.max(jnp.abs(both), axis=0, keepdims=True))
+                most = largest(most, both)
         if m < coded:
-            level = jnp.ceil(jnp.log2(jnp.maximum(most, 1e-30)))
-            scale = jnp.exp2(TOP - level)
-            for t in range(CAP):
-                v = held[t] * scale
-                v2 = v * v
-                v4 = v2 * v2
-                outs[m][t * BLK:(t + 1) * BLK, :] = (v4 * v4 * v).astype(BF16)
-            outs[m][CAP * BLK:, :] = jnp.broadcast_to(level, (TAIL, BLK)).astype(BF16)
+            encode(held, most, outs[m])
 
 
 def code(table, first, last, total, other, plain):
@@ -151,19 +171,46 @@
     )(table, total, other)
 
 
+def relay_kernel(counts, *refs):
+    outs, held = refs[-1 - len(counts):-1], refs[-1]
+    at = 0
+    for m, count in enumerate(counts):
+        before, arrived = refs[at], refs[at + 1:at + 1 + count]
+        at += 1 + count
+        scales = [scale_of(ref) for ref in arrived]
+        most = jnp.zeros((1, BLK), F32)
+        for t in range(CAP):
+            acc = before[t]
+            for ref, scale in zip(arrived, scales):
+                acc = acc + decode(ref, t, scale)
+            held[t] = acc
+            most = largest(most, acc)
+        encode(held, most, outs[m])
+
+
+def relay(groups):
+    counts = tuple(len(arrived) for _, arrived in groups)
+    args = [v for before, arrived in groups for v in (before, *arrived)]
+    return pl.pallas_call(
+        functools.partial(relay_kernel, counts),
+        out_shape=[jax.ShapeDtypeStruct((CAP * BLK + TAIL, BLK), BF16)] * len(counts),
+        in_specs=[vmem_spec()] * len(args),
+        out_specs=[vmem_spec()] * len(counts),
+        scratch_shapes=[pltpu.VMEM((CAP, BLK, BLK), F32)],
+        compiler_params=params(CODE_MIB),
+        cost_estimate=pl.CostEstimate(
+            flops=len(args) * CAP * BLK * BLK * 8, bytes_accessed=len(args) * CAP * BLK * BLK * 4,
+            transcendentals=0),
+    )(*args)
+
+
 def sum_kernel(before, *refs):
     arrived, out = refs[:-1], refs[-1]
-    scales = []
-    for ref in arrived:
-        level = ref[CAP * BLK:CAP * BLK + TAIL, :].astype(F32)[0:1, :]
-        scales.append(level - TOP)
+    scales = [scale_of(ref) for ref in arrived]
     for t in range(CAP):
         acc = before[t]
         for ref, scale in zip(arrived, scales):
-            y = ref[t * BLK:(t + 1) * BLK, :].astype(F32)
-            size = jnp.exp2(jnp.log2(jnp.maximum(jnp.abs(y), 1e-37)) * (1.0 / POWER) + scale)
-            size = jnp.where(jnp.abs(y) > 1e-37, size, 0.0)
-            acc = acc + jnp.where(y < 0, -size, size)
+            acc = acc + decode(ref, t, scale)
         out[t] = acc
 
 
@@ -321,19 +368,25 @@
     total = dense(total, table, xt, [of3, or3, of4], LAST)
     cols = [grad_out, f1, r1, f2, r2, o0, f3, r3, of2, f4, of1, or1, or2, of3, or3, of4]
 
-    other_early = to_core(pick(table, 0, EARLY, total))
-    early = code(table, 0, EARLY, total, other_early, 0)
-    *early, theirs, late_table = together((*early, theirs, table))
+    theirs, early_table = together((theirs, table))
+    other_early = to_core(pick(early_table, 0, EARLY, total))
+    early = code(early_table, 0, EARLY, total, other_early, 0)
+    *early, late_table = together((*early, table))
     other_late = to_core(pick(late_table, EARLY, 8, total))
     parts = [mine, theirs]
-    late = code(late_table, EARLY, 8, total, other_late, 1)
-    coded = list(early) + list(late[:-1])
-    arrived = [to_row(v, dx, dy) for v, (dx, dy) in zip(coded, DESTS)]
-    own, grad_table = together((late[-1], late_table))
+    late = code(late_table, EARLY, 8, total, other_late, 3)
+    next_y, last_y, beside, opposite, own = late
+
+    cross = to_row(early[0], 1, 0)
+    ups, downs = to_row(early[1], 0, 1), to_row(early[2], 0, 3)
+    near = [to_row(next_y, 0, 1), to_row(last_y, 0, 3)]
+    beside, opposite = relay([(beside, [ups, downs]), (opposite, [cross])])
+    pushed = add_coded(own, near)
+    far = [to_row(beside, 1, 0), to_row(opposite, 0, 2)]
+    pushed, grad_table = together((pushed, late_table))
     grad_in = grad_sum(grad_table, range(16), cols, parts)
-    first, second, grad_in = together((arrived[0], arrived[1], grad_in))
-    pushed = add_coded(own, [first, second, arrived[2], arrived[3]])
-    pushed = add_coded(pushed, arrived[4:])
+    pushed, grad_in = together((pushed, grad_in))
+    pushed = add_coded(pushed, far)
     return grad_in, pushed.reshape(1, CAP, BLK, BLK)
 
 

time: 126 us -> 125 us (level)
  the two profiles are of different devices: /device:TPU:1 before, /device:TPU:126 now
where the time goes in v5:
time: 125 us
  waiting for transfers between devices  62.4 us (50%)
  starting transfers between devices  32.4 us (26%)
  Pallas kernels  21.4 us (17%)
  other arithmetic  4.67 us (4%)
  local copies, waits for them, and re-layouts  3.23 us (3%)
    ppermute x4, waiting for transfers between devices, across(): return lax.ppermute(v, 'col', X_SWAP)  24.5 us
    ppermute x6, starting transfers between devices, ahead(): return lax.ppermute(v, ('col', 'srv'), z_shift(1))  14.7 us
    ppermute x8, waiting for transfers between devices, to_row(): return lax.ppermute(v, 'row', row_shift(dx, dy))  13.1 us
    ppermute x5, waiting for transfers between devices, back(): return lax.ppermute(v, ('col', 'srv'), z_shift(-1))  12.2 us
    pallas_call x5, Pallas kernels, dense(): pl.pallas_call(functools.partial(dense_kernel, count, place, first), out_...  7.91 us
    ppermute x8, starting transfers between devices, to_row(): return lax.ppermute(v, 'row', row_shift(dx, dy))  7.35 us
    ppermute x4, starting transfers between devices, across(): return lax.ppermute(v, 'col', X_SWAP)  7.06 us
    pallas_call x1, Pallas kernels, grad_sum(): pl.pallas_call(functools.partial(grad_kernel, tuple(ids)), out_shape=jax....  5.9 us
  transfers between devices with their start and end apart: 29, of which 17 were waited for; matrix products, arithmetic and copies ran while one was open for 5% of the time, Pallas kernels for 14%

profile of v5, /device:TPU:126, one launch (start us, length us, event | category | flops | bytes accessed | tf_op | source)
XLA Modules:
  0.0 124.9 jit_solution(3066914418126866109)
XLA Ops:
  0.8 3.1 %collective-permute-start.2 = (bf16[512,512]{1,0:T(8,128)(2,1)}, bf16[512,512]{1,0:T(8,128)(2,1)S(1)}, u32[]{:S(2)}, u32[]{:S(2)}) collective-permute-start(bf16[512,512]{1,0:T(8,128)(2,1)} %refs_0_.3), channel_id=1, source_target_pairs={{0,4},{1,29},{2,6},{3,31},{4,8},{5,1},{6,10},{7,3},{8,12},{9,5},{1... | collective-permute-start | bytes 1572872 | tf_op jit(solution)/shard_map/ppermute | solution.py:296
  8.0 2.0 %copy.22 = bf16[512,512]{0,1:T(8,128)(2,1)} copy(bf16[512,512]{1,0:T(8,128)(2,1)} %param.15) | data formatting | bytes 1048576 | tf_op args[0]
  11.8 3.4 %collective-permute-done.1.refs_2_ = bf16[512,512]{1,0:T(8,128)(2,1)S(1)} collective-permute-done((bf16[512,512]{1,0:T(8,128)(2,1)}, bf16[512,512]{1,0:T(8,128)(2,1)S(1)}, u32[]{:S(2)}, u32[]{:S(2)}) %collective-permute-start.1) | collective-permute-done | bytes 524320 | tf_op jit(solution)/shard_map/ppermute | solution.py:299
  15.4 2.1 %collective-permute-done.refs_1_ = bf16[256,1024]{1,0:T(8,128)(2,1)} collective-permute-done((bf16[256,1024]{1,0:T(8,128)(2,1)S(1)}, bf16[256,1024]{1,0:T(8,128)(2,1)}, u32[]{:S(2)}, u32[]{:S(2)}) %collective-permute-start) | collective-permute-done | bytes 524320 | tf_op jit(solution)/shard_map/ppermute | solution.py:308
  18.9 3.2 %collective-permute-start.9 = (bf16[512,512]{1,0:T(8,128)(2,1)S(1)}, bf16[512,512]{1,0:T(8,128)(2,1)S(1)}, u32[]{:S(2)}, u32[]{:S(2)}) collective-permute-start(bf16[512,512]{1,0:T(8,128)(2,1)S(1)} %collective-permute-done.2.refs_1_), channel_id=1, source_target_pairs={{0,4},{1,29},{2,6},{3,31},{4,8},{5,1},{6,10},{7,3},{8,12},{9,5},{1... | collective-permute-start | bytes 1572872 | tf_op jit(solution)/shard_map/ppermute | solution.py:296
  26.1 6.2 %collective-permute-done.7.refs_2_.refs_5_ = bf16[512,512]{1,0:T(8,128)(2,1)S(1)} collective-permute-done((bf16[512,512]{1,0:T(8,128)(2,1)}, bf16[512,512]{1,0:T(8,128)(2,1)S(1)}, u32[]{:S(2)}, u32[]{:S(2)}) %collective-permute-start.7) | collective-permute-done | bytes 524320 | tf_op jit(solution)/shard_map/ppermute | solution.py:302
  33.8 2.1 %collective-permute-start.12 = (bf16[512,512]{1,0:T(8,128)(2,1)S(1)}, bf16[512,512]{1,0:T(8,128)(2,1)S(1)}, u32[]{:S(2)}, u32[]{:S(2)}) collective-permute-start(bf16[512,512]{1,0:T(8,128)(2,1)S(1)} %collective-permute-done.9.refs_0_.refs_3_), channel_id=1, source_target_pairs={{0,2},{2,0},{4,6},{6,4},{8,10},{10,8},{12,14},{14,12},{16,18},{18,... | collective-permute-start | bytes 1572872 | tf_op jit(solution)/shard_map/ppermute | solution.py:302
  35.9 2.6 %collective-permute-start.15 = (bf16[512,512]{1,0:T(8,128)(2,1)S(1)}, bf16[512,512]{1,0:T(8,128)(2,1)S(1)}, u32[]{:S(2)}, u32[]{:S(2)}) collective-permute-start(bf16[512,512]{1,0:T(8,128)(2,1)S(1)} %collective-permute-done.9.refs_0_.refs_3_), channel_id=1, source_target_pairs={{0,4},{1,29},{2,6},{3,31},{4,8},{5,1},{6,10},{7,3},{8,12},{9,5},{1... | collective-permute-start | bytes 1572872 | tf_op jit(solution)/shard_map/ppermute | solution.py:296
  38.5 2.0 %collective-permute-start.14 = (bf16[512,512]{1,0:T(8,128)(2,1)S(1)}, bf16[512,512]{1,0:T(8,128)(2,1)S(1)}, u32[]{:S(2)}, u32[]{:S(2)}) collective-permute-start(bf16[512,512]{1,0:T(8,128)(2,1)S(1)} %collective-permute-done.8.refs_1_.refs_4_), channel_id=1, source_target_pairs={{0,28},{1,5},{2,30},{3,7},{4,0},{5,9},{6,2},{7,11},{8,4},{9,13},{1... | collective-permute-start | bytes 1572872 | tf_op jit(solution)/shard_map/ppermute | solution.py:299
  42.2 7.8 %collective-permute-done.12.refs_2_.refs_8_ = bf16[512,512]{1,0:T(8,128)(2,1)S(1)} collective-permute-done((bf16[512,512]{1,0:T(8,128)(2,1)S(1)}, bf16[512,512]{1,0:T(8,128)(2,1)S(1)}, u32[]{:S(2)}, u32[]{:S(2)}) %collective-permute-start.12) | collective-permute-done | bytes 524320 | tf_op jit(solution)/shard_map/ppermute | solution.py:302
  50.1 2.1 %collective-permute-start.10 = (bf16[512,512]{1,0:T(8,128)(2,1)S(1)}, bf16[512,512]{1,0:T(8,128)(2,1)S(1)}, u32[]{:S(2)}, u32[]{:S(2)}) collective-permute-start(bf16[512,512]{1,0:T(8,128)(2,1)S(1)} %collective-permute-done.8.refs_1_.refs_4_), channel_id=1, source_target_pairs={{0,2},{2,0},{4,6},{6,4},{8,10},{10,8},{12,14},{14,12},{16,18},{18,... | collective-permute-start | bytes 1572872 | tf_op jit(solution)/shard_map/ppermute | solution.py:302
  52.2 4.2 %collective-permute-done.13.refs_1_.refs_10_ = bf16[512,512]{1,0:T(8,128)(2,1)S(1)} collective-permute-done((bf16[512,512]{1,0:T(8,128)(2,1)S(1)}, bf16[512,512]{1,0:T(8,128)(2,1)S(1)}, u32[]{:S(2)}, u32[]{:S(2)}) %collective-permute-start.13) | collective-permute-done | bytes 524320 | tf_op jit(solution)/shard_map/ppermute | solution.py:296
  56.4 4.0 %collective-permute-start.16 = (bf16[512,512]{1,0:T(8,128)(2,1)S(1)}, bf16[512,512]{1,0:T(8,128)(2,1)S(1)}, u32[]{:S(2)}, u32[]{:S(2)}) collective-permute-start(bf16[512,512]{1,0:T(8,128)(2,1)S(1)} %collective-permute-done.15.refs_0_.refs_6_), channel_id=1, source_target_pairs={{0,4},{1,29},{2,6},{3,31},{4,8},{5,1},{6,10},{7,3},{8,12},{9,5},{1... | collective-permute-start | bytes 1572872 | tf_op jit(solution)/shard_map/ppermute | solution.py:296
  60.3 1.8 %collective-permute-start.19 = (bf16[512,512]{1,0:T(8,128)(2,1)S(1)}, bf16[512,512]{1,0:T(8,128)(2,1)S(1)}, u32[]{:S(2)}, u32[]{:S(2)}) collective-permute-start(bf16[512,512]{1,0:T(8,128)(2,1)S(1)} %collective-permute-done.12.refs_2_.refs_8_), channel_id=1, source_target_pairs={{0,4},{1,29},{2,6},{3,31},{4,8},{5,1},{6,10},{7,3},{8,12},{9,5},{1... | collective-permute-start | bytes 1572872 | tf_op jit(solution)/shard_map/ppermute | solution.py:296
  63.9 1.6 %collective-permute-done.10.refs_3_.refs_12_ = bf16[512,512]{1,0:T(8,128)(2,1)S(1)} collective-permute-done((bf16[512,512]{1,0:T(8,128)(2,1)S(1)}, bf16[512,512]{1,0:T(8,128)(2,1)S(1)}, u32[]{:S(2)}, u32[]{:S(2)}) %collective-permute-start.10) | collective-permute-done | bytes 524320 | tf_op jit(solution)/shard_map/ppermute | solution.py:302
  65.5 7.3 %collective-permute-done.11.refs_2_.refs_11_ = bf16[512,512]{1,0:T(8,128)(2,1)S(1)} collective-permute-done((bf16[512,512]{1,0:T(8,128)(2,1)S(1)}, bf16[512,512]{1,0:T(8,128)(2,1)S(1)}, u32[]{:S(2)}, u32[]{:S(2)}) %collective-permute-start.11) | collective-permute-done | bytes 524320 | tf_op jit(solution)/shard_map/ppermute | solution.py:299
  74.2 2.7 %collective-permute-done.5.refs_3_ = bf16[512,1024]{1,0:T(8,128)(2,1)S(1)} collective-permute-done((bf16[512,1024]{1,0:T(8,128)(2,1)S(1)}, bf16[512,1024]{1,0:T(8,128)(2,1)S(1)}, u32[]{:S(2)}, u32[]{:S(2)}) %collective-permute-start.5) | collective-permute-done | bytes 1048608 | tf_op jit(solution)/shard_map/ppermute | solution.py:305
  77.3 1.8 %shard_map.163.refs_3_ = f32[256,128,128]{2,1,0:T(8,128)S(1)} custom-call(s32[194]{0:T(256)S(1)} %concatenate.3.table, bf16[512,512]{1,0:T(8,128)(2,1)S(1)} %bitcast.30, bf16[512,512]{1,0:T(8,128)(2,1)S(1)} %collective-permute-done.16.refs_0_.refs_9_, bf16[512,512]{1,0:T(8,128)(2,1)S(1)} %collective-permute-done.13.refs_1_.refs_10_, ...), custom_call_target="tpu_custom_call", output_to_operand_aliasing={{}: (6, {})} | custom-call | flops 30000001024 | bytes 6291456 | tf_op jit(solution)/shard_map/pallas_call | solution.py:79
  79.1 8.8 %collective-permute-done.17.refs_2_.refs_15_ = bf16[512,512]{1,0:T(8,128)(2,1)S(1)} collective-permute-done((bf16[512,512]{1,0:T(8,128)(2,1)S(1)}, bf16[512,512]{1,0:T(8,128)(2,1)S(1)}, u32[]{:S(2)}, u32[]{:S(2)}) %collective-permute-start.17) | collective-permute-done | bytes 524320 | tf_op jit(solution)/shard_map/ppermute | solution.py:302
  90.2 3.4 %collective-permute-done.20.other = f32[24,128,128]{2,1,0:T(8,128)S(1)} collective-permute-done((f32[24,128,128]{2,1,0:T(8,128)S(1)}, f32[24,128,128]{2,1,0:T(8,128)S(1)}, u32[]{:S(2)}, u32[]{:S(2)}) %collective-permute-start.20) | collective-permute-done | bytes 1572896 | tf_op jit(solution)/shard_map/ppermute | solution.py:311
  98.2 2.2 %collective-permute-done.21.other = f32[40,128,128]{2,1,0:T(8,128)S(1)} collective-permute-done((f32[40,128,128]{2,1,0:T(8,128)S(1)}, f32[40,128,128]{2,1,0:T(8,128)S(1)}, u32[]{:S(2)}, u32[]{:S(2)}) %collective-permute-start.21) | collective-permute-done | bytes 2621472 | tf_op jit(solution)/shard_map/ppermute | solution.py:311
  108.6 1.9 %collective-permute-done.22.refs_0_ = bf16[1040,128]{1,0:T(8,128)(2,1)S(1)} collective-permute-done((bf16[1040,128]{1,0:T(8,128)(2,1)S(1)}, bf16[1040,128]{1,0:T(8,128)(2,1)S(1)}, u32[]{:S(2)}, u32[]{:S(2)}) %collective-permute-start.22) | collective-permute-done | bytes 266272 | tf_op jit(solution)/shard_map/ppermute | solution.py:308
  110.6 6.7 %collective-permute-done.23.refs_1_ = bf16[1040,128]{1,0:T(8,128)(2,1)S(1)} collective-permute-done((bf16[1040,128]{1,0:T(8,128)(2,1)S(1)}, bf16[1040,128]{1,0:T(8,128)(2,1)S(1)}, u32[]{:S(2)}, u32[]{:S(2)}) %collective-permute-start.23) | collective-permute-done | bytes 266272 | tf_op jit(solution)/shard_map/ppermute | solution.py:308
  117.8 5.9 %shard_map.170 = bf16[512,512]{1,0:T(8,128)(2,1)} custom-call(s32[194]{0:T(256)S(1)} %concatenate.3.table, bf16[512,512]{1,0:T(8,128)(2,1)S(1)} %copy-done.1, bf16[512,512]{1,0:T(8,128)(2,1)S(1)} %collective-permute-done.2.refs_1_, bf16[512,512]{1,0:T(8,128)(2,1)S(1)} %collective-permute-done.1.refs_2_, ...), custom_call_target="tpu_custom_call" | custom-call | flops 4294967296 | bytes 25165824 | tf_op jit(solution)/shard_map/pallas_call | solution.py:254
  (70 shorter events, 35.0 us)
Async XLA Ops:
  0.7 14.5 %collective-permute-start.1 = (bf16[512,512]{1,0:T(8,128)(2,1)}, bf16[512,512]{1,0:T(8,128)(2,1)S(1)}, u32[]{:S(2)}, u32[]{:S(2)}) collective-permute-start(bf16[512,512]{1,0:T(8,128)(2,1)} %refs_0_.3), channel_id=1, source_target_pairs={{0,28},{1,5},{2,30},{3,7},{4,0},{5,9},{6,2},{7,11},{8,4},{9,13},{1... | collective-permute-start | bytes 1572872 | tf_op jit(solution)/shard_map/ppermute | solution.py:299
  0.8 14.5 %collective-permute-start.2 = (bf16[512,512]{1,0:T(8,128)(2,1)}, bf16[512,512]{1,0:T(8,128)(2,1)S(1)}, u32[]{:S(2)}, u32[]{:S(2)}) collective-permute-start(bf16[512,512]{1,0:T(8,128)(2,1)} %refs_0_.3), channel_id=1, source_target_pairs={{0,4},{1,29},{2,6},{3,31},{4,8},{5,1},{6,10},{7,3},{8,12},{9,5},{1... | collective-permute-start | bytes 1572872 | tf_op jit(solution)/shard_map/ppermute | solution.py:296
  4.0 13.5 %collective-permute-start = (bf16[256,1024]{1,0:T(8,128)(2,1)S(1)}, bf16[256,1024]{1,0:T(8,128)(2,1)}, u32[]{:S(2)}, u32[]{:S(2)}) collective-permute-start(bf16[256,1024]{1,0:T(8,128)(2,1)S(1)} %constant_dynamic-slice_fusion.refs_0_), channel_id=1, source_target_pairs={{0,128},{32,160},{64,192},{96,224},{128,0},{160,32},{192,64},{224,... | collective-permute-start | bytes 1572872 | tf_op jit(solution)/shard_map/ppermute | solution.py:308
  17.5 14.8 %collective-permute-start.7 = (bf16[512,512]{1,0:T(8,128)(2,1)}, bf16[512,512]{1,0:T(8,128)(2,1)S(1)}, u32[]{:S(2)}, u32[]{:S(2)}) collective-permute-start(bf16[512,512]{1,0:T(8,128)(2,1)} %refs_0_.3), channel_id=1, source_target_pairs={{0,2},{2,0},{4,6},{6,4},{8,10},{10,8},{12,14},{14,12},{16,18},{18,... | collective-permute-start | bytes 1572872 | tf_op jit(solution)/shard_map/ppermute | solution.py:302
  18.9 14.9 %collective-permute-start.8 = (bf16[512,512]{1,0:T(8,128)(2,1)S(1)}, bf16[512,512]{1,0:T(8,128)(2,1)S(1)}, u32[]{:S(2)}, u32[]{:S(2)}) collective-permute-start(bf16[512,512]{1,0:T(8,128)(2,1)S(1)} %collective-permute-done.1.refs_2_), channel_id=1, source_target_pairs={{0,28},{1,5},{2,30},{3,7},{4,0},{5,9},{6,2},{7,11},{8,4},{9,13},{1... | collective-permute-start | bytes 1572872 | tf_op jit(solution)/shard_map/ppermute | solution.py:299
  18.9 14.9 %collective-permute-start.9 = (bf16[512,512]{1,0:T(8,128)(2,1)S(1)}, bf16[512,512]{1,0:T(8,128)(2,1)S(1)}, u32[]{:S(2)}, u32[]{:S(2)}) collective-permute-start(bf16[512,512]{1,0:T(8,128)(2,1)S(1)} %collective-permute-done.2.refs_1_), channel_id=1, source_target_pairs={{0,4},{1,29},{2,6},{3,31},{4,8},{5,1},{6,10},{7,3},{8,12},{9,5},{1... | collective-permute-start | bytes 1572872 | tf_op jit(solution)/shard_map/ppermute | solution.py:296
  23.2 17.2 %collective-permute-start.3 = (bf16[512,1024]{1,0:T(8,128)(2,1)S(1)}, bf16[512,1024]{1,0:T(8,128)(2,1)S(1)}, u32[]{:S(2)}, u32[]{:S(2)}) collective-permute-start(bf16[512,1024]{1,0:T(8,128)(2,1)S(1)} %shard_map.158.refs_0_), channel_id=1, source_target_pairs={{0,32},{1,97},{32,64},{33,1},{64,96},{65,33},{96,0},{97,65},{128,1... | collective-permute-start | bytes 3145736 | tf_op jit(solution)/shard_map/ppermute | solution.py:305
  33.8 16.3 %collective-permute-start.12 = (bf16[512,512]{1,0:T(8,128)(2,1)S(1)}, bf16[512,512]{1,0:T(8,128)(2,1)S(1)}, u32[]{:S(2)}, u32[]{:S(2)}) collective-permute-start(bf16[512,512]{1,0:T(8,128)(2,1)S(1)} %collective-permute-done.9.refs_0_.refs_3_), channel_id=1, source_target_pairs={{0,2},{2,0},{4,6},{6,4},{8,10},{10,8},{12,14},{14,12},{16,18},{18,... | collective-permute-start | bytes 1572872 | tf_op jit(solution)/shard_map/ppermute | solution.py:302
  35.9 20.5 %collective-permute-start.15 = (bf16[512,512]{1,0:T(8,128)(2,1)S(1)}, bf16[512,512]{1,0:T(8,128)(2,1)S(1)}, u32[]{:S(2)}, u32[]{:S(2)}) collective-permute-start(bf16[512,512]{1,0:T(8,128)(2,1)S(1)} %collective-permute-done.9.refs_0_.refs_3_), channel_id=1, source_target_pairs={{0,4},{1,29},{2,6},{3,31},{4,8},{5,1},{6,10},{7,3},{8,12},{9,5},{1... | collective-permute-start | bytes 1572872 | tf_op jit(solution)/shard_map/ppermute | solution.py:296
  38.4 17.9 %collective-permute-start.13 = (bf16[512,512]{1,0:T(8,128)(2,1)S(1)}, bf16[512,512]{1,0:T(8,128)(2,1)S(1)}, u32[]{:S(2)}, u32[]{:S(2)}) collective-permute-start(bf16[512,512]{1,0:T(8,128)(2,1)S(1)} %collective-permute-done.7.refs_2_.refs_5_), channel_id=1, source_target_pairs={{0,4},{1,29},{2,6},{3,31},{4,8},{5,1},{6,10},{7,3},{8,12},{9,5},{1... | collective-permute-start | bytes 1572872 | tf_op jit(solution)/shard_map/ppermute | solution.py:296
  38.5 17.9 %collective-permute-start.14 = (bf16[512,512]{1,0:T(8,128)(2,1)S(1)}, bf16[512,512]{1,0:T(8,128)(2,1)S(1)}, u32[]{:S(2)}, u32[]{:S(2)}) collective-permute-start(bf16[512,512]{1,0:T(8,128)(2,1)S(1)} %collective-permute-done.8.refs_1_.refs_4_), channel_id=1, source_target_pairs={{0,28},{1,5},{2,30},{3,7},{4,0},{5,9},{6,2},{7,11},{8,4},{9,13},{1... | collective-permute-start | bytes 1572872 | tf_op jit(solution)/shard_map/ppermute | solution.py:299
  40.5 21.6 %collective-permute-start.4 = (bf16[512,1024]{1,0:T(8,128)(2,1)S(1)}, bf16[512,1024]{1,0:T(8,128)(2,1)S(1)}, u32[]{:S(2)}, u32[]{:S(2)}) collective-permute-start(bf16[512,1024]{1,0:T(8,128)(2,1)S(1)} %collective-permute-done.3.refs_1_), channel_id=1, source_target_pairs={{0,32},{1,97},{32,64},{33,1},{64,96},{65,33},{96,0},{97,65},{128,1... | collective-permute-start | bytes 3145736 | tf_op jit(solution)/shard_map/ppermute | solution.py:305
  50.1 15.4 %collective-permute-start.10 = (bf16[512,512]{1,0:T(8,128)(2,1)S(1)}, bf16[512,512]{1,0:T(8,128)(2,1)S(1)}, u32[]{:S(2)}, u32[]{:S(2)}) collective-permute-start(bf16[512,512]{1,0:T(8,128)(2,1)S(1)} %collective-permute-done.8.refs_1_.refs_4_), channel_id=1, source_target_pairs={{0,2},{2,0},{4,6},{6,4},{8,10},{10,8},{12,14},{14,12},{16,18},{18,... | collective-permute-start | bytes 1572872 | tf_op jit(solution)/shard_map/ppermute | solution.py:302
  56.4 16.5 %collective-permute-start.11 = (bf16[512,512]{1,0:T(8,128)(2,1)S(1)}, bf16[512,512]{1,0:T(8,128)(2,1)S(1)}, u32[]{:S(2)}, u32[]{:S(2)}) collective-permute-start(bf16[512,512]{1,0:T(8,128)(2,1)S(1)} %collective-permute-done.7.refs_2_.refs_5_), channel_id=1, source_target_pairs={{0,28},{1,5},{2,30},{3,7},{4,0},{5,9},{6,2},{7,11},{8,4},{9,13},{1... | collective-permute-start | bytes 1572872 | tf_op jit(solution)/shard_map/ppermute | solution.py:299
  56.4 16.5 %collective-permute-start.16 = (bf16[512,512]{1,0:T(8,128)(2,1)S(1)}, bf16[512,512]{1,0:T(8,128)(2,1)S(1)}, u32[]{:S(2)}, u32[]{:S(2)}) collective-permute-start(bf16[512,512]{1,0:T(8,128)(2,1)S(1)} %collective-permute-done.15.refs_0_.refs_6_), channel_id=1, source_target_pairs={{0,4},{1,29},{2,6},{3,31},{4,8},{5,1},{6,10},{7,3},{8,12},{9,5},{1... | collective-permute-start | bytes 1572872 | tf_op jit(solution)/shard_map/ppermute | solution.py:296
  60.3 18.8 %collective-permute-start.19 = (bf16[512,512]{1,0:T(8,128)(2,1)S(1)}, bf16[512,512]{1,0:T(8,128)(2,1)S(1)}, u32[]{:S(2)}, u32[]{:S(2)}) collective-permute-start(bf16[512,512]{1,0:T(8,128)(2,1)S(1)} %collective-permute-done.12.refs_2_.refs_8_), channel_id=1, source_target_pairs={{0,4},{1,29},{2,6},{3,31},{4,8},{5,1},{6,10},{7,3},{8,12},{9,5},{1... | collective-permute-start | bytes 1572872 | tf_op jit(solution)/shard_map/ppermute | solution.py:296
  62.1 14.8 %collective-permute-start.5 = (bf16[512,1024]{1,0:T(8,128)(2,1)S(1)}, bf16[512,1024]{1,0:T(8,128)(2,1)S(1)}, u32[]{:S(2)}, u32[]{:S(2)}) collective-permute-start(bf16[512,1024]{1,0:T(8,128)(2,1)S(1)} %collective-permute-done.4.refs_2_), channel_id=1, source_target_pairs={{0,32},{1,97},{32,64},{33,1},{64,96},{65,33},{96,0},{97,65},{128,1... | collective-permute-start | bytes 3145736 | tf_op jit(solution)/shard_map/ppermute | solution.py:305
  72.8 15.1 %collective-permute-start.17 = (bf16[512,512]{1,0:T(8,128)(2,1)S(1)}, bf16[512,512]{1,0:T(8,128)(2,1)S(1)}, u32[]{:S(2)}, u32[]{:S(2)}) collective-permute-start(bf16[512,512]{1,0:T(8,128)(2,1)S(1)} %collective-permute-done.16.refs_0_.refs_9_), channel_id=1, source_target_pairs={{0,2},{2,0},{4,6},{6,4},{8,10},{10,8},{12,14},{14,12},{16,18},{18,... | collective-permute-start | bytes 1572872 | tf_op jit(solution)/shard_map/ppermute | solution.py:302
  74.2 13.7 %collective-permute-start.18 = (bf16[512,512]{1,0:T(8,128)(2,1)S(1)}, bf16[512,512]{1,0:T(8,128)(2,1)S(1)}, u32[]{:S(2)}, u32[]{:S(2)}) collective-permute-start(bf16[512,512]{1,0:T(8,128)(2,1)S(1)} %collective-permute-done.10.refs_3_.refs_12_), channel_id=1, source_target_pairs={{0,28},{1,5},{2,30},{3,7},{4,0},{5,9},{6,2},{7,11},{8,4},{9,13},{1... | collective-permute-start | bytes 1572872 | tf_op jit(solution)/shard_map/ppermute | solution.py:299
  77.2 12.3 %collective-permute-start.6 = (bf16[2048,1024]{1,0:T(8,128)(2,1)S(1)}, bf16[2048,1024]{1,0:T(8,128)(2,1)S(1)}, u32[]{:S(2)}, u32[]{:S(2)}) collective-permute-start(bf16[2048,1024]{1,0:T(8,128)(2,1)S(1)} %shard_map.159.refs_16_), channel_id=1, source_target_pairs={{0,1},{1,0},{2,3},{3,2},{4,5},{5,4},{6,7},{7,6},{8,9},{9,8},{10,11... | collective-permute-start | bytes 12582920 | tf_op jit(solution)/shard_map/ppermute | solution.py:311
  96.3 9.6 %collective-permute-start.25 = (bf16[1040,128]{1,0:T(8,128)(2,1)S(1)}, bf16[1040,128]{1,0:T(8,128)(2,1)S(1)}, u32[]{:S(2)}, u32[]{:S(2)}) collective-permute-start(bf16[1040,128]{1,0:T(8,128)(2,1)S(1)} %get-tuple-element.101), channel_id=1, source_target_pairs={{0,96},{32,0},{64,32},{96,64},{128,224},{160,128},{192,160},{224,1... | collective-permute-start | bytes 798728 | tf_op jit(solution)/shard_map/ppermute | solution.py:308
  102.2 15.1 %collective-permute-start.23 = (bf16[1040,128]{1,0:T(8,128)(2,1)S(1)}, bf16[1040,128]{1,0:T(8,128)(2,1)S(1)}, u32[]{:S(2)}, u32[]{:S(2)}) collective-permute-start(bf16[1040,128]{1,0:T(8,128)(2,1)S(1)} %get-tuple-element.93), channel_id=1, source_target_pairs={{0,96},{32,0},{64,32},{96,64},{128,224},{160,128},{192,160},{224,1... | collective-permute-start | bytes 798728 | tf_op jit(solution)/shard_map/ppermute | solution.py:308
  106.9 16.8 %collective-permute-start.27 = (bf16[1040,128]{1,0:T(8,128)(2,1)S(1)}, bf16[1040,128]{1,0:T(8,128)(2,1)S(1)}, u32[]{:S(2)}, u32[]{:S(2)}) collective-permute-start(bf16[1040,128]{1,0:T(8,128)(2,1)S(1)} %get-tuple-element.104), channel_id=1, source_target_pairs={{0,128},{32,160},{64,192},{96,224},{128,0},{160,32},{192,64},{224,... | collective-permute-start | bytes 798728 | tf_op jit(solution)/shard_map/ppermute | solution.py:308
  107.7 16.0 %collective-permute-start.28 = (bf16[1040,128]{1,0:T(8,128)(2,1)S(1)}, bf16[1040,128]{1,0:T(8,128)(2,1)S(1)}, u32[]{:S(2)}, u32[]{:S(2)}) collective-permute-start(bf16[1040,128]{1,0:T(8,128)(2,1)S(1)} %get-tuple-element.105), channel_id=1, source_target_pairs={{0,64},{32,96},{64,0},{96,32},{128,192},{160,224},{192,128},{224,1... | collective-permute-start | bytes 798728 | tf_op jit(solution)/shard_map/ppermute | solution.py:308
  (9 other events, 77.8 us)

commit v6 on v5

--- a/solution.py
+++ b/solution.py
@@ -228,9 +228,10 @@
     )(before, *arrived)
 
 
-def grad_kernel(ids, table, *refs):
+def grad_kernel(ids, last, table, *refs):
     count = len(ids)
-    blocks, mine, theirs, out, total = refs[:count], *refs[count:]
+    blocks, mine, theirs = refs[:count], refs[count], refs[count + 1]
+    before, out, total = refs[count + 2] if last else None, refs[-2], refs[-1]
     side = table[SIDE_AT]
     core = table[SIDE_AT + 1]
     for k, place in enumerate(ids):
@@ -243,24 +244,29 @@
                 blocks[k][...], weights, (((1,), (1,)), ((), ())), preferred_element_type=F32)
             if k > 0:
                 made = made + total[part]
+            elif last:
+                made = made + before[part]
             if k < count - 1:
                 total[part] = made
+            elif last:
+                out[:, pl.ds(pl.multiple_of(half * 256, 256), 256)] = made.astype(out.dtype)
             else:
-                out[:, pl.ds(pl.multiple_of(half * 256, 256), 256)] = made.astype(out.dtype)
-
-
-def grad_sum(table, ids, blocks, parts):
+                out[part] = made
+
+
+def grad_sum(table, ids, blocks, parts, before=None):
     count = len(ids)
-    return pl.pallas_call(
-        functools.partial(grad_kernel, tuple(ids)),
-        out_shape=jax.ShapeDtypeStruct((512, 512), BF16),
-        in_specs=[smem_spec()] + [vmem_spec()] * (count + 2),
+    last = before is not None
+    return pl.pallas_call(
+        functools.partial(grad_kernel, tuple(ids), last),
+        out_shape=jax.ShapeDtypeStruct((512, 512), BF16) if last
+        else jax.ShapeDtypeStruct((2, 512, 256), F32),
+        in_specs=[smem_spec()] + [vmem_spec()] * (count + 2 + last),
         out_specs=vmem_spec(),
         scratch_shapes=[pltpu.VMEM((2, 512, 256), F32)],
         compiler_params=params(GRAD_MIB),
-        cost_estimate=pl.CostEstimate(
-            flops=2 * 512 ** 3 * count, bytes_accessed=(8 + count) * 1024 * 1024, transcendentals=0),
-    )(table, *blocks, *parts)
+        cost_estimate=pl.CostEstimate(flops=0, bytes_accessed=0, transcendentals=0),
+    )(table, *blocks, *parts, *([before] if last else []))
 
 
 def join_kernel(*refs):
@@ -369,11 +375,13 @@
     cols = [grad_out, f1, r1, f2, r2, o0, f3, r3, of2, f4, of1, or1, or2, of3, or3, of4]
 
     theirs, early_table = together((theirs, table))
+    parts = [mine, theirs]
     other_early = to_core(pick(early_table, 0, EARLY, total))
+    first_half = grad_sum(early_table, range(8), cols[:8], parts)
+    first_half, early_table = together((first_half, early_table))
     early = code(early_table, 0, EARLY, total, other_early, 0)
     *early, late_table = together((*early, table))
     other_late = to_core(pick(late_table, EARLY, 8, total))
-    parts = [mine, theirs]
     late = code(late_table, EARLY, 8, total, other_late, 3)
     next_y, last_y, beside, opposite, own = late
 
@@ -381,11 +389,11 @@
     ups, downs = to_row(early[1], 0, 1), to_row(early[2], 0, 3)
     near = [to_row(next_y, 0, 1), to_row(last_y, 0, 3)]
     beside, opposite = relay([(beside, [ups, downs]), (opposite, [cross])])
+    beside, opposite, grad_table = together((beside, opposite, late_table))
+    far = [to_row(beside, 1, 0), to_row(opposite, 0, 2)]
+    grad_in = grad_sum(grad_table, range(8, 16), cols[8:], parts, first_half)
+    own, grad_in = together((own, grad_in))
     pushed = add_coded(own, near)
-    far = [to_row(beside, 1, 0), to_row(opposite, 0, 2)]
-    pushed, grad_table = together((pushed, late_table))
-    grad_in = grad_sum(grad_table, range(16), cols, parts)
-    pushed, grad_in = together((pushed, grad_in))
     pushed = add_coded(pushed, far)
     return grad_in, pushed.reshape(1, CAP, BLK, BLK)
 

time: 125 us -> 120 us (0.960)
  the two profiles are of different devices: /device:TPU:126 before, /device:TPU:102 now
where the time goes in v6:
time: 120 us
  waiting for transfers between devices  48.9 us (41%)
  starting transfers between devices  39.9 us (33%)
  Pallas kernels  22.1 us (18%)
  other arithmetic  4.67 us (4%)
  local copies, waits for them, and re-layouts  3.23 us (3%)
    ppermute x4, waiting for transfers between devices, across(): return lax.ppermute(v, 'col', X_SWAP)  19 us
    ppermute x6, starting transfers between devices, ahead(): return lax.ppermute(v, ('col', 'srv'), z_shift(1))  14.7 us
    ppermute x5, waiting for transfers between devices, back(): return lax.ppermute(v, ('col', 'srv'), z_shift(-1))  12.4 us
    ppermute x8, starting transfers between devices, to_row(): return lax.ppermute(v, 'row', row_shift(dx, dy))  10.6 us
    pallas_call x5, Pallas kernels, dense(): pl.pallas_call(functools.partial(dense_kernel, count, place, first), out_...  7.91 us
    ppermute x8, waiting for transfers between devices, to_row(): return lax.ppermute(v, 'row', row_shift(dx, dy))  7.71 us
    ppermute x4, starting transfers between devices, across(): return lax.ppermute(v, 'col', X_SWAP)  7.17 us
    pallas_call x2, Pallas kernels, grad_sum(): pl.pallas_call(functools.partial(grad_kernel, tuple(ids), last), out_shap...  6.66 us
  transfers between devices with their start and end apart: 29, of which 16 were waited for; matrix products, arithmetic and copies ran while one was open for 6% of the time, Pallas kernels for 15%

profile of v6, /device:TPU:102, one launch (start us, length us, event | category | flops | bytes accessed | tf_op | source)
XLA Modules:
  0.0 119.6 jit_solution(14573067574364271194)
XLA Ops:
  0.8 3.1 %collective-permute-start.2 = (bf16[512,512]{1,0:T(8,128)(2,1)}, bf16[512,512]{1,0:T(8,128)(2,1)S(1)}, u32[]{:S(2)}, u32[]{:S(2)}) collective-permute-start(bf16[512,512]{1,0:T(8,128)(2,1)} %refs_0_.3), channel_id=1, source_target_pairs={{0,4},{1,29},{2,6},{3,31},{4,8},{5,1},{6,10},{7,3},{8,12},{9,5},{1... | collective-permute-start | bytes 1572872 | tf_op jit(solution)/shard_map/ppermute | solution.py:302
  8.0 2.0 %copy.22 = bf16[512,512]{0,1:T(8,128)(2,1)} copy(bf16[512,512]{1,0:T(8,128)(2,1)} %param.15) | data formatting | bytes 1048576 | tf_op args[0]
  11.8 3.4 %collective-permute-done.1.refs_2_ = bf16[512,512]{1,0:T(8,128)(2,1)S(1)} collective-permute-done((bf16[512,512]{1,0:T(8,128)(2,1)}, bf16[512,512]{1,0:T(8,128)(2,1)S(1)}, u32[]{:S(2)}, u32[]{:S(2)}) %collective-permute-start.1) | collective-permute-done | bytes 524320 | tf_op jit(solution)/shard_map/ppermute | solution.py:305
  15.4 2.1 %collective-permute-done.refs_1_ = bf16[256,1024]{1,0:T(8,128)(2,1)} collective-permute-done((bf16[256,1024]{1,0:T(8,128)(2,1)S(1)}, bf16[256,1024]{1,0:T(8,128)(2,1)}, u32[]{:S(2)}, u32[]{:S(2)}) %collective-permute-start) | collective-permute-done | bytes 524320 | tf_op jit(solution)/shard_map/ppermute | solution.py:314
  18.9 3.2 %collective-permute-start.9 = (bf16[512,512]{1,0:T(8,128)(2,1)S(1)}, bf16[512,512]{1,0:T(8,128)(2,1)S(1)}, u32[]{:S(2)}, u32[]{:S(2)}) collective-permute-start(bf16[512,512]{1,0:T(8,128)(2,1)S(1)} %collective-permute-done.2.refs_1_), channel_id=1, source_target_pairs={{0,4},{1,29},{2,6},{3,31},{4,8},{5,1},{6,10},{7,3},{8,12},{9,5},{1... | collective-permute-start | bytes 1572872 | tf_op jit(solution)/shard_map/ppermute | solution.py:302
  23.2 1.7 %collective-permute-start.3 = (bf16[512,1024]{1,0:T(8,128)(2,1)S(1)}, bf16[512,1024]{1,0:T(8,128)(2,1)S(1)}, u32[]{:S(2)}, u32[]{:S(2)}) collective-permute-start(bf16[512,1024]{1,0:T(8,128)(2,1)S(1)} %shard_map.158.refs_0_), channel_id=1, source_target_pairs={{0,32},{1,97},{32,64},{33,1},{64,96},{65,33},{96,0},{97,65},{128,1... | collective-permute-start | bytes 3145736 | tf_op jit(solution)/shard_map/ppermute | solution.py:311
  27.5 4.9 %collective-permute-done.7.refs_2_.refs_5_ = bf16[512,512]{1,0:T(8,128)(2,1)S(1)} collective-permute-done((bf16[512,512]{1,0:T(8,128)(2,1)}, bf16[512,512]{1,0:T(8,128)(2,1)S(1)}, u32[]{:S(2)}, u32[]{:S(2)}) %collective-permute-start.7) | collective-permute-done | bytes 524320 | tf_op jit(solution)/shard_map/ppermute | solution.py:308
  33.8 2.1 %collective-permute-start.10 = (bf16[512,512]{1,0:T(8,128)(2,1)S(1)}, bf16[512,512]{1,0:T(8,128)(2,1)S(1)}, u32[]{:S(2)}, u32[]{:S(2)}) collective-permute-start(bf16[512,512]{1,0:T(8,128)(2,1)S(1)} %collective-permute-done.9.refs_0_.refs_3_), channel_id=1, source_target_pairs={{0,2},{2,0},{4,6},{6,4},{8,10},{10,8},{12,14},{14,12},{16,18},{18,... | collective-permute-start | bytes 1572872 | tf_op jit(solution)/shard_map/ppermute | solution.py:308
  35.9 2.6 %collective-permute-start.13 = (bf16[512,512]{1,0:T(8,128)(2,1)S(1)}, bf16[512,512]{1,0:T(8,128)(2,1)S(1)}, u32[]{:S(2)}, u32[]{:S(2)}) collective-permute-start(bf16[512,512]{1,0:T(8,128)(2,1)S(1)} %collective-permute-done.9.refs_0_.refs_3_), channel_id=1, source_target_pairs={{0,4},{1,29},{2,6},{3,31},{4,8},{5,1},{6,10},{7,3},{8,12},{9,5},{1... | collective-permute-start | bytes 1572872 | tf_op jit(solution)/shard_map/ppermute | solution.py:302
  38.5 2.0 %collective-permute-start.12 = (bf16[512,512]{1,0:T(8,128)(2,1)S(1)}, bf16[512,512]{1,0:T(8,128)(2,1)S(1)}, u32[]{:S(2)}, u32[]{:S(2)}) collective-permute-start(bf16[512,512]{1,0:T(8,128)(2,1)S(1)} %collective-permute-done.8.refs_1_.refs_4_), channel_id=1, source_target_pairs={{0,28},{1,5},{2,30},{3,7},{4,0},{5,9},{6,2},{7,11},{8,4},{9,13},{1... | collective-permute-start | bytes 1572872 | tf_op jit(solution)/shard_map/ppermute | solution.py:305
  43.6 6.2 %collective-permute-done.10.refs_2_.refs_0_ = bf16[512,512]{1,0:T(8,128)(2,1)S(1)} collective-permute-done((bf16[512,512]{1,0:T(8,128)(2,1)S(1)}, bf16[512,512]{1,0:T(8,128)(2,1)S(1)}, u32[]{:S(2)}, u32[]{:S(2)}) %collective-permute-start.10) | collective-permute-done | bytes 524320 | tf_op jit(solution)/shard_map/ppermute | solution.py:308
  49.8 2.1 %collective-permute-start.14 = (bf16[512,512]{1,0:T(8,128)(2,1)S(1)}, bf16[512,512]{1,0:T(8,128)(2,1)S(1)}, u32[]{:S(2)}, u32[]{:S(2)}) collective-permute-start(bf16[512,512]{1,0:T(8,128)(2,1)S(1)} %collective-permute-done.8.refs_1_.refs_4_), channel_id=1, source_target_pairs={{0,2},{2,0},{4,6},{6,4},{8,10},{10,8},{12,14},{14,12},{16,18},{18,... | collective-permute-start | bytes 1572872 | tf_op jit(solution)/shard_map/ppermute | solution.py:308
  51.9 4.5 %collective-permute-done.11.refs_1_.refs_2_ = bf16[512,512]{1,0:T(8,128)(2,1)S(1)} collective-permute-done((bf16[512,512]{1,0:T(8,128)(2,1)S(1)}, bf16[512,512]{1,0:T(8,128)(2,1)S(1)}, u32[]{:S(2)}, u32[]{:S(2)}) %collective-permute-start.11) | collective-permute-done | bytes 524320 | tf_op jit(solution)/shard_map/ppermute | solution.py:302
  56.4 4.0 %collective-permute-start.16 = (bf16[512,512]{1,0:T(8,128)(2,1)S(1)}, bf16[512,512]{1,0:T(8,128)(2,1)S(1)}, u32[]{:S(2)}, u32[]{:S(2)}) collective-permute-start(bf16[512,512]{1,0:T(8,128)(2,1)S(1)} %collective-permute-done.13.refs_6_.refs_0_), channel_id=1, source_target_pairs={{0,4},{1,29},{2,6},{3,31},{4,8},{5,1},{6,10},{7,3},{8,12},{9,5},{1... | collective-permute-start | bytes 1572872 | tf_op jit(solution)/shard_map/ppermute | solution.py:302
  60.3 1.8 %collective-permute-start.19 = (bf16[512,512]{1,0:T(8,128)(2,1)S(1)}, bf16[512,512]{1,0:T(8,128)(2,1)S(1)}, u32[]{:S(2)}, u32[]{:S(2)}) collective-permute-start(bf16[512,512]{1,0:T(8,128)(2,1)S(1)} %collective-permute-done.10.refs_2_.refs_0_), channel_id=1, source_target_pairs={{0,4},{1,29},{2,6},{3,31},{4,8},{5,1},{6,10},{7,3},{8,12},{9,5},{1... | collective-permute-start | bytes 1572872 | tf_op jit(solution)/shard_map/ppermute | solution.py:302
  65.2 7.5 %collective-permute-done.15.refs_2_.refs_3_ = bf16[512,512]{1,0:T(8,128)(2,1)S(1)} collective-permute-done((bf16[512,512]{1,0:T(8,128)(2,1)S(1)}, bf16[512,512]{1,0:T(8,128)(2,1)S(1)}, u32[]{:S(2)}, u32[]{:S(2)}) %collective-permute-start.15) | collective-permute-done | bytes 524320 | tf_op jit(solution)/shard_map/ppermute | solution.py:305
  74.2 3.9 %collective-permute-done.5.refs_3_ = bf16[512,1024]{1,0:T(8,128)(2,1)S(1)} collective-permute-done((bf16[512,1024]{1,0:T(8,128)(2,1)S(1)}, bf16[512,1024]{1,0:T(8,128)(2,1)S(1)}, u32[]{:S(2)}, u32[]{:S(2)}) %collective-permute-start.5) | collective-permute-done | bytes 1048608 | tf_op jit(solution)/shard_map/ppermute | solution.py:311
  78.5 1.8 %shard_map.164.refs_3_ = f32[256,128,128]{2,1,0:T(8,128)S(1)} custom-call(s32[194]{0:T(256)S(1)} %concatenate.3.table, bf16[512,512]{1,0:T(8,128)(2,1)S(1)} %bitcast.30, bf16[512,512]{1,0:T(8,128)(2,1)S(1)} %collective-permute-done.16.refs_0_.refs_1_, bf16[512,512]{1,0:T(8,128)(2,1)S(1)} %collective-permute-done.11.refs_1_.refs_2_, ...), custom_call_target="tpu_custom_call", output_to_operand_aliasing={{}: (6, {})} | custom-call | flops 30000001024 | bytes 6291456 | tf_op jit(solution)/shard_map/pallas_call | solution.py:79
  80.3 8.0 %collective-permute-done.17.refs_2_.refs_7_ = bf16[512,512]{1,0:T(8,128)(2,1)S(1)} collective-permute-done((bf16[512,512]{1,0:T(8,128)(2,1)S(1)}, bf16[512,512]{1,0:T(8,128)(2,1)S(1)}, u32[]{:S(2)}, u32[]{:S(2)}) %collective-permute-start.17) | collective-permute-done | bytes 524320 | tf_op jit(solution)/shard_map/ppermute | solution.py:308
  90.6 2.9 %shard_map.162.refs_10_ = f32[2,512,256]{2,1,0:T(8,128)S(1)} custom-call(s32[194]{0:T(256)S(1)} %concatenate.3.table, bf16[512,512]{1,0:T(8,128)(2,1)S(1)} %copy-done.1, bf16[512,512]{1,0:T(8,128)(2,1)S(1)} %collective-permute-done.2.refs_1_, bf16[512,512]{1,0:T(8,128)(2,1)S(1)} %collective-permute-done.1.refs_2_, ...), custom_call_target="tpu_custom_call" | custom-call | tf_op jit(solution)/shard_map/pallas_call | solution.py:260
  97.2 2.0 %collective-permute-start.23 = (bf16[1040,128]{1,0:T(8,128)(2,1)S(1)}, bf16[1040,128]{1,0:T(8,128)(2,1)S(1)}, u32[]{:S(2)}, u32[]{:S(2)}) collective-permute-start(bf16[1040,128]{1,0:T(8,128)(2,1)S(1)} %get-tuple-element.99), channel_id=1, source_target_pairs={{0,96},{32,0},{64,32},{96,64},{128,224},{160,128},{192,160},{224,1... | collective-permute-start | bytes 798728 | tf_op jit(solution)/shard_map/ppermute | solution.py:314
  103.3 2.0 %collective-permute-start.26 = (bf16[1040,128]{1,0:T(8,128)(2,1)S(1)}, bf16[1040,128]{1,0:T(8,128)(2,1)S(1)}, u32[]{:S(2)}, u32[]{:S(2)}) collective-permute-start(bf16[1040,128]{1,0:T(8,128)(2,1)S(1)} %get-tuple-element.109), channel_id=1, source_target_pairs={{0,96},{32,0},{64,32},{96,64},{128,224},{160,128},{192,160},{224,1... | collective-permute-start | bytes 798728 | tf_op jit(solution)/shard_map/ppermute | solution.py:314
  110.5 3.7 %shard_map.171 = bf16[512,512]{1,0:T(8,128)(2,1)} custom-call(s32[194]{0:T(256)S(1)} %concatenate.3.table, bf16[512,512]{1,0:T(8,128)(2,1)S(1)} %collective-permute-done.10.refs_2_.refs_0_, bf16[512,512]{1,0:T(8,128)(2,1)S(1)} %collective-permute-done.16.refs_0_.refs_1_, bf16[512,512]{1,0:T(8,128)(2,1)S(1)} %collective-permute-done.11.refs_1_.refs_2_, ...), custom_call_target="tpu_custom_call" | custom-call | tf_op jit(solution)/shard_map/pallas_call | solution.py:260
  114.3 2.5 %collective-permute-done.26.refs_1_ = bf16[1040,128]{1,0:T(8,128)(2,1)S(1)} collective-permute-done((bf16[1040,128]{1,0:T(8,128)(2,1)S(1)}, bf16[1040,128]{1,0:T(8,128)(2,1)S(1)}, u32[]{:S(2)}, u32[]{:S(2)}) %collective-permute-start.26) | collective-permute-done | bytes 266272 | tf_op jit(solution)/shard_map/ppermute | solution.py:314
  (71 shorter events, 38.7 us)
Async XLA Ops:
  0.7 14.5 %collective-permute-start.1 = (bf16[512,512]{1,0:T(8,128)(2,1)}, bf16[512,512]{1,0:T(8,128)(2,1)S(1)}, u32[]{:S(2)}, u32[]{:S(2)}) collective-permute-start(bf16[512,512]{1,0:T(8,128)(2,1)} %refs_0_.3), channel_id=1, source_target_pairs={{0,28},{1,5},{2,30},{3,7},{4,0},{5,9},{6,2},{7,11},{8,4},{9,13},{1... | collective-permute-start | bytes 1572872 | tf_op jit(solution)/shard_map/ppermute | solution.py:305
  0.8 14.5 %collective-permute-start.2 = (bf16[512,512]{1,0:T(8,128)(2,1)}, bf16[512,512]{1,0:T(8,128)(2,1)S(1)}, u32[]{:S(2)}, u32[]{:S(2)}) collective-permute-start(bf16[512,512]{1,0:T(8,128)(2,1)} %refs_0_.3), channel_id=1, source_target_pairs={{0,4},{1,29},{2,6},{3,31},{4,8},{5,1},{6,10},{7,3},{8,12},{9,5},{1... | collective-permute-start | bytes 1572872 | tf_op jit(solution)/shard_map/ppermute | solution.py:302
  4.0 13.5 %collective-permute-start = (bf16[256,1024]{1,0:T(8,128)(2,1)S(1)}, bf16[256,1024]{1,0:T(8,128)(2,1)}, u32[]{:S(2)}, u32[]{:S(2)}) collective-permute-start(bf16[256,1024]{1,0:T(8,128)(2,1)S(1)} %constant_dynamic-slice_fusion.refs_0_), channel_id=1, source_target_pairs={{0,128},{32,160},{64,192},{96,224},{128,0},{160,32},{192,64},{224,... | collective-permute-start | bytes 1572872 | tf_op jit(solution)/shard_map/ppermute | solution.py:314
  17.5 14.8 %collective-permute-start.7 = (bf16[512,512]{1,0:T(8,128)(2,1)}, bf16[512,512]{1,0:T(8,128)(2,1)S(1)}, u32[]{:S(2)}, u32[]{:S(2)}) collective-permute-start(bf16[512,512]{1,0:T(8,128)(2,1)} %refs_0_.3), channel_id=1, source_target_pairs={{0,2},{2,0},{4,6},{6,4},{8,10},{10,8},{12,14},{14,12},{16,18},{18,... | collective-permute-start | bytes 1572872 | tf_op jit(solution)/shard_map/ppermute | solution.py:308
  18.9 14.9 %collective-permute-start.8 = (bf16[512,512]{1,0:T(8,128)(2,1)S(1)}, bf16[512,512]{1,0:T(8,128)(2,1)S(1)}, u32[]{:S(2)}, u32[]{:S(2)}) collective-permute-start(bf16[512,512]{1,0:T(8,128)(2,1)S(1)} %collective-permute-done.1.refs_2_), channel_id=1, source_target_pairs={{0,28},{1,5},{2,30},{3,7},{4,0},{5,9},{6,2},{7,11},{8,4},{9,13},{1... | collective-permute-start | bytes 1572872 | tf_op jit(solution)/shard_map/ppermute | solution.py:305
  18.9 14.9 %collective-permute-start.9 = (bf16[512,512]{1,0:T(8,128)(2,1)S(1)}, bf16[512,512]{1,0:T(8,128)(2,1)S(1)}, u32[]{:S(2)}, u32[]{:S(2)}) collective-permute-start(bf16[512,512]{1,0:T(8,128)(2,1)S(1)} %collective-permute-done.2.refs_1_), channel_id=1, source_target_pairs={{0,4},{1,29},{2,6},{3,31},{4,8},{5,1},{6,10},{7,3},{8,12},{9,5},{1... | collective-permute-start | bytes 1572872 | tf_op jit(solution)/shard_map/ppermute | solution.py:302
  23.2 17.2 %collective-permute-start.3 = (bf16[512,1024]{1,0:T(8,128)(2,1)S(1)}, bf16[512,1024]{1,0:T(8,128)(2,1)S(1)}, u32[]{:S(2)}, u32[]{:S(2)}) collective-permute-start(bf16[512,1024]{1,0:T(8,128)(2,1)S(1)} %shard_map.158.refs_0_), channel_id=1, source_target_pairs={{0,32},{1,97},{32,64},{33,1},{64,96},{65,33},{96,0},{97,65},{128,1... | collective-permute-start | bytes 3145736 | tf_op jit(solution)/shard_map/ppermute | solution.py:311
  33.8 16.0 %collective-permute-start.10 = (bf16[512,512]{1,0:T(8,128)(2,1)S(1)}, bf16[512,512]{1,0:T(8,128)(2,1)S(1)}, u32[]{:S(2)}, u32[]{:S(2)}) collective-permute-start(bf16[512,512]{1,0:T(8,128)(2,1)S(1)} %collective-permute-done.9.refs_0_.refs_3_), channel_id=1, source_target_pairs={{0,2},{2,0},{4,6},{6,4},{8,10},{10,8},{12,14},{14,12},{16,18},{18,... | collective-permute-start | bytes 1572872 | tf_op jit(solution)/shard_map/ppermute | solution.py:308
  35.9 20.5 %collective-permute-start.13 = (bf16[512,512]{1,0:T(8,128)(2,1)S(1)}, bf16[512,512]{1,0:T(8,128)(2,1)S(1)}, u32[]{:S(2)}, u32[]{:S(2)}) collective-permute-start(bf16[512,512]{1,0:T(8,128)(2,1)S(1)} %collective-permute-done.9.refs_0_.refs_3_), channel_id=1, source_target_pairs={{0,4},{1,29},{2,6},{3,31},{4,8},{5,1},{6,10},{7,3},{8,12},{9,5},{1... | collective-permute-start | bytes 1572872 | tf_op jit(solution)/shard_map/ppermute | solution.py:302
  38.4 17.9 %collective-permute-start.11 = (bf16[512,512]{1,0:T(8,128)(2,1)S(1)}, bf16[512,512]{1,0:T(8,128)(2,1)S(1)}, u32[]{:S(2)}, u32[]{:S(2)}) collective-permute-start(bf16[512,512]{1,0:T(8,128)(2,1)S(1)} %collective-permute-done.7.refs_2_.refs_5_), channel_id=1, source_target_pairs={{0,4},{1,29},{2,6},{3,31},{4,8},{5,1},{6,10},{7,3},{8,12},{9,5},{1... | collective-permute-start | bytes 1572872 | tf_op jit(solution)/shard_map/ppermute | solution.py:302
  38.5 17.9 %collective-permute-start.12 = (bf16[512,512]{1,0:T(8,128)(2,1)S(1)}, bf16[512,512]{1,0:T(8,128)(2,1)S(1)}, u32[]{:S(2)}, u32[]{:S(2)}) collective-permute-start(bf16[512,512]{1,0:T(8,128)(2,1)S(1)} %collective-permute-done.8.refs_1_.refs_4_), channel_id=1, source_target_pairs={{0,28},{1,5},{2,30},{3,7},{4,0},{5,9},{6,2},{7,11},{8,4},{9,13},{1... | collective-permute-start | bytes 1572872 | tf_op jit(solution)/shard_map/ppermute | solution.py:305
  40.5 21.6 %collective-permute-start.4 = (bf16[512,1024]{1,0:T(8,128)(2,1)S(1)}, bf16[512,1024]{1,0:T(8,128)(2,1)S(1)}, u32[]{:S(2)}, u32[]{:S(2)}) collective-permute-start(bf16[512,1024]{1,0:T(8,128)(2,1)S(1)} %collective-permute-done.3.refs_1_), channel_id=1, source_target_pairs={{0,32},{1,97},{32,64},{33,1},{64,96},{65,33},{96,0},{97,65},{128,1... | collective-permute-start | bytes 3145736 | tf_op jit(solution)/shard_map/ppermute | solution.py:311
  49.8 15.4 %collective-permute-start.14 = (bf16[512,512]{1,0:T(8,128)(2,1)S(1)}, bf16[512,512]{1,0:T(8,128)(2,1)S(1)}, u32[]{:S(2)}, u32[]{:S(2)}) collective-permute-start(bf16[512,512]{1,0:T(8,128)(2,1)S(1)} %collective-permute-done.8.refs_1_.refs_4_), channel_id=1, source_target_pairs={{0,2},{2,0},{4,6},{6,4},{8,10},{10,8},{12,14},{14,12},{16,18},{18,... | collective-permute-start | bytes 1572872 | tf_op jit(solution)/shard_map/ppermute | solution.py:308
  56.4 16.4 %collective-permute-start.15 = (bf16[512,512]{1,0:T(8,128)(2,1)S(1)}, bf16[512,512]{1,0:T(8,128)(2,1)S(1)}, u32[]{:S(2)}, u32[]{:S(2)}) collective-permute-start(bf16[512,512]{1,0:T(8,128)(2,1)S(1)} %collective-permute-done.7.refs_2_.refs_5_), channel_id=1, source_target_pairs={{0,28},{1,5},{2,30},{3,7},{4,0},{5,9},{6,2},{7,11},{8,4},{9,13},{1... | collective-permute-start | bytes 1572872 | tf_op jit(solution)/shard_map/ppermute | solution.py:305
  56.4 16.3 %collective-permute-start.16 = (bf16[512,512]{1,0:T(8,128)(2,1)S(1)}, bf16[512,512]{1,0:T(8,128)(2,1)S(1)}, u32[]{:S(2)}, u32[]{:S(2)}) collective-permute-start(bf16[512,512]{1,0:T(8,128)(2,1)S(1)} %collective-permute-done.13.refs_6_.refs_0_), channel_id=1, source_target_pairs={{0,4},{1,29},{2,6},{3,31},{4,8},{5,1},{6,10},{7,3},{8,12},{9,5},{1... | collective-permute-start | bytes 1572872 | tf_op jit(solution)/shard_map/ppermute | solution.py:302
  60.3 20.0 %collective-permute-start.19 = (bf16[512,512]{1,0:T(8,128)(2,1)S(1)}, bf16[512,512]{1,0:T(8,128)(2,1)S(1)}, u32[]{:S(2)}, u32[]{:S(2)}) collective-permute-start(bf16[512,512]{1,0:T(8,128)(2,1)S(1)} %collective-permute-done.10.refs_2_.refs_0_), channel_id=1, source_target_pairs={{0,4},{1,29},{2,6},{3,31},{4,8},{5,1},{6,10},{7,3},{8,12},{9,5},{1... | collective-permute-start | bytes 1572872 | tf_op jit(solution)/shard_map/ppermute | solution.py:302
  62.1 16.0 %collective-permute-start.5 = (bf16[512,1024]{1,0:T(8,128)(2,1)S(1)}, bf16[512,1024]{1,0:T(8,128)(2,1)S(1)}, u32[]{:S(2)}, u32[]{:S(2)}) collective-permute-start(bf16[512,1024]{1,0:T(8,128)(2,1)S(1)} %collective-permute-done.4.refs_2_), channel_id=1, source_target_pairs={{0,32},{1,97},{32,64},{33,1},{64,96},{65,33},{96,0},{97,65},{128,1... | collective-permute-start | bytes 3145736 | tf_op jit(solution)/shard_map/ppermute | solution.py:311
  72.7 15.6 %collective-permute-start.17 = (bf16[512,512]{1,0:T(8,128)(2,1)S(1)}, bf16[512,512]{1,0:T(8,128)(2,1)S(1)}, u32[]{:S(2)}, u32[]{:S(2)}) collective-permute-start(bf16[512,512]{1,0:T(8,128)(2,1)S(1)} %collective-permute-done.16.refs_0_.refs_1_), channel_id=1, source_target_pairs={{0,2},{2,0},{4,6},{6,4},{8,10},{10,8},{12,14},{14,12},{16,18},{18,... | collective-permute-start | bytes 1572872 | tf_op jit(solution)/shard_map/ppermute | solution.py:308
  74.2 14.0 %collective-permute-start.18 = (bf16[512,512]{1,0:T(8,128)(2,1)S(1)}, bf16[512,512]{1,0:T(8,128)(2,1)S(1)}, u32[]{:S(2)}, u32[]{:S(2)}) collective-permute-start(bf16[512,512]{1,0:T(8,128)(2,1)S(1)} %collective-permute-done.14.refs_3_.refs_4_), channel_id=1, source_target_pairs={{0,28},{1,5},{2,30},{3,7},{4,0},{5,9},{6,2},{7,11},{8,4},{9,13},{1... | collective-permute-start | bytes 1572872 | tf_op jit(solution)/shard_map/ppermute | solution.py:305
  78.4 11.4 %collective-permute-start.6 = (bf16[2048,1024]{1,0:T(8,128)(2,1)S(1)}, bf16[2048,1024]{1,0:T(8,128)(2,1)S(1)}, u32[]{:S(2)}, u32[]{:S(2)}) collective-permute-start(bf16[2048,1024]{1,0:T(8,128)(2,1)S(1)} %shard_map.159.refs_8_), channel_id=1, source_target_pairs={{0,1},{1,0},{2,3},{3,2},{4,5},{5,4},{6,7},{7,6},{8,9},{9,8},{10,11... | collective-permute-start | bytes 12582920 | tf_op jit(solution)/shard_map/ppermute | solution.py:317
  96.0 9.9 %collective-permute-start.22 = (bf16[1040,128]{1,0:T(8,128)(2,1)S(1)}, bf16[1040,128]{1,0:T(8,128)(2,1)S(1)}, u32[]{:S(2)}, u32[]{:S(2)}) collective-permute-start(bf16[1040,128]{1,0:T(8,128)(2,1)S(1)} %get-tuple-element.98), channel_id=1, source_target_pairs={{0,32},{32,64},{64,96},{96,0},{128,160},{160,192},{192,224},{224,1... | collective-permute-start | bytes 798728 | tf_op jit(solution)/shard_map/ppermute | solution.py:314
  101.8 12.4 %collective-permute-start.25 = (bf16[1040,128]{1,0:T(8,128)(2,1)S(1)}, bf16[1040,128]{1,0:T(8,128)(2,1)S(1)}, u32[]{:S(2)}, u32[]{:S(2)}) collective-permute-start(bf16[1040,128]{1,0:T(8,128)(2,1)S(1)} %get-tuple-element.108), channel_id=1, source_target_pairs={{0,32},{32,64},{64,96},{96,0},{128,160},{160,192},{192,224},{224,1... | collective-permute-start | bytes 798728 | tf_op jit(solution)/shard_map/ppermute | solution.py:314
  103.3 13.5 %collective-permute-start.26 = (bf16[1040,128]{1,0:T(8,128)(2,1)S(1)}, bf16[1040,128]{1,0:T(8,128)(2,1)S(1)}, u32[]{:S(2)}, u32[]{:S(2)}) collective-permute-start(bf16[1040,128]{1,0:T(8,128)(2,1)S(1)} %get-tuple-element.109), channel_id=1, source_target_pairs={{0,96},{32,0},{64,32},{96,64},{128,224},{160,128},{192,160},{224,1... | collective-permute-start | bytes 798728 | tf_op jit(solution)/shard_map/ppermute | solution.py:314
  109.1 9.2 %collective-permute-start.28 = (bf16[1040,128]{1,0:T(8,128)(2,1)S(1)}, bf16[1040,128]{1,0:T(8,128)(2,1)S(1)}, u32[]{:S(2)}, u32[]{:S(2)}) collective-permute-start(bf16[1040,128]{1,0:T(8,128)(2,1)S(1)} %get-tuple-element.111), channel_id=1, source_target_pairs={{0,64},{32,96},{64,0},{96,32},{128,192},{160,224},{192,128},{224,1... | collective-permute-start | bytes 798728 | tf_op jit(solution)/shard_map/ppermute | solution.py:314
  (9 other events, 78.9 us)

commit v7 on v6

--- a/solution.py
+++ b/solution.py
@@ -349,16 +349,18 @@
     r1, f1, own, table, xt = together((back(grad_out), ahead(grad_out), grad_out, table, xt))
 
     near_half, far_half, own, now = together((half, far_half, own, table))
+    f2, r2 = ahead(f1), back(r1)
     o0 = across(own)
     pair = join([near_half, far_half])
     w1 = around(pair)
     total = dense(None, now, xt, [grad_out, f1, r1], 0)
-    o0, r2, f2, total = together((o0, back(r1), ahead(f1), total))
+    r2, f2, total = together((r2, f2, total))
 
     w1, now = together((w1, table))
     w2 = around(w1)
     total = dense(total, now, xt, [f2, r2, o0], 3)
-    of2, of1, r3, f3, total = together((across(f2), ahead(o0), back(r2), ahead(f2), total))
+    f3, r3, of1 = ahead(f2), back(r2), ahead(o0)
+    of2, of1, r3, f3, total = together((across(f2), of1, r3, f3, total))
 
     w2, now = together((w2, table))
     w3 = around(w2)
@@ -369,7 +371,8 @@
     mine = join([pair, w1, w2, w3])
     theirs = to_core(mine)
     total = dense(total, now, xt, [f4, of1, or1, or2], 9)
-    of4, or3, of3, total = together((across(f4), back(or2), ahead(of2), total))
+    of3, or3 = ahead(of2), back(or2)
+    of4, or3, of3, total = together((across(f4), or3, of3, total))
 
     total = dense(total, table, xt, [of3, or3, of4], LAST)
     cols = [grad_out, f1, r1, f2, r2, o0, f3, r3, of2, f4, of1, or1, or2, of3, or3, of4]

time: 120 us -> 116 us (0.967)
  the two profiles are of different devices: /device:TPU:102 before, /device:TPU:1 now
where the time goes in v7:
time: 116 us; the launch traced here: 115 us
  starting transfers between devices  46.8 us (40%)
  waiting for transfers between devices  37.3 us (32%)
  Pallas kernels  22.1 us (19%)
  other arithmetic  4.67 us (4%)
  local copies, waits for them, and re-layouts  3.23 us (3%)
    ppermute x4, waiting for transfers between devices, across(): return lax.ppermute(v, 'col', X_SWAP)  16.1 us
    ppermute x6, starting transfers between devices, ahead(): return lax.ppermute(v, ('col', 'srv'), z_shift(1))  14.2 us
    ppermute x6, waiting for transfers between devices, ahead(): return lax.ppermute(v, ('col', 'srv'), z_shift(1))  9.08 us
    ppermute x4, starting transfers between devices, across(): return lax.ppermute(v, 'col', X_SWAP)  8.46 us
    ppermute x8, starting transfers between devices, to_row(): return lax.ppermute(v, 'row', row_shift(dx, dy))  8.37 us
    ppermute x3, starting transfers between devices, around(): return lax.ppermute(v, ('row', 'srv'), y_shift(1))  8.28 us
    pallas_call x5, Pallas kernels, dense(): pl.pallas_call(functools.partial(dense_kernel, count, place, first), out_...  7.9 us
    pallas_call x2, Pallas kernels, grad_sum(): pl.pallas_call(functools.partial(grad_kernel, tuple(ids), last), out_shap...  6.66 us
  transfers between devices with their start and end apart: 29, of which 17 were waited for; matrix products, arithmetic and copies ran while one was open for 6% of the time, Pallas kernels for 16%

profile of v7, /device:TPU:1, one launch (start us, length us, event | category | flops | bytes accessed | tf_op | source)
XLA Modules:
  0.0 114.9 jit_solution(6350506216508651213)
XLA Ops:
  0.7 2.5 %collective-permute-start.1 = (bf16[512,512]{1,0:T(8,128)(2,1)}, bf16[512,512]{1,0:T(8,128)(2,1)S(1)}, u32[]{:S(2)}, u32[]{:S(2)}) collective-permute-start(bf16[512,512]{1,0:T(8,128)(2,1)} %refs_0_.3), channel_id=1, source_target_pairs={{0,28},{1,5},{2,30},{3,7},{4,0},{5,9},{6,2},{7,11},{8,4},{9,13},{1... | collective-permute-start | bytes 1572872 | tf_op jit(solution)/shard_map/ppermute | solution.py:305
  3.2 4.0 %collective-permute-start.2 = (bf16[512,512]{1,0:T(8,128)(2,1)}, bf16[512,512]{1,0:T(8,128)(2,1)S(1)}, u32[]{:S(2)}, u32[]{:S(2)}) collective-permute-start(bf16[512,512]{1,0:T(8,128)(2,1)} %refs_0_.3), channel_id=1, source_target_pairs={{0,4},{1,29},{2,6},{3,31},{4,8},{5,1},{6,10},{7,3},{8,12},{9,5},{1... | collective-permute-start | bytes 1572872 | tf_op jit(solution)/shard_map/ppermute | solution.py:302
  15.7 2.6 %collective-permute-done.2.refs_1_ = bf16[512,512]{1,0:T(8,128)(2,1)S(1)} collective-permute-done((bf16[512,512]{1,0:T(8,128)(2,1)}, bf16[512,512]{1,0:T(8,128)(2,1)S(1)}, u32[]{:S(2)}, u32[]{:S(2)}) %collective-permute-start.2) | collective-permute-done | bytes 524320 | tf_op jit(solution)/shard_map/ppermute | solution.py:302
  20.0 2.7 %collective-permute-start.8 = (bf16[512,512]{1,0:T(8,128)(2,1)S(1)}, bf16[512,512]{1,0:T(8,128)(2,1)S(1)}, u32[]{:S(2)}, u32[]{:S(2)}) collective-permute-start(bf16[512,512]{1,0:T(8,128)(2,1)S(1)} %collective-permute-done.2.refs_1_), channel_id=1, source_target_pairs={{0,4},{1,29},{2,6},{3,31},{4,8},{5,1},{6,10},{7,3},{8,12},{9,5},{1... | collective-permute-start | bytes 1572872 | tf_op jit(solution)/shard_map/ppermute | solution.py:302
  23.8 2.8 %collective-permute-start.3 = (bf16[512,1024]{1,0:T(8,128)(2,1)S(1)}, bf16[512,1024]{1,0:T(8,128)(2,1)S(1)}, u32[]{:S(2)}, u32[]{:S(2)}) collective-permute-start(bf16[512,1024]{1,0:T(8,128)(2,1)S(1)} %shard_map.158.refs_0_), channel_id=1, source_target_pairs={{0,32},{1,97},{32,64},{33,1},{64,96},{65,33},{96,0},{97,65},{128,1... | collective-permute-start | bytes 3145736 | tf_op jit(solution)/shard_map/ppermute | solution.py:311
  26.6 2.7 %collective-permute-start.9 = (bf16[512,512]{1,0:T(8,128)(2,1)S(1)}, bf16[512,512]{1,0:T(8,128)(2,1)S(1)}, u32[]{:S(2)}, u32[]{:S(2)}) collective-permute-start(bf16[512,512]{1,0:T(8,128)(2,1)S(1)} %copy-done.1), channel_id=1, source_target_pairs={{0,2},{2,0},{4,6},{6,4},{8,10},{10,8},{12,14},{14,12},{16,18},{18,... | collective-permute-start | bytes 1572872 | tf_op jit(solution)/shard_map/ppermute | solution.py:308
  33.5 2.7 %collective-permute-start.10 = (bf16[512,512]{1,0:T(8,128)(2,1)S(1)}, bf16[512,512]{1,0:T(8,128)(2,1)S(1)}, u32[]{:S(2)}, u32[]{:S(2)}) collective-permute-start(bf16[512,512]{1,0:T(8,128)(2,1)S(1)} %collective-permute-done.8.refs_0_.refs_3_), channel_id=1, source_target_pairs={{0,2},{2,0},{4,6},{6,4},{8,10},{10,8},{12,14},{14,12},{16,18},{18,... | collective-permute-start | bytes 1572872 | tf_op jit(solution)/shard_map/ppermute | solution.py:308
  36.3 3.4 %collective-permute-start.13 = (bf16[512,512]{1,0:T(8,128)(2,1)S(1)}, bf16[512,512]{1,0:T(8,128)(2,1)S(1)}, u32[]{:S(2)}, u32[]{:S(2)}) collective-permute-start(bf16[512,512]{1,0:T(8,128)(2,1)S(1)} %collective-permute-done.8.refs_0_.refs_3_), channel_id=1, source_target_pairs={{0,4},{1,29},{2,6},{3,31},{4,8},{5,1},{6,10},{7,3},{8,12},{9,5},{1... | collective-permute-start | bytes 1572872 | tf_op jit(solution)/shard_map/ppermute | solution.py:302
  39.7 2.0 %collective-permute-done.9.refs_2_.refs_5_ = bf16[512,512]{1,0:T(8,128)(2,1)S(1)} collective-permute-done((bf16[512,512]{1,0:T(8,128)(2,1)S(1)}, bf16[512,512]{1,0:T(8,128)(2,1)S(1)}, u32[]{:S(2)}, u32[]{:S(2)}) %collective-permute-start.9) | collective-permute-done | bytes 524320 | tf_op jit(solution)/shard_map/ppermute | solution.py:308
  42.4 2.7 %collective-permute-start.4 = (bf16[512,1024]{1,0:T(8,128)(2,1)S(1)}, bf16[512,1024]{1,0:T(8,128)(2,1)S(1)}, u32[]{:S(2)}, u32[]{:S(2)}) collective-permute-start(bf16[512,1024]{1,0:T(8,128)(2,1)S(1)} %collective-permute-done.3.refs_1_), channel_id=1, source_target_pairs={{0,32},{1,97},{32,64},{33,1},{64,96},{65,33},{96,0},{97,65},{128,1... | collective-permute-start | bytes 3145736 | tf_op jit(solution)/shard_map/ppermute | solution.py:311
  46.6 6.3 %collective-permute-done.10.refs_2_.refs_0_ = bf16[512,512]{1,0:T(8,128)(2,1)S(1)} collective-permute-done((bf16[512,512]{1,0:T(8,128)(2,1)S(1)}, bf16[512,512]{1,0:T(8,128)(2,1)S(1)}, u32[]{:S(2)}, u32[]{:S(2)}) %collective-permute-start.10) | collective-permute-done | bytes 524320 | tf_op jit(solution)/shard_map/ppermute | solution.py:308
  53.0 2.7 %collective-permute-start.14 = (bf16[512,512]{1,0:T(8,128)(2,1)S(1)}, bf16[512,512]{1,0:T(8,128)(2,1)S(1)}, u32[]{:S(2)}, u32[]{:S(2)}) collective-permute-start(bf16[512,512]{1,0:T(8,128)(2,1)S(1)} %collective-permute-done.7.refs_1_.refs_4_), channel_id=1, source_target_pairs={{0,2},{2,0},{4,6},{6,4},{8,10},{10,8},{12,14},{14,12},{16,18},{18,... | collective-permute-start | bytes 1572872 | tf_op jit(solution)/shard_map/ppermute | solution.py:308
  57.0 3.4 %collective-permute-start.16 = (bf16[512,512]{1,0:T(8,128)(2,1)S(1)}, bf16[512,512]{1,0:T(8,128)(2,1)S(1)}, u32[]{:S(2)}, u32[]{:S(2)}) collective-permute-start(bf16[512,512]{1,0:T(8,128)(2,1)S(1)} %collective-permute-done.13.refs_6_.refs_0_), channel_id=1, source_target_pairs={{0,4},{1,29},{2,6},{3,31},{4,8},{5,1},{6,10},{7,3},{8,12},{9,5},{1... | collective-permute-start | bytes 1572872 | tf_op jit(solution)/shard_map/ppermute | solution.py:302
  60.5 2.7 %collective-permute-start.5 = (bf16[512,1024]{1,0:T(8,128)(2,1)S(1)}, bf16[512,1024]{1,0:T(8,128)(2,1)S(1)}, u32[]{:S(2)}, u32[]{:S(2)}) collective-permute-start(bf16[512,1024]{1,0:T(8,128)(2,1)S(1)} %collective-permute-done.4.refs_2_), channel_id=1, source_target_pairs={{0,32},{1,97},{32,64},{33,1},{64,96},{65,33},{96,0},{97,65},{128,1... | collective-permute-start | bytes 3145736 | tf_op jit(solution)/shard_map/ppermute | solution.py:311
  64.8 2.4 %collective-permute-done.14.refs_3_.refs_4_ = bf16[512,512]{1,0:T(8,128)(2,1)S(1)} collective-permute-done((bf16[512,512]{1,0:T(8,128)(2,1)S(1)}, bf16[512,512]{1,0:T(8,128)(2,1)S(1)}, u32[]{:S(2)}, u32[]{:S(2)}) %collective-permute-start.14) | collective-permute-done | bytes 524320 | tf_op jit(solution)/shard_map/ppermute | solution.py:308
  67.2 3.6 %collective-permute-done.16.refs_0_.refs_1_ = bf16[512,512]{1,0:T(8,128)(2,1)S(1)} collective-permute-done((bf16[512,512]{1,0:T(8,128)(2,1)S(1)}, bf16[512,512]{1,0:T(8,128)(2,1)S(1)}, u32[]{:S(2)}, u32[]{:S(2)}) %collective-permute-start.16) | collective-permute-done | bytes 524320 | tf_op jit(solution)/shard_map/ppermute | solution.py:302
  71.1 3.9 %collective-permute-done.5.refs_3_ = bf16[512,1024]{1,0:T(8,128)(2,1)S(1)} collective-permute-done((bf16[512,1024]{1,0:T(8,128)(2,1)S(1)}, bf16[512,1024]{1,0:T(8,128)(2,1)S(1)}, u32[]{:S(2)}, u32[]{:S(2)}) %collective-permute-start.5) | collective-permute-done | bytes 1048608 | tf_op jit(solution)/shard_map/ppermute | solution.py:311
  75.2 2.8 %collective-permute-start.6 = (bf16[2048,1024]{1,0:T(8,128)(2,1)S(1)}, bf16[2048,1024]{1,0:T(8,128)(2,1)S(1)}, u32[]{:S(2)}, u32[]{:S(2)}) collective-permute-start(bf16[2048,1024]{1,0:T(8,128)(2,1)S(1)} %shard_map.159.refs_8_), channel_id=1, source_target_pairs={{0,1},{1,0},{2,3},{3,2},{4,5},{5,4},{6,7},{7,6},{8,9},{9,8},{10,11... | collective-permute-start | bytes 12582920 | tf_op jit(solution)/shard_map/ppermute | solution.py:317
  79.8 5.2 %collective-permute-done.17.refs_2_.refs_7_ = bf16[512,512]{1,0:T(8,128)(2,1)S(1)} collective-permute-done((bf16[512,512]{1,0:T(8,128)(2,1)S(1)}, bf16[512,512]{1,0:T(8,128)(2,1)S(1)}, u32[]{:S(2)}, u32[]{:S(2)}) %collective-permute-start.17) | collective-permute-done | bytes 524320 | tf_op jit(solution)/shard_map/ppermute | solution.py:308
  89.0 2.9 %shard_map.162.refs_10_ = f32[2,512,256]{2,1,0:T(8,128)S(1)} custom-call(s32[194]{0:T(256)S(1)} %concatenate.3.table, bf16[512,512]{1,0:T(8,128)(2,1)S(1)} %copy-done.1, bf16[512,512]{1,0:T(8,128)(2,1)S(1)} %collective-permute-done.2.refs_1_, bf16[512,512]{1,0:T(8,128)(2,1)S(1)} %collective-permute-done.1.refs_2_, ...), custom_call_target="tpu_custom_call" | custom-call | tf_op jit(solution)/shard_map/pallas_call | solution.py:260
  94.6 2.4 %collective-permute-start.23 = (bf16[1040,128]{1,0:T(8,128)(2,1)S(1)}, bf16[1040,128]{1,0:T(8,128)(2,1)S(1)}, u32[]{:S(2)}, u32[]{:S(2)}) collective-permute-start(bf16[1040,128]{1,0:T(8,128)(2,1)S(1)} %get-tuple-element.97), channel_id=1, source_target_pairs={{0,96},{32,0},{64,32},{96,64},{128,224},{160,128},{192,160},{224,1... | collective-permute-start | bytes 798728 | tf_op jit(solution)/shard_map/ppermute | solution.py:314
  100.5 2.4 %collective-permute-start.26 = (bf16[1040,128]{1,0:T(8,128)(2,1)S(1)}, bf16[1040,128]{1,0:T(8,128)(2,1)S(1)}, u32[]{:S(2)}, u32[]{:S(2)}) collective-permute-start(bf16[1040,128]{1,0:T(8,128)(2,1)S(1)} %get-tuple-element.107), channel_id=1, source_target_pairs={{0,96},{32,0},{64,32},{96,64},{128,224},{160,128},{192,160},{224,1... | collective-permute-start | bytes 798728 | tf_op jit(solution)/shard_map/ppermute | solution.py:314
  106.2 3.7 %shard_map.171 = bf16[512,512]{1,0:T(8,128)(2,1)} custom-call(s32[194]{0:T(256)S(1)} %concatenate.3.table, bf16[512,512]{1,0:T(8,128)(2,1)S(1)} %collective-permute-done.10.refs_2_.refs_0_, bf16[512,512]{1,0:T(8,128)(2,1)S(1)} %collective-permute-done.16.refs_0_.refs_1_, bf16[512,512]{1,0:T(8,128)(2,1)S(1)} %collective-permute-done.11.refs_1_.refs_2_, ...), custom_call_target="tpu_custom_call" | custom-call | tf_op jit(solution)/shard_map/pallas_call | solution.py:260
  111.5 2.1 %collective-permute-done.28.refs_1_ = bf16[1040,128]{1,0:T(8,128)(2,1)S(1)} collective-permute-done((bf16[1040,128]{1,0:T(8,128)(2,1)S(1)}, bf16[1040,128]{1,0:T(8,128)(2,1)S(1)}, u32[]{:S(2)}, u32[]{:S(2)}) %collective-permute-start.28) | collective-permute-done | bytes 266272 | tf_op jit(solution)/shard_map/ppermute | solution.py:314
  (71 shorter events, 39.0 us)
Async XLA Ops:
  0.7 15.0 %collective-permute-start.1 = (bf16[512,512]{1,0:T(8,128)(2,1)}, bf16[512,512]{1,0:T(8,128)(2,1)S(1)}, u32[]{:S(2)}, u32[]{:S(2)}) collective-permute-start(bf16[512,512]{1,0:T(8,128)(2,1)} %refs_0_.3), channel_id=1, source_target_pairs={{0,28},{1,5},{2,30},{3,7},{4,0},{5,9},{6,2},{7,11},{8,4},{9,13},{1... | collective-permute-start | bytes 1572872 | tf_op jit(solution)/shard_map/ppermute | solution.py:305
  3.2 15.0 %collective-permute-start.2 = (bf16[512,512]{1,0:T(8,128)(2,1)}, bf16[512,512]{1,0:T(8,128)(2,1)S(1)}, u32[]{:S(2)}, u32[]{:S(2)}) collective-permute-start(bf16[512,512]{1,0:T(8,128)(2,1)} %refs_0_.3), channel_id=1, source_target_pairs={{0,4},{1,29},{2,6},{3,31},{4,8},{5,1},{6,10},{7,3},{8,12},{9,5},{1... | collective-permute-start | bytes 1572872 | tf_op jit(solution)/shard_map/ppermute | solution.py:302
  7.3 12.8 %collective-permute-start = (bf16[256,1024]{1,0:T(8,128)(2,1)S(1)}, bf16[256,1024]{1,0:T(8,128)(2,1)}, u32[]{:S(2)}, u32[]{:S(2)}) collective-permute-start(bf16[256,1024]{1,0:T(8,128)(2,1)S(1)} %constant_dynamic-slice_fusion.refs_0_), channel_id=1, source_target_pairs={{0,128},{32,160},{64,192},{96,224},{128,0},{160,32},{192,64},{224,... | collective-permute-start | bytes 1572872 | tf_op jit(solution)/shard_map/ppermute | solution.py:314
  20.0 11.9 %collective-permute-start.7 = (bf16[512,512]{1,0:T(8,128)(2,1)S(1)}, bf16[512,512]{1,0:T(8,128)(2,1)S(1)}, u32[]{:S(2)}, u32[]{:S(2)}) collective-permute-start(bf16[512,512]{1,0:T(8,128)(2,1)S(1)} %collective-permute-done.1.refs_2_), channel_id=1, source_target_pairs={{0,28},{1,5},{2,30},{3,7},{4,0},{5,9},{6,2},{7,11},{8,4},{9,13},{1... | collective-permute-start | bytes 1572872 | tf_op jit(solution)/shard_map/ppermute | solution.py:305
  20.0 13.5 %collective-permute-start.8 = (bf16[512,512]{1,0:T(8,128)(2,1)S(1)}, bf16[512,512]{1,0:T(8,128)(2,1)S(1)}, u32[]{:S(2)}, u32[]{:S(2)}) collective-permute-start(bf16[512,512]{1,0:T(8,128)(2,1)S(1)} %collective-permute-done.2.refs_1_), channel_id=1, source_target_pairs={{0,4},{1,29},{2,6},{3,31},{4,8},{5,1},{6,10},{7,3},{8,12},{9,5},{1... | collective-permute-start | bytes 1572872 | tf_op jit(solution)/shard_map/ppermute | solution.py:302
  23.8 18.5 %collective-permute-start.3 = (bf16[512,1024]{1,0:T(8,128)(2,1)S(1)}, bf16[512,1024]{1,0:T(8,128)(2,1)S(1)}, u32[]{:S(2)}, u32[]{:S(2)}) collective-permute-start(bf16[512,1024]{1,0:T(8,128)(2,1)S(1)} %shard_map.158.refs_0_), channel_id=1, source_target_pairs={{0,32},{1,97},{32,64},{33,1},{64,96},{65,33},{96,0},{97,65},{128,1... | collective-permute-start | bytes 3145736 | tf_op jit(solution)/shard_map/ppermute | solution.py:311
  26.6 15.1 %collective-permute-start.9 = (bf16[512,512]{1,0:T(8,128)(2,1)S(1)}, bf16[512,512]{1,0:T(8,128)(2,1)S(1)}, u32[]{:S(2)}, u32[]{:S(2)}) collective-permute-start(bf16[512,512]{1,0:T(8,128)(2,1)S(1)} %copy-done.1), channel_id=1, source_target_pairs={{0,2},{2,0},{4,6},{6,4},{8,10},{10,8},{12,14},{14,12},{16,18},{18,... | collective-permute-start | bytes 1572872 | tf_op jit(solution)/shard_map/ppermute | solution.py:308
  33.5 19.4 %collective-permute-start.10 = (bf16[512,512]{1,0:T(8,128)(2,1)S(1)}, bf16[512,512]{1,0:T(8,128)(2,1)S(1)}, u32[]{:S(2)}, u32[]{:S(2)}) collective-permute-start(bf16[512,512]{1,0:T(8,128)(2,1)S(1)} %collective-permute-done.8.refs_0_.refs_3_), channel_id=1, source_target_pairs={{0,2},{2,0},{4,6},{6,4},{8,10},{10,8},{12,14},{14,12},{16,18},{18,... | collective-permute-start | bytes 1572872 | tf_op jit(solution)/shard_map/ppermute | solution.py:308
  36.3 19.5 %collective-permute-start.13 = (bf16[512,512]{1,0:T(8,128)(2,1)S(1)}, bf16[512,512]{1,0:T(8,128)(2,1)S(1)}, u32[]{:S(2)}, u32[]{:S(2)}) collective-permute-start(bf16[512,512]{1,0:T(8,128)(2,1)S(1)} %collective-permute-done.8.refs_0_.refs_3_), channel_id=1, source_target_pairs={{0,4},{1,29},{2,6},{3,31},{4,8},{5,1},{6,10},{7,3},{8,12},{9,5},{1... | collective-permute-start | bytes 1572872 | tf_op jit(solution)/shard_map/ppermute | solution.py:302
  39.7 16.0 %collective-permute-start.12 = (bf16[512,512]{1,0:T(8,128)(2,1)S(1)}, bf16[512,512]{1,0:T(8,128)(2,1)S(1)}, u32[]{:S(2)}, u32[]{:S(2)}) collective-permute-start(bf16[512,512]{1,0:T(8,128)(2,1)S(1)} %collective-permute-done.7.refs_1_.refs_4_), channel_id=1, source_target_pairs={{0,28},{1,5},{2,30},{3,7},{4,0},{5,9},{6,2},{7,11},{8,4},{9,13},{1... | collective-permute-start | bytes 1572872 | tf_op jit(solution)/shard_map/ppermute | solution.py:305
  41.7 15.3 %collective-permute-start.11 = (bf16[512,512]{1,0:T(8,128)(2,1)S(1)}, bf16[512,512]{1,0:T(8,128)(2,1)S(1)}, u32[]{:S(2)}, u32[]{:S(2)}) collective-permute-start(bf16[512,512]{1,0:T(8,128)(2,1)S(1)} %collective-permute-done.9.refs_2_.refs_5_), channel_id=1, source_target_pairs={{0,4},{1,29},{2,6},{3,31},{4,8},{5,1},{6,10},{7,3},{8,12},{9,5},{1... | collective-permute-start | bytes 1572872 | tf_op jit(solution)/shard_map/ppermute | solution.py:302
  42.4 18.1 %collective-permute-start.4 = (bf16[512,1024]{1,0:T(8,128)(2,1)S(1)}, bf16[512,1024]{1,0:T(8,128)(2,1)S(1)}, u32[]{:S(2)}, u32[]{:S(2)}) collective-permute-start(bf16[512,1024]{1,0:T(8,128)(2,1)S(1)} %collective-permute-done.3.refs_1_), channel_id=1, source_target_pairs={{0,32},{1,97},{32,64},{33,1},{64,96},{65,33},{96,0},{97,65},{128,1... | collective-permute-start | bytes 3145736 | tf_op jit(solution)/shard_map/ppermute | solution.py:311
  53.0 14.2 %collective-permute-start.14 = (bf16[512,512]{1,0:T(8,128)(2,1)S(1)}, bf16[512,512]{1,0:T(8,128)(2,1)S(1)}, u32[]{:S(2)}, u32[]{:S(2)}) collective-permute-start(bf16[512,512]{1,0:T(8,128)(2,1)S(1)} %collective-permute-done.7.refs_1_.refs_4_), channel_id=1, source_target_pairs={{0,2},{2,0},{4,6},{6,4},{8,10},{10,8},{12,14},{14,12},{16,18},{18,... | collective-permute-start | bytes 1572872 | tf_op jit(solution)/shard_map/ppermute | solution.py:308
  55.7 11.5 %collective-permute-start.15 = (bf16[512,512]{1,0:T(8,128)(2,1)S(1)}, bf16[512,512]{1,0:T(8,128)(2,1)S(1)}, u32[]{:S(2)}, u32[]{:S(2)}) collective-permute-start(bf16[512,512]{1,0:T(8,128)(2,1)S(1)} %collective-permute-done.9.refs_2_.refs_5_), channel_id=1, source_target_pairs={{0,28},{1,5},{2,30},{3,7},{4,0},{5,9},{6,2},{7,11},{8,4},{9,13},{1... | collective-permute-start | bytes 1572872 | tf_op jit(solution)/shard_map/ppermute | solution.py:305
  57.0 13.8 %collective-permute-start.16 = (bf16[512,512]{1,0:T(8,128)(2,1)S(1)}, bf16[512,512]{1,0:T(8,128)(2,1)S(1)}, u32[]{:S(2)}, u32[]{:S(2)}) collective-permute-start(bf16[512,512]{1,0:T(8,128)(2,1)S(1)} %collective-permute-done.13.refs_6_.refs_0_), channel_id=1, source_target_pairs={{0,4},{1,29},{2,6},{3,31},{4,8},{5,1},{6,10},{7,3},{8,12},{9,5},{1... | collective-permute-start | bytes 1572872 | tf_op jit(solution)/shard_map/ppermute | solution.py:302
  60.5 19.4 %collective-permute-start.19 = (bf16[512,512]{1,0:T(8,128)(2,1)S(1)}, bf16[512,512]{1,0:T(8,128)(2,1)S(1)}, u32[]{:S(2)}, u32[]{:S(2)}) collective-permute-start(bf16[512,512]{1,0:T(8,128)(2,1)S(1)} %collective-permute-done.10.refs_2_.refs_0_), channel_id=1, source_target_pairs={{0,4},{1,29},{2,6},{3,31},{4,8},{5,1},{6,10},{7,3},{8,12},{9,5},{1... | collective-permute-start | bytes 1572872 | tf_op jit(solution)/shard_map/ppermute | solution.py:302
  60.5 14.5 %collective-permute-start.5 = (bf16[512,1024]{1,0:T(8,128)(2,1)S(1)}, bf16[512,1024]{1,0:T(8,128)(2,1)S(1)}, u32[]{:S(2)}, u32[]{:S(2)}) collective-permute-start(bf16[512,1024]{1,0:T(8,128)(2,1)S(1)} %collective-permute-done.4.refs_2_), channel_id=1, source_target_pairs={{0,32},{1,97},{32,64},{33,1},{64,96},{65,33},{96,0},{97,65},{128,1... | collective-permute-start | bytes 3145736 | tf_op jit(solution)/shard_map/ppermute | solution.py:311
  70.8 14.3 %collective-permute-start.17 = (bf16[512,512]{1,0:T(8,128)(2,1)S(1)}, bf16[512,512]{1,0:T(8,128)(2,1)S(1)}, u32[]{:S(2)}, u32[]{:S(2)}) collective-permute-start(bf16[512,512]{1,0:T(8,128)(2,1)S(1)} %collective-permute-done.16.refs_0_.refs_1_), channel_id=1, source_target_pairs={{0,2},{2,0},{4,6},{6,4},{8,10},{10,8},{12,14},{14,12},{16,18},{18,... | collective-permute-start | bytes 1572872 | tf_op jit(solution)/shard_map/ppermute | solution.py:308
  71.1 14.0 %collective-permute-start.18 = (bf16[512,512]{1,0:T(8,128)(2,1)S(1)}, bf16[512,512]{1,0:T(8,128)(2,1)S(1)}, u32[]{:S(2)}, u32[]{:S(2)}) collective-permute-start(bf16[512,512]{1,0:T(8,128)(2,1)S(1)} %collective-permute-done.14.refs_3_.refs_4_), channel_id=1, source_target_pairs={{0,28},{1,5},{2,30},{3,7},{4,0},{5,9},{6,2},{7,11},{8,4},{9,13},{1... | collective-permute-start | bytes 1572872 | tf_op jit(solution)/shard_map/ppermute | solution.py:305
  75.2 11.4 %collective-permute-start.6 = (bf16[2048,1024]{1,0:T(8,128)(2,1)S(1)}, bf16[2048,1024]{1,0:T(8,128)(2,1)S(1)}, u32[]{:S(2)}, u32[]{:S(2)}) collective-permute-start(bf16[2048,1024]{1,0:T(8,128)(2,1)S(1)} %shard_map.159.refs_8_), channel_id=1, source_target_pairs={{0,1},{1,0},{2,3},{3,2},{4,5},{5,4},{6,7},{7,6},{8,9},{9,8},{10,11... | collective-permute-start | bytes 12582920 | tf_op jit(solution)/shard_map/ppermute | solution.py:317
  94.3 9.1 %collective-permute-start.22 = (bf16[1040,128]{1,0:T(8,128)(2,1)S(1)}, bf16[1040,128]{1,0:T(8,128)(2,1)S(1)}, u32[]{:S(2)}, u32[]{:S(2)}) collective-permute-start(bf16[1040,128]{1,0:T(8,128)(2,1)S(1)} %get-tuple-element.96), channel_id=1, source_target_pairs={{0,32},{32,64},{64,96},{96,0},{128,160},{160,192},{192,224},{224,1... | collective-permute-start | bytes 798728 | tf_op jit(solution)/shard_map/ppermute | solution.py:314
  94.6 8.8 %collective-permute-start.23 = (bf16[1040,128]{1,0:T(8,128)(2,1)S(1)}, bf16[1040,128]{1,0:T(8,128)(2,1)S(1)}, u32[]{:S(2)}, u32[]{:S(2)}) collective-permute-start(bf16[1040,128]{1,0:T(8,128)(2,1)S(1)} %get-tuple-element.97), channel_id=1, source_target_pairs={{0,96},{32,0},{64,32},{96,64},{128,224},{160,128},{192,160},{224,1... | collective-permute-start | bytes 798728 | tf_op jit(solution)/shard_map/ppermute | solution.py:314
  99.9 10.1 %collective-permute-start.25 = (bf16[1040,128]{1,0:T(8,128)(2,1)S(1)}, bf16[1040,128]{1,0:T(8,128)(2,1)S(1)}, u32[]{:S(2)}, u32[]{:S(2)}) collective-permute-start(bf16[1040,128]{1,0:T(8,128)(2,1)S(1)} %get-tuple-element.106), channel_id=1, source_target_pairs={{0,32},{32,64},{64,96},{96,0},{128,160},{160,192},{192,224},{224,1... | collective-permute-start | bytes 798728 | tf_op jit(solution)/shard_map/ppermute | solution.py:314
  100.5 9.5 %collective-permute-start.26 = (bf16[1040,128]{1,0:T(8,128)(2,1)S(1)}, bf16[1040,128]{1,0:T(8,128)(2,1)S(1)}, u32[]{:S(2)}, u32[]{:S(2)}) collective-permute-start(bf16[1040,128]{1,0:T(8,128)(2,1)S(1)} %get-tuple-element.107), channel_id=1, source_target_pairs={{0,96},{32,0},{64,32},{96,64},{128,224},{160,128},{192,160},{224,1... | collective-permute-start | bytes 798728 | tf_op jit(solution)/shard_map/ppermute | solution.py:314
  (9 other events, 78.3 us)

commit v8 on v7

--- a/solution.py
+++ b/solution.py
@@ -380,11 +380,12 @@
     theirs, early_table = together((theirs, table))
     parts = [mine, theirs]
     other_early = to_core(pick(early_table, 0, EARLY, total))
-    first_half = grad_sum(early_table, range(8), cols[:8], parts)
-    first_half, early_table = together((first_half, early_table))
+    picked_late = pick(early_table, EARLY, 8, total)
+    first_half = grad_sum(early_table, range(5), cols[:5], parts)
+    first_half, picked_late, early_table = together((first_half, picked_late, early_table))
     early = code(early_table, 0, EARLY, total, other_early, 0)
-    *early, late_table = together((*early, table))
-    other_late = to_core(pick(late_table, EARLY, 8, total))
+    *early, picked_late, late_table = together((*early, picked_late, table))
+    other_late = to_core(picked_late)
     late = code(late_table, EARLY, 8, total, other_late, 3)
     next_y, last_y, beside, opposite, own = late
 
@@ -394,7 +395,7 @@
     beside, opposite = relay([(beside, [ups, downs]), (opposite, [cross])])
     beside, opposite, grad_table = together((beside, opposite, late_table))
     far = [to_row(beside, 1, 0), to_row(opposite, 0, 2)]
-    grad_in = grad_sum(grad_table, range(8, 16), cols[8:], parts, first_half)
+    grad_in = grad_sum(grad_table, range(5, 16), cols[5:], parts, first_half)
     own, grad_in = together((own, grad_in))
     pushed = add_coded(own, near)
     pushed = add_coded(pushed, far)

time: 116 us -> 116 us (level)
  transfers between devices with their start and end apart: 29 -> 29, of which waited for: 17 -> 17; matrix products, arithmetic and copies ran while one was open for 6% -> 6% of each run, Pallas kernels for 16% -> 17%
where the time goes in v8:
time: 116 us; the launch traced here: 114 us
  starting transfers between devices  46.7 us (40%)
  waiting for transfers between devices  36.3 us (31%)
  Pallas kernels  22.3 us (19%)
  other arithmetic  4.67 us (4%)
  local copies, waits for them, and re-layouts  3.23 us (3%)
    ppermute x4, waiting for transfers between devices, across(): return lax.ppermute(v, 'col', X_SWAP)  16.1 us
    ppermute x6, starting transfers between devices, ahead(): return lax.ppermute(v, ('col', 'srv'), z_shift(1))  14.1 us
    ppermute x6, waiting for transfers between devices, ahead(): return lax.ppermute(v, ('col', 'srv'), z_shift(1))  8.84 us
    ppermute x4, starting transfers between devices, across(): return lax.ppermute(v, 'col', X_SWAP)  8.46 us
    ppermute x3, starting transfers between devices, around(): return lax.ppermute(v, ('row', 'srv'), y_shift(1))  8.28 us
    ppermute x8, starting transfers between devices, to_row(): return lax.ppermute(v, 'row', row_shift(dx, dy))  8.21 us
    pallas_call x5, Pallas kernels, dense(): pl.pallas_call(functools.partial(dense_kernel, count, place, first), out_...  7.9 us
    pallas_call x2, Pallas kernels, grad_sum(): pl.pallas_call(functools.partial(grad_kernel, tuple(ids), last), out_shap...  6.66 us
  transfers between devices with their start and end apart: 29, of which 17 were waited for; matrix products, arithmetic and copies ran while one was open for 6% of the time, Pallas kernels for 17%

profile of v8, /device:TPU:1, one launch (start us, length us, event | category | flops | bytes accessed | tf_op | source)
XLA Modules:
  0.0 113.9 jit_solution(11858954037061212438)
XLA Ops:
  0.7 2.5 %collective-permute-start.1 = (bf16[512,512]{1,0:T(8,128)(2,1)}, bf16[512,512]{1,0:T(8,128)(2,1)S(1)}, u32[]{:S(2)}, u32[]{:S(2)}) collective-permute-start(bf16[512,512]{1,0:T(8,128)(2,1)} %refs_0_.3), channel_id=1, source_target_pairs={{0,28},{1,5},{2,30},{3,7},{4,0},{5,9},{6,2},{7,11},{8,4},{9,13},{1... | collective-permute-start | bytes 1572872 | tf_op jit(solution)/shard_map/ppermute | solution.py:305
  3.2 4.0 %collective-permute-start.2 = (bf16[512,512]{1,0:T(8,128)(2,1)}, bf16[512,512]{1,0:T(8,128)(2,1)S(1)}, u32[]{:S(2)}, u32[]{:S(2)}) collective-permute-start(bf16[512,512]{1,0:T(8,128)(2,1)} %refs_0_.3), channel_id=1, source_target_pairs={{0,4},{1,29},{2,6},{3,31},{4,8},{5,1},{6,10},{7,3},{8,12},{9,5},{1... | collective-permute-start | bytes 1572872 | tf_op jit(solution)/shard_map/ppermute | solution.py:302
  11.6 2.0 %copy.22 = bf16[512,512]{0,1:T(8,128)(2,1)} copy(bf16[512,512]{1,0:T(8,128)(2,1)} %param.15) | data formatting | bytes 1048576 | tf_op args[0]
  15.7 2.6 %collective-permute-done.2.refs_1_ = bf16[512,512]{1,0:T(8,128)(2,1)S(1)} collective-permute-done((bf16[512,512]{1,0:T(8,128)(2,1)}, bf16[512,512]{1,0:T(8,128)(2,1)S(1)}, u32[]{:S(2)}, u32[]{:S(2)}) %collective-permute-start.2) | collective-permute-done | bytes 524320 | tf_op jit(solution)/shard_map/ppermute | solution.py:302
  20.0 2.7 %collective-permute-start.8 = (bf16[512,512]{1,0:T(8,128)(2,1)S(1)}, bf16[512,512]{1,0:T(8,128)(2,1)S(1)}, u32[]{:S(2)}, u32[]{:S(2)}) collective-permute-start(bf16[512,512]{1,0:T(8,128)(2,1)S(1)} %collective-permute-done.2.refs_1_), channel_id=1, source_target_pairs={{0,4},{1,29},{2,6},{3,31},{4,8},{5,1},{6,10},{7,3},{8,12},{9,5},{1... | collective-permute-start | bytes 1572872 | tf_op jit(solution)/shard_map/ppermute | solution.py:302
  23.9 2.8 %collective-permute-start.3 = (bf16[512,1024]{1,0:T(8,128)(2,1)S(1)}, bf16[512,1024]{1,0:T(8,128)(2,1)S(1)}, u32[]{:S(2)}, u32[]{:S(2)}) collective-permute-start(bf16[512,1024]{1,0:T(8,128)(2,1)S(1)} %shard_map.158.refs_0_), channel_id=1, source_target_pairs={{0,32},{1,97},{32,64},{33,1},{64,96},{65,33},{96,0},{97,65},{128,1... | collective-permute-start | bytes 3145736 | tf_op jit(solution)/shard_map/ppermute | solution.py:311
  26.7 2.7 %collective-permute-start.10 = (bf16[512,512]{1,0:T(8,128)(2,1)S(1)}, bf16[512,512]{1,0:T(8,128)(2,1)S(1)}, u32[]{:S(2)}, u32[]{:S(2)}) collective-permute-start(bf16[512,512]{1,0:T(8,128)(2,1)S(1)} %copy-done.1), channel_id=1, source_target_pairs={{0,2},{2,0},{4,6},{6,4},{8,10},{10,8},{12,14},{14,12},{16,18},{18,... | collective-permute-start | bytes 1572872 | tf_op jit(solution)/shard_map/ppermute | solution.py:308
  33.5 2.7 %collective-permute-start.12 = (bf16[512,512]{1,0:T(8,128)(2,1)S(1)}, bf16[512,512]{1,0:T(8,128)(2,1)S(1)}, u32[]{:S(2)}, u32[]{:S(2)}) collective-permute-start(bf16[512,512]{1,0:T(8,128)(2,1)S(1)} %collective-permute-done.8.refs_3_.refs_0_), channel_id=1, source_target_pairs={{0,2},{2,0},{4,6},{6,4},{8,10},{10,8},{12,14},{14,12},{16,18},{18,... | collective-permute-start | bytes 1572872 | tf_op jit(solution)/shard_map/ppermute | solution.py:308
  36.3 3.4 %collective-permute-start.15 = (bf16[512,512]{1,0:T(8,128)(2,1)S(1)}, bf16[512,512]{1,0:T(8,128)(2,1)S(1)}, u32[]{:S(2)}, u32[]{:S(2)}) collective-permute-start(bf16[512,512]{1,0:T(8,128)(2,1)S(1)} %collective-permute-done.8.refs_3_.refs_0_), channel_id=1, source_target_pairs={{0,4},{1,29},{2,6},{3,31},{4,8},{5,1},{6,10},{7,3},{8,12},{9,5},{1... | collective-permute-start | bytes 1572872 | tf_op jit(solution)/shard_map/ppermute | solution.py:302
  39.7 2.1 %collective-permute-done.10.refs_2_.refs_0_ = bf16[512,512]{1,0:T(8,128)(2,1)S(1)} collective-permute-done((bf16[512,512]{1,0:T(8,128)(2,1)S(1)}, bf16[512,512]{1,0:T(8,128)(2,1)S(1)}, u32[]{:S(2)}, u32[]{:S(2)}) %collective-permute-start.10) | collective-permute-done | bytes 524320 | tf_op jit(solution)/shard_map/ppermute | solution.py:308
  42.4 2.7 %collective-permute-start.4 = (bf16[512,1024]{1,0:T(8,128)(2,1)S(1)}, bf16[512,1024]{1,0:T(8,128)(2,1)S(1)}, u32[]{:S(2)}, u32[]{:S(2)}) collective-permute-start(bf16[512,1024]{1,0:T(8,128)(2,1)S(1)} %collective-permute-done.3.refs_1_), channel_id=1, source_target_pairs={{0,32},{1,97},{32,64},{33,1},{64,96},{65,33},{96,0},{97,65},{128,1... | collective-permute-start | bytes 3145736 | tf_op jit(solution)/shard_map/ppermute | solution.py:311
  46.6 6.4 %collective-permute-done.12.refs_2_.refs_3_ = bf16[512,512]{1,0:T(8,128)(2,1)S(1)} collective-permute-done((bf16[512,512]{1,0:T(8,128)(2,1)S(1)}, bf16[512,512]{1,0:T(8,128)(2,1)S(1)}, u32[]{:S(2)}, u32[]{:S(2)}) %collective-permute-start.12) | collective-permute-done | bytes 524320 | tf_op jit(solution)/shard_map/ppermute | solution.py:308
  53.0 2.7 %collective-permute-start.9 = (bf16[512,512]{1,0:T(8,128)(2,1)S(1)}, bf16[512,512]{1,0:T(8,128)(2,1)S(1)}, u32[]{:S(2)}, u32[]{:S(2)}) collective-permute-start(bf16[512,512]{1,0:T(8,128)(2,1)S(1)} %collective-permute-done.7.refs_4_.refs_1_), channel_id=1, source_target_pairs={{0,2},{2,0},{4,6},{6,4},{8,10},{10,8},{12,14},{14,12},{16,18},{18,... | collective-permute-start | bytes 1572872 | tf_op jit(solution)/shard_map/ppermute | solution.py:308
  57.0 3.4 %collective-permute-start.16 = (bf16[512,512]{1,0:T(8,128)(2,1)S(1)}, bf16[512,512]{1,0:T(8,128)(2,1)S(1)}, u32[]{:S(2)}, u32[]{:S(2)}) collective-permute-start(bf16[512,512]{1,0:T(8,128)(2,1)S(1)} %collective-permute-done.15.refs_0_.refs_1_), channel_id=1, source_target_pairs={{0,4},{1,29},{2,6},{3,31},{4,8},{5,1},{6,10},{7,3},{8,12},{9,5},{1... | collective-permute-start | bytes 1572872 | tf_op jit(solution)/shard_map/ppermute | solution.py:302
  60.5 2.7 %collective-permute-start.5 = (bf16[512,1024]{1,0:T(8,128)(2,1)S(1)}, bf16[512,1024]{1,0:T(8,128)(2,1)S(1)}, u32[]{:S(2)}, u32[]{:S(2)}) collective-permute-start(bf16[512,1024]{1,0:T(8,128)(2,1)S(1)} %collective-permute-done.4.refs_2_), channel_id=1, source_target_pairs={{0,32},{1,97},{32,64},{33,1},{64,96},{65,33},{96,0},{97,65},{128,1... | collective-permute-start | bytes 3145736 | tf_op jit(solution)/shard_map/ppermute | solution.py:311
  64.8 2.5 %collective-permute-done.9.refs_3_.refs_7_ = bf16[512,512]{1,0:T(8,128)(2,1)S(1)} collective-permute-done((bf16[512,512]{1,0:T(8,128)(2,1)S(1)}, bf16[512,512]{1,0:T(8,128)(2,1)S(1)}, u32[]{:S(2)}, u32[]{:S(2)}) %collective-permute-start.9) | collective-permute-done | bytes 524320 | tf_op jit(solution)/shard_map/ppermute | solution.py:308
  67.3 3.5 %collective-permute-done.16.refs_0_.refs_4_ = bf16[512,512]{1,0:T(8,128)(2,1)S(1)} collective-permute-done((bf16[512,512]{1,0:T(8,128)(2,1)S(1)}, bf16[512,512]{1,0:T(8,128)(2,1)S(1)}, u32[]{:S(2)}, u32[]{:S(2)}) %collective-permute-start.16) | collective-permute-done | bytes 524320 | tf_op jit(solution)/shard_map/ppermute | solution.py:302
  71.0 4.0 %collective-permute-done.5.refs_3_ = bf16[512,1024]{1,0:T(8,128)(2,1)S(1)} collective-permute-done((bf16[512,1024]{1,0:T(8,128)(2,1)S(1)}, bf16[512,1024]{1,0:T(8,128)(2,1)S(1)}, u32[]{:S(2)}, u32[]{:S(2)}) %collective-permute-start.5) | collective-permute-done | bytes 1048608 | tf_op jit(solution)/shard_map/ppermute | solution.py:311
  75.2 2.8 %collective-permute-start.6 = (bf16[2048,1024]{1,0:T(8,128)(2,1)S(1)}, bf16[2048,1024]{1,0:T(8,128)(2,1)S(1)}, u32[]{:S(2)}, u32[]{:S(2)}) collective-permute-start(bf16[2048,1024]{1,0:T(8,128)(2,1)S(1)} %shard_map.159.refs_5_.refs_11_), channel_id=1, source_target_pairs={{0,1},{1,0},{2,3},{3,2},{4,5},{5,4},{6,7},{7,6},{8,9},{9,8},{10,11... | collective-permute-start | bytes 12582920 | tf_op jit(solution)/shard_map/ppermute | solution.py:317
  79.8 5.1 %collective-permute-done.17.refs_2_.refs_10_ = bf16[512,512]{1,0:T(8,128)(2,1)S(1)} collective-permute-done((bf16[512,512]{1,0:T(8,128)(2,1)S(1)}, bf16[512,512]{1,0:T(8,128)(2,1)S(1)}, u32[]{:S(2)}, u32[]{:S(2)}) %collective-permute-start.17) | collective-permute-done | bytes 524320 | tf_op jit(solution)/shard_map/ppermute | solution.py:308
  89.6 2.1 %shard_map.161.refs_13_ = f32[2,512,256]{2,1,0:T(8,128)S(1)} custom-call(s32[194]{0:T(256)S(1)} %concatenate.3.table, bf16[512,512]{1,0:T(8,128)(2,1)S(1)} %copy-done.1, bf16[512,512]{1,0:T(8,128)(2,1)S(1)} %collective-permute-done.2.refs_1_, bf16[512,512]{1,0:T(8,128)(2,1)S(1)} %collective-permute-done.1.refs_2_, ...), custom_call_target="tpu_custom_call" | custom-call | tf_op jit(solution)/shard_map/pallas_call | solution.py:260
  93.9 2.3 %collective-permute-start.23 = (bf16[1040,128]{1,0:T(8,128)(2,1)S(1)}, bf16[1040,128]{1,0:T(8,128)(2,1)S(1)}, u32[]{:S(2)}, u32[]{:S(2)}) collective-permute-start(bf16[1040,128]{1,0:T(8,128)(2,1)S(1)} %get-tuple-element.101), channel_id=1, source_target_pairs={{0,96},{32,0},{64,32},{96,64},{128,224},{160,128},{192,160},{224,1... | collective-permute-start | bytes 798728 | tf_op jit(solution)/shard_map/ppermute | solution.py:314
  99.6 2.3 %collective-permute-start.26 = (bf16[1040,128]{1,0:T(8,128)(2,1)S(1)}, bf16[1040,128]{1,0:T(8,128)(2,1)S(1)}, u32[]{:S(2)}, u32[]{:S(2)}) collective-permute-start(bf16[1040,128]{1,0:T(8,128)(2,1)S(1)} %get-tuple-element.111), channel_id=1, source_target_pairs={{0,96},{32,0},{64,32},{96,64},{128,224},{160,128},{192,160},{224,1... | collective-permute-start | bytes 798728 | tf_op jit(solution)/shard_map/ppermute | solution.py:314
  105.6 4.5 %shard_map.171 = bf16[512,512]{1,0:T(8,128)(2,1)} custom-call(s32[194]{0:T(256)S(1)} %concatenate.3.table, bf16[512,512]{1,0:T(8,128)(2,1)S(1)} %collective-permute-done.10.refs_2_.refs_0_, bf16[512,512]{1,0:T(8,128)(2,1)S(1)} %collective-permute-done.15.refs_0_.refs_1_, bf16[512,512]{1,0:T(8,128)(2,1)S(1)} %collective-permute-done.14.refs_1_.refs_2_, ...), custom_call_target="tpu_custom_call" | custom-call | tf_op jit(solution)/shard_map/pallas_call | solution.py:260
  (71 shorter events, 38.3 us)
Async XLA Ops:
  0.7 15.0 %collective-permute-start.1 = (bf16[512,512]{1,0:T(8,128)(2,1)}, bf16[512,512]{1,0:T(8,128)(2,1)S(1)}, u32[]{:S(2)}, u32[]{:S(2)}) collective-permute-start(bf16[512,512]{1,0:T(8,128)(2,1)} %refs_0_.3), channel_id=1, source_target_pairs={{0,28},{1,5},{2,30},{3,7},{4,0},{5,9},{6,2},{7,11},{8,4},{9,13},{1... | collective-permute-start | bytes 1572872 | tf_op jit(solution)/shard_map/ppermute | solution.py:305
  3.2 15.0 %collective-permute-start.2 = (bf16[512,512]{1,0:T(8,128)(2,1)}, bf16[512,512]{1,0:T(8,128)(2,1)S(1)}, u32[]{:S(2)}, u32[]{:S(2)}) collective-permute-start(bf16[512,512]{1,0:T(8,128)(2,1)} %refs_0_.3), channel_id=1, source_target_pairs={{0,4},{1,29},{2,6},{3,31},{4,8},{5,1},{6,10},{7,3},{8,12},{9,5},{1... | collective-permute-start | bytes 1572872 | tf_op jit(solution)/shard_map/ppermute | solution.py:302
  7.3 12.8 %collective-permute-start = (bf16[256,1024]{1,0:T(8,128)(2,1)S(1)}, bf16[256,1024]{1,0:T(8,128)(2,1)}, u32[]{:S(2)}, u32[]{:S(2)}) collective-permute-start(bf16[256,1024]{1,0:T(8,128)(2,1)S(1)} %constant_dynamic-slice_fusion.refs_0_), channel_id=1, source_target_pairs={{0,128},{32,160},{64,192},{96,224},{128,0},{160,32},{192,64},{224,... | collective-permute-start | bytes 1572872 | tf_op jit(solution)/shard_map/ppermute | solution.py:314
  20.0 12.0 %collective-permute-start.7 = (bf16[512,512]{1,0:T(8,128)(2,1)S(1)}, bf16[512,512]{1,0:T(8,128)(2,1)S(1)}, u32[]{:S(2)}, u32[]{:S(2)}) collective-permute-start(bf16[512,512]{1,0:T(8,128)(2,1)S(1)} %collective-permute-done.1.refs_2_), channel_id=1, source_target_pairs={{0,28},{1,5},{2,30},{3,7},{4,0},{5,9},{6,2},{7,11},{8,4},{9,13},{1... | collective-permute-start | bytes 1572872 | tf_op jit(solution)/shard_map/ppermute | solution.py:305
  20.0 13.5 %collective-permute-start.8 = (bf16[512,512]{1,0:T(8,128)(2,1)S(1)}, bf16[512,512]{1,0:T(8,128)(2,1)S(1)}, u32[]{:S(2)}, u32[]{:S(2)}) collective-permute-start(bf16[512,512]{1,0:T(8,128)(2,1)S(1)} %collective-permute-done.2.refs_1_), channel_id=1, source_target_pairs={{0,4},{1,29},{2,6},{3,31},{4,8},{5,1},{6,10},{7,3},{8,12},{9,5},{1... | collective-permute-start | bytes 1572872 | tf_op jit(solution)/shard_map/ppermute | solution.py:302
  23.9 18.5 %collective-permute-start.3 = (bf16[512,1024]{1,0:T(8,128)(2,1)S(1)}, bf16[512,1024]{1,0:T(8,128)(2,1)S(1)}, u32[]{:S(2)}, u32[]{:S(2)}) collective-permute-start(bf16[512,1024]{1,0:T(8,128)(2,1)S(1)} %shard_map.158.refs_0_), channel_id=1, source_target_pairs={{0,32},{1,97},{32,64},{33,1},{64,96},{65,33},{96,0},{97,65},{128,1... | collective-permute-start | bytes 3145736 | tf_op jit(solution)/shard_map/ppermute | solution.py:311
  26.7 15.1 %collective-permute-start.10 = (bf16[512,512]{1,0:T(8,128)(2,1)S(1)}, bf16[512,512]{1,0:T(8,128)(2,1)S(1)}, u32[]{:S(2)}, u32[]{:S(2)}) collective-permute-start(bf16[512,512]{1,0:T(8,128)(2,1)S(1)} %copy-done.1), channel_id=1, source_target_pairs={{0,2},{2,0},{4,6},{6,4},{8,10},{10,8},{12,14},{14,12},{16,18},{18,... | collective-permute-start | bytes 1572872 | tf_op jit(solution)/shard_map/ppermute | solution.py:308
  33.5 19.5 %collective-permute-start.12 = (bf16[512,512]{1,0:T(8,128)(2,1)S(1)}, bf16[512,512]{1,0:T(8,128)(2,1)S(1)}, u32[]{:S(2)}, u32[]{:S(2)}) collective-permute-start(bf16[512,512]{1,0:T(8,128)(2,1)S(1)} %collective-permute-done.8.refs_3_.refs_0_), channel_id=1, source_target_pairs={{0,2},{2,0},{4,6},{6,4},{8,10},{10,8},{12,14},{14,12},{16,18},{18,... | collective-permute-start | bytes 1572872 | tf_op jit(solution)/shard_map/ppermute | solution.py:308
  36.3 19.5 %collective-permute-start.15 = (bf16[512,512]{1,0:T(8,128)(2,1)S(1)}, bf16[512,512]{1,0:T(8,128)(2,1)S(1)}, u32[]{:S(2)}, u32[]{:S(2)}) collective-permute-start(bf16[512,512]{1,0:T(8,128)(2,1)S(1)} %collective-permute-done.8.refs_3_.refs_0_), channel_id=1, source_target_pairs={{0,4},{1,29},{2,6},{3,31},{4,8},{5,1},{6,10},{7,3},{8,12},{9,5},{1... | collective-permute-start | bytes 1572872 | tf_op jit(solution)/shard_map/ppermute | solution.py:302
  39.7 16.1 %collective-permute-start.14 = (bf16[512,512]{1,0:T(8,128)(2,1)S(1)}, bf16[512,512]{1,0:T(8,128)(2,1)S(1)}, u32[]{:S(2)}, u32[]{:S(2)}) collective-permute-start(bf16[512,512]{1,0:T(8,128)(2,1)S(1)} %collective-permute-done.7.refs_4_.refs_1_), channel_id=1, source_target_pairs={{0,28},{1,5},{2,30},{3,7},{4,0},{5,9},{6,2},{7,11},{8,4},{9,13},{1... | collective-permute-start | bytes 1572872 | tf_op jit(solution)/shard_map/ppermute | solution.py:305
  41.8 15.2 %collective-permute-start.13 = (bf16[512,512]{1,0:T(8,128)(2,1)S(1)}, bf16[512,512]{1,0:T(8,128)(2,1)S(1)}, u32[]{:S(2)}, u32[]{:S(2)}) collective-permute-start(bf16[512,512]{1,0:T(8,128)(2,1)S(1)} %collective-permute-done.10.refs_2_.refs_0_), channel_id=1, source_target_pairs={{0,4},{1,29},{2,6},{3,31},{4,8},{5,1},{6,10},{7,3},{8,12},{9,5},{1... | collective-permute-start | bytes 1572872 | tf_op jit(solution)/shard_map/ppermute | solution.py:302
  42.4 18.1 %collective-permute-start.4 = (bf16[512,1024]{1,0:T(8,128)(2,1)S(1)}, bf16[512,1024]{1,0:T(8,128)(2,1)S(1)}, u32[]{:S(2)}, u32[]{:S(2)}) collective-permute-start(bf16[512,1024]{1,0:T(8,128)(2,1)S(1)} %collective-permute-done.3.refs_1_), channel_id=1, source_target_pairs={{0,32},{1,97},{32,64},{33,1},{64,96},{65,33},{96,0},{97,65},{128,1... | collective-permute-start | bytes 3145736 | tf_op jit(solution)/shard_map/ppermute | solution.py:311
  53.0 14.2 %collective-permute-start.9 = (bf16[512,512]{1,0:T(8,128)(2,1)S(1)}, bf16[512,512]{1,0:T(8,128)(2,1)S(1)}, u32[]{:S(2)}, u32[]{:S(2)}) collective-permute-start(bf16[512,512]{1,0:T(8,128)(2,1)S(1)} %collective-permute-done.7.refs_4_.refs_1_), channel_id=1, source_target_pairs={{0,2},{2,0},{4,6},{6,4},{8,10},{10,8},{12,14},{14,12},{16,18},{18,... | collective-permute-start | bytes 1572872 | tf_op jit(solution)/shard_map/ppermute | solution.py:308
  55.8 11.5 %collective-permute-start.11 = (bf16[512,512]{1,0:T(8,128)(2,1)S(1)}, bf16[512,512]{1,0:T(8,128)(2,1)S(1)}, u32[]{:S(2)}, u32[]{:S(2)}) collective-permute-start(bf16[512,512]{1,0:T(8,128)(2,1)S(1)} %collective-permute-done.10.refs_2_.refs_0_), channel_id=1, source_target_pairs={{0,28},{1,5},{2,30},{3,7},{4,0},{5,9},{6,2},{7,11},{8,4},{9,13},{1... | collective-permute-start | bytes 1572872 | tf_op jit(solution)/shard_map/ppermute | solution.py:305
  57.0 13.7 %collective-permute-start.16 = (bf16[512,512]{1,0:T(8,128)(2,1)S(1)}, bf16[512,512]{1,0:T(8,128)(2,1)S(1)}, u32[]{:S(2)}, u32[]{:S(2)}) collective-permute-start(bf16[512,512]{1,0:T(8,128)(2,1)S(1)} %collective-permute-done.15.refs_0_.refs_1_), channel_id=1, source_target_pairs={{0,4},{1,29},{2,6},{3,31},{4,8},{5,1},{6,10},{7,3},{8,12},{9,5},{1... | collective-permute-start | bytes 1572872 | tf_op jit(solution)/shard_map/ppermute | solution.py:302
  60.5 19.4 %collective-permute-start.19 = (bf16[512,512]{1,0:T(8,128)(2,1)S(1)}, bf16[512,512]{1,0:T(8,128)(2,1)S(1)}, u32[]{:S(2)}, u32[]{:S(2)}) collective-permute-start(bf16[512,512]{1,0:T(8,128)(2,1)S(1)} %collective-permute-done.12.refs_2_.refs_3_), channel_id=1, source_target_pairs={{0,4},{1,29},{2,6},{3,31},{4,8},{5,1},{6,10},{7,3},{8,12},{9,5},{1... | collective-permute-start | bytes 1572872 | tf_op jit(solution)/shard_map/ppermute | solution.py:302
  60.5 14.5 %collective-permute-start.5 = (bf16[512,1024]{1,0:T(8,128)(2,1)S(1)}, bf16[512,1024]{1,0:T(8,128)(2,1)S(1)}, u32[]{:S(2)}, u32[]{:S(2)}) collective-permute-start(bf16[512,1024]{1,0:T(8,128)(2,1)S(1)} %collective-permute-done.4.refs_2_), channel_id=1, source_target_pairs={{0,32},{1,97},{32,64},{33,1},{64,96},{65,33},{96,0},{97,65},{128,1... | collective-permute-start | bytes 3145736 | tf_op jit(solution)/shard_map/ppermute | solution.py:311
  70.8 14.1 %collective-permute-start.17 = (bf16[512,512]{1,0:T(8,128)(2,1)S(1)}, bf16[512,512]{1,0:T(8,128)(2,1)S(1)}, u32[]{:S(2)}, u32[]{:S(2)}) collective-permute-start(bf16[512,512]{1,0:T(8,128)(2,1)S(1)} %collective-permute-done.16.refs_0_.refs_4_), channel_id=1, source_target_pairs={{0,2},{2,0},{4,6},{6,4},{8,10},{10,8},{12,14},{14,12},{16,18},{18,... | collective-permute-start | bytes 1572872 | tf_op jit(solution)/shard_map/ppermute | solution.py:308
  71.0 13.9 %collective-permute-start.18 = (bf16[512,512]{1,0:T(8,128)(2,1)S(1)}, bf16[512,512]{1,0:T(8,128)(2,1)S(1)}, u32[]{:S(2)}, u32[]{:S(2)}) collective-permute-start(bf16[512,512]{1,0:T(8,128)(2,1)S(1)} %collective-permute-done.9.refs_3_.refs_7_), channel_id=1, source_target_pairs={{0,28},{1,5},{2,30},{3,7},{4,0},{5,9},{6,2},{7,11},{8,4},{9,13},{1... | collective-permute-start | bytes 1572872 | tf_op jit(solution)/shard_map/ppermute | solution.py:305
  75.2 11.2 %collective-permute-start.6 = (bf16[2048,1024]{1,0:T(8,128)(2,1)S(1)}, bf16[2048,1024]{1,0:T(8,128)(2,1)S(1)}, u32[]{:S(2)}, u32[]{:S(2)}) collective-permute-start(bf16[2048,1024]{1,0:T(8,128)(2,1)S(1)} %shard_map.159.refs_5_.refs_11_), channel_id=1, source_target_pairs={{0,1},{1,0},{2,3},{3,2},{4,5},{5,4},{6,7},{7,6},{8,9},{9,8},{10,11... | collective-permute-start | bytes 12582920 | tf_op jit(solution)/shard_map/ppermute | solution.py:317
  93.5 9.1 %collective-permute-start.22 = (bf16[1040,128]{1,0:T(8,128)(2,1)S(1)}, bf16[1040,128]{1,0:T(8,128)(2,1)S(1)}, u32[]{:S(2)}, u32[]{:S(2)}) collective-permute-start(bf16[1040,128]{1,0:T(8,128)(2,1)S(1)} %get-tuple-element.100), channel_id=1, source_target_pairs={{0,32},{32,64},{64,96},{96,0},{128,160},{160,192},{192,224},{224,1... | collective-permute-start | bytes 798728 | tf_op jit(solution)/shard_map/ppermute | solution.py:314
  93.9 8.7 %collective-permute-start.23 = (bf16[1040,128]{1,0:T(8,128)(2,1)S(1)}, bf16[1040,128]{1,0:T(8,128)(2,1)S(1)}, u32[]{:S(2)}, u32[]{:S(2)}) collective-permute-start(bf16[1040,128]{1,0:T(8,128)(2,1)S(1)} %get-tuple-element.101), channel_id=1, source_target_pairs={{0,96},{32,0},{64,32},{96,64},{128,224},{160,128},{192,160},{224,1... | collective-permute-start | bytes 798728 | tf_op jit(solution)/shard_map/ppermute | solution.py:314
  99.2 10.9 %collective-permute-start.25 = (bf16[1040,128]{1,0:T(8,128)(2,1)S(1)}, bf16[1040,128]{1,0:T(8,128)(2,1)S(1)}, u32[]{:S(2)}, u32[]{:S(2)}) collective-permute-start(bf16[1040,128]{1,0:T(8,128)(2,1)S(1)} %get-tuple-element.110), channel_id=1, source_target_pairs={{0,32},{32,64},{64,96},{96,0},{128,160},{160,192},{192,224},{224,1... | collective-permute-start | bytes 798728 | tf_op jit(solution)/shard_map/ppermute | solution.py:314
  99.6 10.5 %collective-permute-start.26 = (bf16[1040,128]{1,0:T(8,128)(2,1)S(1)}, bf16[1040,128]{1,0:T(8,128)(2,1)S(1)}, u32[]{:S(2)}, u32[]{:S(2)}) collective-permute-start(bf16[1040,128]{1,0:T(8,128)(2,1)S(1)} %get-tuple-element.111), channel_id=1, source_target_pairs={{0,96},{32,0},{64,32},{96,64},{128,224},{160,128},{192,160},{224,1... | collective-permute-start | bytes 798728 | tf_op jit(solution)/shard_map/ppermute | solution.py:314
  (9 other events, 87.4 us)
